TPU v7x, 32 devices: a whole 2x2x4 slice. The times are simulated.
32 devices in a mesh: half: 4 (over x, core), wide: 8 (over z, y).
Axes of the slice: x: 2, y: 2, z: 4, core: 2. Of those that a mesh axis runs over, the one named last changes fastest.
Arguments:
- gains: float32 [4096, 4096], P(('half', 'wide')), parts along dimension 0, may hold values from -4 to 4
- response: bfloat16 [4096, 4096], P('wide', 'half'), parts along dimension 1, may hold values from -6 to 6
- student: bfloat16 [4096, 4096], P('wide', 'half'), parts along dimension 1, may hold values from 0.19921875 to 1
- blocks: bfloat16 [16, 256, 256], P('half'), parts along dimension 0, may hold values from -0.5 to 2.5, as said below
- order: int32 [4096], P('half'), parts along dimension 0, may hold values from 0 to 1023, each once
- lower: float32 [4096], P(('half', 'wide')), parts along dimension 0, may hold values from -1.2 to -0.4
- upper: float32 [4096], P(('half', 'wide')), parts along dimension 0, may hold values from 0.4 to 1.2
- lengths: float32 [4096], replicated, may hold values from 32 to 2048
- amplitude: float32 [4096], replicated, may hold values from 0.5 to 1.5
Outputs:
- tracked: float32 [4096, 4096], P(('half', 'wide')), parts along dimension 0
There are 4 independent parts, one for each index of `half`. A program takes and returns all parts, laid end to end along the dimension named above; an argument that names none is the same for every part. Nothing has to cross between parts.
Inputs may be any that keep to these rules, and one draw needn't show every extreme that they name: `blocks`: each block is symmetric.
All inputs are finite; a program needn't handle non-finite values.
Results may differ from a plain program's by a relative error of at most 0.012.
The roundings to bfloat16 on the way count: a program that leaves them out, or rounds other values in their place, can miss the bound.
Values may be sent and summed in bfloat16 or wider, within the bound.
No kernel may reach another device: no remote copies, remote signals or barrier semaphores. Data moves between devices by JAX's collectives and lax.ppermute only.
A program may use at most 128 MiB of HBM per device.

v0:
```python
import jax
import jax.numpy as jnp
from jax import lax
from jax.sharding import PartitionSpec as P

ITERS = 2


def covar_stack(lengths, amplitude, span):
    total = lengths.shape[0]
    count = total // span
    rows = jnp.arange(total, dtype=jnp.int32)

    def one_block(index):
        start = index * span
        cols = start + jnp.arange(span, dtype=jnp.int32)
        diff = (rows[:, None] - cols[None, :]).astype(lengths.dtype)
        left = lengths[:, None]
        right = lax.dynamic_slice_in_dim(lengths, start, span, 0)[None, :]
        amp_right = lax.dynamic_slice_in_dim(amplitude, start, span, 0)[None, :]
        denom = left * left + right * right
        vals = (
            amplitude[:, None]
            * amp_right
            * jnp.sqrt(2.0 * left * right / denom)
            * jnp.exp(-diff * diff / denom)
        )
        return vals.astype(jnp.bfloat16)

    return lax.map(one_block, jnp.arange(count, dtype=jnp.int32))


def data_rows(packed, resp_perm, stud_perm, blocks, order, inverse):
    rows, chans = packed.shape
    nblk, width = (blocks.shape[0], blocks.shape[1])
    moved = jnp.take(packed, order, axis=1).reshape(rows, nblk, width)
    product = jnp.einsum("rbi,bij->rbj", moved, blocks, preferred_element_type=jnp.float32).reshape(
        rows, chans
    )
    permuted = stud_perm.astype(jnp.float32) * (product - resp_perm.astype(jnp.float32))
    return jnp.take(permuted, inverse, axis=1).astype(jnp.bfloat16)


def per_device(gains, response, student, blocks, order, lower, upper, lengths, amplitude):
    nwide = lax.axis_size("wide")
    chd, epochs = gains.shape
    epd = epochs // nwide
    chans = chd * nwide
    inverse = jnp.zeros((chans,), jnp.int32).at[order].set(jnp.arange(chans, dtype=jnp.int32))
    resp_perm = jnp.take(response, order, axis=1)
    stud_perm = jnp.take(student, order, axis=1)
    span = min(256, epochs)
    kernel_stack = covar_stack(lengths, amplitude, span)
    current = gains
    for step in range(ITERS):
        packed = current.astype(jnp.bfloat16).reshape(chd, nwide, epd)
        got = (
            lax.all_to_all(packed, "wide", split_axis=1, concat_axis=0, tiled=True)
            .reshape(chans, epd)
            .T
        )
        misfit_rows = data_rows(got, resp_perm, stud_perm, blocks, order, inverse)
        misfit = lax.all_to_all(
            misfit_rows.T.reshape(chans, 1, epd), "wide", split_axis=0, concat_axis=1, tiled=True
        ).reshape(chd, epochs)
        smoothed = jnp.einsum(
            "ce,bes->cbs", misfit, kernel_stack, preferred_element_type=jnp.float32
        ).reshape(chd, epochs)
        current = jnp.clip(current - 0.02 * smoothed, lower[:, None], upper[:, None])
    return current


def solution(mesh):
    placed = (
        P(("half", "wide"), None),
        P("wide", "half"),
        P("wide", "half"),
        P("half", None, None),
        P("half"),
        P(("half", "wide")),
        P(("half", "wide")),
        P(),
        P(),
    )
    return jax.shard_map(
        per_device, mesh=mesh, in_specs=placed, out_specs=P(("half", "wide"), None), check_vma=False
    )
```

profile of v0, /device:TPU:0, one launch (start us, length us, event | category | flops | bytes accessed | tf_op | source)
XLA Modules:
  0.0 352.2 jit_solution(1145889868230269508)
XLA Ops:
  2.9 7.3 %all-to-all-start = ((bf16[128,8,512]{2,0,1:T(8,128)(2,1)}), bf16[128,8,512]{2,0,1:T(8,128)(2,1)S(1)}, u32[]{:S(2)}, u32[]{:S(2)}) async-start(bf16[128,8,512]{2,0,1:T(8,128)(2,1)} %bitcast.79), calls=%async_computation | async-start | bytes 2097152 | tf_op jit(solution)/shard_map/all_to_all | solution.py:58
  13.0 6.5 %gather_fusion = bf16[1024,512]{1,0:T(8,128)(2,1)} fusion(bf16[512,1024]{0,1:T(8,128)(2,1)} %copy.40, s32[1024]{0:T(1024)S(1)} %get-tuple-element.98), kind=kCustom, calls=%fused_computation.clone | custom fusion | bytes 2101248 | tf_op jit(solution)/shard_map/jit(_take)/gather | solution.py:51
  19.5 5.1 %gather_fusion.2 = bf16[1024,512]{1,0:T(8,128)(2,1)} fusion(bf16[512,1024]{0,1:T(8,128)(2,1)S(1)} %copy.44, s32[1024]{0:T(1024)S(1)} %get-tuple-element.98), kind=kCustom, calls=%fused_computation.3.clone | custom fusion | bytes 2101248 | tf_op jit(solution)/shard_map/jit(_take)/gather | solution.py:50
  24.5 4.3 %scatter_custom_fusion = s32[1024]{0:T(1024)S(1)} fusion(s32[1024]{0:T(1024)S(1)} %get-tuple-element.97, s32[1024]{0:T(1024)S(1)} %iota.15, s32[]{:T(128)} %constant.36.clone.1), kind=kCustom, calls=%fused_computation.49 | custom fusion | bytes 4100 | tf_op jit(solution)/shard_map/scatter | solution.py:49
  28.9 7.0 %all-to-all-done = bf16[128,8,512]{2,0,1:T(8,128)(2,1)S(1)} async-done(((bf16[128,8,512]{2,0,1:T(8,128)(2,1)}), bf16[128,8,512]{2,0,1:T(8,128)(2,1)S(1)}, u32[]{:S(2)}, u32[]{:S(2)}) %all-to-all-start) | async-done | bytes 1048608 | tf_op jit(solution)/shard_map/all_to_all | solution.py:58
  35.9 4.0 %gather_fusion.1 = bf16[1024,512]{1,0:T(8,128)(2,1)S(1)} fusion(bf16[512,1024]{0,1:T(8,128)(2,1)S(1)} %bitcast.86, s32[1024]{0:T(1024)S(1)} %get-tuple-element.98), kind=kCustom, calls=%fused_computation.2.clone | custom fusion | bytes 2101248 | tf_op jit(solution)/shard_map/jit(_take)/gather | solution.py:36
  42.2 4.0 %gather_fusion.3 = bf16[1024,512]{1,0:T(8,128)(2,1)S(1)} fusion(bf16[512,1024]{0,1:T(8,128)(2,1)S(1)} %convert_multiply_fusion.1, s32[1024]{0:T(1024)S(1)} %fusion.16), kind=kCustom, calls=%fused_computation.1.clone | custom fusion | bytes 2101248 | tf_op jit(solution)/shard_map/jit(_take)/gather | solution.py:41
  52.3 4.2 %all-to-all-start.1 = ((bf16[8,2,32768]{2,1,0:T(2,128)(2,1)}), bf16[8,2,32768]{2,1,0:T(2,128)(2,1)}, u32[]{:S(2)}, u32[]{:S(2)}) async-start(bf16[8,2,32768]{2,1,0:T(2,128)(2,1)} %reshape.377), calls=%async_computation.1 | async-start | bytes 2097152 | tf_op jit(solution)/shard_map/all_to_all | solution.py:63
  56.6 166.7 %while.12 = (s32[]{:T(128)}, bf16[16,4096,256]{1,2,0:T(8,128)(2,1)}, f32[4096]{0:T(1024)S(1)}, s32[16]{0:T(128)S(1)}, f32[4096]{0:T(1024)S(1)}, /*index=5*/f32[4...) while((s32[]{:T(128)}, bf16[16,4096,256]{1,2,0:T(8,128)(2,1)}, ...), condition=%wide.region_2.5_spmd.clone, body=%wide.region_1.4_spmd.clone.sunk | while | flops 12587526 | bytes 10578603 | solution.py:30
  58.0 4.6 %fusion.34 = bf16[1,4096,256]{2,1,0:T(8,128)(2,1)} fusion(s32[256]{0:T(256)S(1)} %iota_add_fusion.2, f32[256]{0:T(256)S(1)} %get-tuple-element.140, f32[4096]{0:T(1024)S(1)} %bitcast.98, f32[256]{0:T(256)S(1)} %get-tuple-element.141, f32[4096]{0:T(1024)S(1)} %broadcast_multiply_fusion.2, f32[256]{0:T(256)S(1)} %dynamic_slice.22, ...), kind=kLoop, calls=%fused_computation.17.clone.1 | loop fusion | flops 12582912 | bytes 2150400 | tf_op jit(solution)/shard_map/while/body/eval_jaxpr/convert_element_type | solution.py:28
  68.4 4.6 %fusion.34 = bf16[1,4096,256]{2,1,0:T(8,128)(2,1)} fusion(s32[256]{0:T(256)S(1)} %iota_add_fusion.2, f32[256]{0:T(256)S(1)} %get-tuple-element.140, f32[4096]{0:T(1024)S(1)} %bitcast.98, f32[256]{0:T(256)S(1)} %get-tuple-element.141, f32[4096]{0:T(1024)S(1)} %broadcast_multiply_fusion.2, f32[256]{0:T(256)S(1)} %dynamic_slice.22, ...), kind=kLoop, calls=%fused_computation.17.clone.1 | loop fusion | flops 12582912 | bytes 2150400 | tf_op jit(solution)/shard_map/while/body/eval_jaxpr/convert_element_type | solution.py:28
  78.8 4.6 %fusion.34 = bf16[1,4096,256]{2,1,0:T(8,128)(2,1)} fusion(s32[256]{0:T(256)S(1)} %iota_add_fusion.2, f32[256]{0:T(256)S(1)} %get-tuple-element.140, f32[4096]{0:T(1024)S(1)} %bitcast.98, f32[256]{0:T(256)S(1)} %get-tuple-element.141, f32[4096]{0:T(1024)S(1)} %broadcast_multiply_fusion.2, f32[256]{0:T(256)S(1)} %dynamic_slice.22, ...), kind=kLoop, calls=%fused_computation.17.clone.1 | loop fusion | flops 12582912 | bytes 2150400 | tf_op jit(solution)/shard_map/while/body/eval_jaxpr/convert_element_type | solution.py:28
  89.2 4.6 %fusion.34 = bf16[1,4096,256]{2,1,0:T(8,128)(2,1)} fusion(s32[256]{0:T(256)S(1)} %iota_add_fusion.2, f32[256]{0:T(256)S(1)} %get-tuple-element.140, f32[4096]{0:T(1024)S(1)} %bitcast.98, f32[256]{0:T(256)S(1)} %get-tuple-element.141, f32[4096]{0:T(1024)S(1)} %broadcast_multiply_fusion.2, f32[256]{0:T(256)S(1)} %dynamic_slice.22, ...), kind=kLoop, calls=%fused_computation.17.clone.1 | loop fusion | flops 12582912 | bytes 2150400 | tf_op jit(solution)/shard_map/while/body/eval_jaxpr/convert_element_type | solution.py:28
  99.7 4.6 %fusion.34 = bf16[1,4096,256]{2,1,0:T(8,128)(2,1)} fusion(s32[256]{0:T(256)S(1)} %iota_add_fusion.2, f32[256]{0:T(256)S(1)} %get-tuple-element.140, f32[4096]{0:T(1024)S(1)} %bitcast.98, f32[256]{0:T(256)S(1)} %get-tuple-element.141, f32[4096]{0:T(1024)S(1)} %broadcast_multiply_fusion.2, f32[256]{0:T(256)S(1)} %dynamic_slice.22, ...), kind=kLoop, calls=%fused_computation.17.clone.1 | loop fusion | flops 12582912 | bytes 2150400 | tf_op jit(solution)/shard_map/while/body/eval_jaxpr/convert_element_type | solution.py:28
  110.1 4.6 %fusion.34 = bf16[1,4096,256]{2,1,0:T(8,128)(2,1)} fusion(s32[256]{0:T(256)S(1)} %iota_add_fusion.2, f32[256]{0:T(256)S(1)} %get-tuple-element.140, f32[4096]{0:T(1024)S(1)} %bitcast.98, f32[256]{0:T(256)S(1)} %get-tuple-element.141, f32[4096]{0:T(1024)S(1)} %broadcast_multiply_fusion.2, f32[256]{0:T(256)S(1)} %dynamic_slice.22, ...), kind=kLoop, calls=%fused_computation.17.clone.1 | loop fusion | flops 12582912 | bytes 2150400 | tf_op jit(solution)/shard_map/while/body/eval_jaxpr/convert_element_type | solution.py:28
  120.6 4.6 %fusion.34 = bf16[1,4096,256]{2,1,0:T(8,128)(2,1)} fusion(s32[256]{0:T(256)S(1)} %iota_add_fusion.2, f32[256]{0:T(256)S(1)} %get-tuple-element.140, f32[4096]{0:T(1024)S(1)} %bitcast.98, f32[256]{0:T(256)S(1)} %get-tuple-element.141, f32[4096]{0:T(1024)S(1)} %broadcast_multiply_fusion.2, f32[256]{0:T(256)S(1)} %dynamic_slice.22, ...), kind=kLoop, calls=%fused_computation.17.clone.1 | loop fusion | flops 12582912 | bytes 2150400 | tf_op jit(solution)/shard_map/while/body/eval_jaxpr/convert_element_type | solution.py:28
  131.0 4.6 %fusion.34 = bf16[1,4096,256]{2,1,0:T(8,128)(2,1)} fusion(s32[256]{0:T(256)S(1)} %iota_add_fusion.2, f32[256]{0:T(256)S(1)} %get-tuple-element.140, f32[4096]{0:T(1024)S(1)} %bitcast.98, f32[256]{0:T(256)S(1)} %get-tuple-element.141, f32[4096]{0:T(1024)S(1)} %broadcast_multiply_fusion.2, f32[256]{0:T(256)S(1)} %dynamic_slice.22, ...), kind=kLoop, calls=%fused_computation.17.clone.1 | loop fusion | flops 12582912 | bytes 2150400 | tf_op jit(solution)/shard_map/while/body/eval_jaxpr/convert_element_type | solution.py:28
  141.4 4.6 %fusion.34 = bf16[1,4096,256]{2,1,0:T(8,128)(2,1)} fusion(s32[256]{0:T(256)S(1)} %iota_add_fusion.2, f32[256]{0:T(256)S(1)} %get-tuple-element.140, f32[4096]{0:T(1024)S(1)} %bitcast.98, f32[256]{0:T(256)S(1)} %get-tuple-element.141, f32[4096]{0:T(1024)S(1)} %broadcast_multiply_fusion.2, f32[256]{0:T(256)S(1)} %dynamic_slice.22, ...), kind=kLoop, calls=%fused_computation.17.clone.1 | loop fusion | flops 12582912 | bytes 2150400 | tf_op jit(solution)/shard_map/while/body/eval_jaxpr/convert_element_type | solution.py:28
  151.8 4.6 %fusion.34 = bf16[1,4096,256]{2,1,0:T(8,128)(2,1)} fusion(s32[256]{0:T(256)S(1)} %iota_add_fusion.2, f32[256]{0:T(256)S(1)} %get-tuple-element.140, f32[4096]{0:T(1024)S(1)} %bitcast.98, f32[256]{0:T(256)S(1)} %get-tuple-element.141, f32[4096]{0:T(1024)S(1)} %broadcast_multiply_fusion.2, f32[256]{0:T(256)S(1)} %dynamic_slice.22, ...), kind=kLoop, calls=%fused_computation.17.clone.1 | loop fusion | flops 12582912 | bytes 2150400 | tf_op jit(solution)/shard_map/while/body/eval_jaxpr/convert_element_type | solution.py:28
  162.2 4.6 %fusion.34 = bf16[1,4096,256]{2,1,0:T(8,128)(2,1)} fusion(s32[256]{0:T(256)S(1)} %iota_add_fusion.2, f32[256]{0:T(256)S(1)} %get-tuple-element.140, f32[4096]{0:T(1024)S(1)} %bitcast.98, f32[256]{0:T(256)S(1)} %get-tuple-element.141, f32[4096]{0:T(1024)S(1)} %broadcast_multiply_fusion.2, f32[256]{0:T(256)S(1)} %dynamic_slice.22, ...), kind=kLoop, calls=%fused_computation.17.clone.1 | loop fusion | flops 12582912 | bytes 2150400 | tf_op jit(solution)/shard_map/while/body/eval_jaxpr/convert_element_type | solution.py:28
  172.6 4.6 %fusion.34 = bf16[1,4096,256]{2,1,0:T(8,128)(2,1)} fusion(s32[256]{0:T(256)S(1)} %iota_add_fusion.2, f32[256]{0:T(256)S(1)} %get-tuple-element.140, f32[4096]{0:T(1024)S(1)} %bitcast.98, f32[256]{0:T(256)S(1)} %get-tuple-element.141, f32[4096]{0:T(1024)S(1)} %broadcast_multiply_fusion.2, f32[256]{0:T(256)S(1)} %dynamic_slice.22, ...), kind=kLoop, calls=%fused_computation.17.clone.1 | loop fusion | flops 12582912 | bytes 2150400 | tf_op jit(solution)/shard_map/while/body/eval_jaxpr/convert_element_type | solution.py:28
  183.0 4.6 %fusion.34 = bf16[1,4096,256]{2,1,0:T(8,128)(2,1)} fusion(s32[256]{0:T(256)S(1)} %iota_add_fusion.2, f32[256]{0:T(256)S(1)} %get-tuple-element.140, f32[4096]{0:T(1024)S(1)} %bitcast.98, f32[256]{0:T(256)S(1)} %get-tuple-element.141, f32[4096]{0:T(1024)S(1)} %broadcast_multiply_fusion.2, f32[256]{0:T(256)S(1)} %dynamic_slice.22, ...), kind=kLoop, calls=%fused_computation.17.clone.1 | loop fusion | flops 12582912 | bytes 2150400 | tf_op jit(solution)/shard_map/while/body/eval_jaxpr/convert_element_type | solution.py:28
  193.5 4.6 %fusion.34 = bf16[1,4096,256]{2,1,0:T(8,128)(2,1)} fusion(s32[256]{0:T(256)S(1)} %iota_add_fusion.2, f32[256]{0:T(256)S(1)} %get-tuple-element.140, f32[4096]{0:T(1024)S(1)} %bitcast.98, f32[256]{0:T(256)S(1)} %get-tuple-element.141, f32[4096]{0:T(1024)S(1)} %broadcast_multiply_fusion.2, f32[256]{0:T(256)S(1)} %dynamic_slice.22, ...), kind=kLoop, calls=%fused_computation.17.clone.1 | loop fusion | flops 12582912 | bytes 2150400 | tf_op jit(solution)/shard_map/while/body/eval_jaxpr/convert_element_type | solution.py:28
  203.9 4.6 %fusion.34 = bf16[1,4096,256]{2,1,0:T(8,128)(2,1)} fusion(s32[256]{0:T(256)S(1)} %iota_add_fusion.2, f32[256]{0:T(256)S(1)} %get-tuple-element.140, f32[4096]{0:T(1024)S(1)} %bitcast.98, f32[256]{0:T(256)S(1)} %get-tuple-element.141, f32[4096]{0:T(1024)S(1)} %broadcast_multiply_fusion.2, f32[256]{0:T(256)S(1)} %dynamic_slice.22, ...), kind=kLoop, calls=%fused_computation.17.clone.1 | loop fusion | flops 12582912 | bytes 2150400 | tf_op jit(solution)/shard_map/while/body/eval_jaxpr/convert_element_type | solution.py:28
  214.3 4.6 %fusion.34 = bf16[1,4096,256]{2,1,0:T(8,128)(2,1)} fusion(s32[256]{0:T(256)S(1)} %iota_add_fusion.2, f32[256]{0:T(256)S(1)} %get-tuple-element.140, f32[4096]{0:T(1024)S(1)} %bitcast.98, f32[256]{0:T(256)S(1)} %get-tuple-element.141, f32[4096]{0:T(1024)S(1)} %broadcast_multiply_fusion.2, f32[256]{0:T(256)S(1)} %dynamic_slice.22, ...), kind=kLoop, calls=%fused_computation.17.clone.1 | loop fusion | flops 12582912 | bytes 2150400 | tf_op jit(solution)/shard_map/while/body/eval_jaxpr/convert_element_type | solution.py:28
  223.3 5.8 %reshape.378 = bf16[1024,1,512]{2,1,0:T(2,128)(2,1)} reshape(bf16[8,2,32768]{2,1,0:T(2,128)(2,1)} %all-to-all-done.1) | data formatting | bytes 2097152
  234.3 17.4 %fusion.20 = (bf16[128,4096]{1,0:T(8,128)(2,1)S(1)}, f32[128,4096]{1,0:T(8,128)}) fusion(f32[128,4096]{1,0:T(8,128)S(1)} %copy-done.6, bf16[128,4096]{0,1:T(8,128)(2,1)} %bitcast.88, bf16[4096,4096]{1,0:T(8,128)(2,1)} %bitcast.84, f32[128]{0:T(128)S(1)} %copy-done.10, f32[128]{0:T(128)S(1)} %copy-done.11), kind=kOutput, calls=%fused_computation.52 | convolution fusion | flops 4297588736 | bytes 39846912 | tf_op jit(solution)/shard_map/ce,bes->cbs/dot_general | solution.py:66
  251.8 30.6 %all_to_all.60 = bf16[128,8,512]{2,0,1:T(8,128)(2,1)S(1)} all-to-all(bf16[128,8,512]{2,0,1:T(8,128)(2,1)S(1)} %bitcast.96), channel_id=1, replica_groups=mesh['half'=4,'wide'=8] {'wide'}, dimensions={1} | all-to-all | bytes 2097152 | tf_op jit(solution)/shard_map/all_to_all | solution.py:58
  282.4 4.0 %gather_fusion.4 = bf16[1024,512]{1,0:T(8,128)(2,1)S(1)} fusion(bf16[512,1024]{0,1:T(8,128)(2,1)S(1)} %bitcast.87, s32[1024]{0:T(1024)S(1)} %get-tuple-element.98), kind=kCustom, calls=%fused_computation.4.clone | custom fusion | bytes 2101248 | tf_op jit(solution)/shard_map/jit(_take)/gather | solution.py:36
  288.6 4.0 %gather_fusion.5 = bf16[1024,512]{1,0:T(8,128)(2,1)S(1)} fusion(bf16[512,1024]{0,1:T(8,128)(2,1)S(1)} %convert_multiply_fusion, s32[1024]{0:T(1024)S(1)} %fusion.16), kind=kCustom, calls=%fused_computation.5.clone | custom fusion | bytes 2101248 | tf_op jit(solution)/shard_map/jit(_take)/gather | solution.py:41
  297.5 28.7 %all_to_all.61 = bf16[8,2,32768]{2,1,0:T(2,128)(2,1)S(1)} all-to-all(bf16[8,2,32768]{2,1,0:T(2,128)(2,1)S(1)} %reshape.379), channel_id=1, replica_groups=mesh['half'=4,'wide'=8] {'wide'}, dimensions={0} | all-to-all | bytes 2097152 | tf_op jit(solution)/shard_map/all_to_all | solution.py:63
  334.9 17.3 %fusion.13 = f32[128,4096]{1,0:T(8,128)} fusion(f32[128,4096]{1,0:T(8,128)S(1)} %copy-done.5, bf16[128,4096]{0,1:T(8,128)(2,1)} %bitcast.89, bf16[4096,4096]{1,0:T(8,128)(2,1)} %bitcast.85, f32[128]{0:T(128)S(1)} %copy-done.10, f32[128]{0:T(128)S(1)} %copy-done.11), kind=kOutput, calls=%fused_computation.28 | convolution fusion | flops 4297064448 | bytes 38798336 | tf_op jit(solution)/shard_map/ce,bes->cbs/dot_general | solution.py:66
  (170 shorter events, 117.3 us)
Async XLA Ops:
  0.0 40.1 %copy-start = (bf16[4,256,256]{2,1,0:T(8,128)(2,1)S(1)}, bf16[4,256,256]{2,1,0:T(8,128)(2,1)}, u32[]{:S(2)}) copy-start(bf16[4,256,256]{2,1,0:T(8,128)(2,1)} %param.18) | copy-start | bytes 1572868
  1.8 8.4 %copy-start.7 = (bf16[512,1024]{1,0:T(8,128)(2,1)S(1)}, bf16[512,1024]{1,0:T(8,128)(2,1)}, u32[]{:S(2)}) copy-start(bf16[512,1024]{1,0:T(8,128)(2,1)} %param.17) | copy-start | bytes 3145732
  2.9 33.0 %all-to-all-start = ((bf16[128,8,512]{2,0,1:T(8,128)(2,1)}), bf16[128,8,512]{2,0,1:T(8,128)(2,1)S(1)}, u32[]{:S(2)}, u32[]{:S(2)}) async-start(bf16[128,8,512]{2,0,1:T(8,128)(2,1)} %bitcast.79), calls=%async_computation | async-start | bytes 2097152 | tf_op jit(solution)/shard_map/all_to_all | solution.py:58
  10.1 2.8 copy-start.9
  19.5 5.1 %copy-start.8 = (f32[4096]{0:T(1024)S(1)}, f32[4096]{0:T(1024)}, u32[]{:S(2)}) copy-start(f32[4096]{0:T(1024)} %param.22) | copy-start | bytes 49156
  40.1 1.2 copy-start.1
  40.1 1.5 copy-start.3
  50.7 5.9 %copy-start.12 = (f32[4096]{0:T(1024)S(1)}, f32[4096]{0:T(1024)}, u32[]{:S(2)}) copy-start(f32[4096]{0:T(1024)} %param.23) | copy-start | bytes 49156
  52.3 171.0 %all-to-all-start.1 = ((bf16[8,2,32768]{2,1,0:T(2,128)(2,1)}), bf16[8,2,32768]{2,1,0:T(2,128)(2,1)}, u32[]{:S(2)}, u32[]{:S(2)}) async-start(bf16[8,2,32768]{2,1,0:T(2,128)(2,1)} %reshape.377), calls=%async_computation.1 | async-start | bytes 2097152 | tf_op jit(solution)/shard_map/all_to_all | solution.py:63
  229.1 5.3 %copy-start.6 = (f32[128,4096]{1,0:T(8,128)S(1)}, f32[128,4096]{1,0:T(8,128)}, u32[]{:S(2)}) copy-start(f32[128,4096]{1,0:T(8,128)} %param.15) | copy-start | bytes 6291460
  229.1 5.3 %copy-start.10 = (f32[128]{0:T(128)S(1)}, f32[128]{0:T(128)}, u32[]{:S(2)}) copy-start(f32[128]{0:T(128)} %param.20) | copy-start | bytes 1540
  229.1 5.3 %copy-start.11 = (f32[128]{0:T(128)S(1)}, f32[128]{0:T(128)}, u32[]{:S(2)}) copy-start(f32[128]{0:T(128)} %param.21) | copy-start | bytes 1540
  286.6 1.2 copy-start.2
  286.6 1.5 copy-start.4
  329.6 5.3 %copy-start.5 = (f32[128,4096]{1,0:T(8,128)S(1)}, f32[128,4096]{1,0:T(8,128)}, u32[]{:S(2)}) copy-start(f32[128,4096]{1,0:T(8,128)} %get-tuple-element.100) | copy-start | bytes 6291460
where the time goes:
time: 354 us; the launch traced here: 352 us
  local copies, waits for them, and re-layouts  141 us (40%)
  other arithmetic  86.7 us (24%)
  blocking collectives  59.2 us (17%)
  matrix products  35.7 us (10%)
  starting transfers between devices  11.5 us (3%)
  loops' own time  10.7 us (3%)
  waiting for transfers between devices  7.01 us (2%)
    convert_element_type x16, other arithmetic, one_block(): return vals.astype(jnp.bfloat16)  74 us
    dynamic_update_slice x32, local copies, waits for them, and re-layouts, covar_stack(): return lax.map(one_block, jnp.arange(count, dtype=jnp.int32))  70.1 us
    dot_general x2, matrix products, per_device(): jnp.einsum('ce,bes->cbs', misfit, kernel_stack, preferred_element_type=jn...  34.7 us
    all_to_all x1, blocking collectives, per_device(): lax.all_to_all(packed, 'wide', split_axis=1, concat_axis=0, tiled=True)  30.6 us
    all_to_all x1, blocking collectives, per_device(): lax.all_to_all(misfit_rows.T.reshape(chans, 1, epd), 'wide', split_axis=0...  28.7 us
    unnamed x34, local copies, waits for them, and re-layouts  22.5 us
    another operation x1, loops' own time, covar_stack(): return lax.map(one_block, jnp.arange(count, dtype=jnp.int32))  10.7 us
    dynamic_slice x16, local copies, waits for them, and re-layouts, covar_stack(): return lax.map(one_block, jnp.arange(count, dtype=jnp.int32))  9.32 us
  transfers between devices with their start and end apart: 2, of which 1 were waited for; matrix products, arithmetic and copies ran while one was open for 50% of the time, Pallas kernels for 0%

commit v1 on v0

--- a/solution.py
+++ b/solution.py
@@ -1,9 +1,334 @@
+import math
 import jax
 import jax.numpy as jnp
 from jax import lax
+from jax.experimental import pallas as pl
+from jax.experimental.pallas import tpu as pltpu
 from jax.sharding import PartitionSpec as P
 
 ITERS = 2
+LN2 = math.log(2.0)
+F32 = jnp.float32
+BF16 = jnp.bfloat16
+
+
+def params(mib):
+    return pltpu.CompilerParams(vmem_limit_bytes=mib * 1024 * 1024)
+
+
+def cost(flops, moved, special=0):
+    return pl.CostEstimate(flops=int(flops), bytes_accessed=int(moved), transcendentals=int(special))
+
+
+def dot(a, b):
+    return jnp.dot(a, b, preferred_element_type=F32)
+
+
+def pack(me, gains, ndev, epd):
+    chd = gains.shape[0]
+
+    def body(me_ref, gains_ref, *outs):
+        step = pl.program_id(0)
+        for r in range(ndev):
+
+            @pl.when(step == r)
+            def _():
+                outs[r][...] = gains_ref[...].astype(BF16)
+
+    return pl.pallas_call(
+        body,
+        out_shape=[jax.ShapeDtypeStruct((chd, epd), BF16)] * ndev,
+        grid_spec=pltpu.PrefetchScalarGridSpec(
+            num_scalar_prefetch=1,
+            grid=(ndev,),
+            in_specs=[pl.BlockSpec((chd, epd), lambda r, me_ref: (0, me_ref[0] ^ r))],
+            out_specs=[pl.BlockSpec((chd, epd), lambda r, me_ref: (0, 0))] * ndev,
+        ),
+        compiler_params=params(16),
+        cost_estimate=cost(0, gains.size * 6),
+        name="pack_gains",
+    )(me, gains)
+
+
+def flip(me, data, ndev):
+    epd, chans = data.shape
+    chd = chans // ndev
+
+    def body(me_ref, data_ref, out_ref):
+        out_ref[...] = data_ref[...].astype(F32).T.astype(BF16)
+
+    return pl.pallas_call(
+        body,
+        out_shape=jax.ShapeDtypeStruct((chans, epd), BF16),
+        grid_spec=pltpu.PrefetchScalarGridSpec(
+            num_scalar_prefetch=1,
+            grid=(ndev,),
+            in_specs=[pl.BlockSpec((epd, chd), lambda r, me_ref: (0, me_ref[0] ^ r))],
+            out_specs=pl.BlockSpec((chd, epd), lambda r, me_ref: (r, 0)),
+        ),
+        compiler_params=params(16),
+        cost_estimate=cost(0, data.size * 4),
+        name="flip",
+    )(me, data)
+
+
+def dense(me, blocks, order, ndev):
+    nblk, width, _ = blocks.shape
+    chans = nblk * width
+    chd = chans // ndev
+
+    def body(me_ref, blocks_ref, order_ref, out_ref, hot_ref, left_ref):
+        row = lax.broadcasted_iota(jnp.int32, (chans, width), 0)
+        chan = ((row // chd) ^ me_ref[0]) * chd + row % chd
+        for b in range(nblk):
+            hot = jnp.where(chan == order_ref[b : b + 1, :], 1.0, 0.0).astype(BF16)
+            hot_ref[b] = hot
+            left_ref[b] = dot(hot, blocks_ref[b]).astype(BF16)
+        for r in range(ndev):
+            rows = pl.ds(r * chd, chd)
+            total = jnp.zeros((chd, chans), F32)
+            for b in range(nblk):
+                total += lax.dot_general(
+                    left_ref[b, rows, :], hot_ref[b], (((1,), (1,)), ((), ())), preferred_element_type=F32
+                )
+            out_ref[rows, :] = total.astype(BF16)
+
+    return pl.pallas_call(
+        body,
+        out_shape=jax.ShapeDtypeStruct((chans, chans), BF16),
+        in_specs=[
+            pl.BlockSpec(memory_space=pltpu.SMEM),
+            pl.BlockSpec(memory_space=pltpu.VMEM),
+            pl.BlockSpec(memory_space=pltpu.VMEM),
+        ],
+        out_specs=pl.BlockSpec(memory_space=pltpu.VMEM),
+        scratch_shapes=[pltpu.VMEM((nblk, chans, width), BF16)] * 2,
+        compiler_params=params(24),
+        cost_estimate=cost(2 * chans * chans * (chans + width), chans * chans * 2),
+        name="dense_blocks",
+    )(me, blocks, order.reshape(nblk, width))
+
+
+def covar(me, squares, scales, offsets, epd, rows=256):
+    total = squares.shape[1]
+    per = epd // rows
+    first = offsets[0]
+
+    def body(me_ref, sq_row, sc_row, sq_all, sc_all, out_ref, sq_col, sc_col):
+        step = pl.program_id(0)
+        device = me_ref[0] ^ (first + step // per)
+        base = device * epd + (step % per) * rows
+        for k in range(rows // 128):
+            piece = pl.ds(k * 128, 128)
+            sq_col[piece, :] = jnp.broadcast_to(sq_row[:, piece], (128, 128)).T
+            sc_col[piece, :] = jnp.broadcast_to(sc_row[:, piece], (128, 128)).T
+        lane = lax.broadcasted_iota(jnp.int32, (16, 128), 1)
+        sub = lax.broadcasted_iota(jnp.int32, (16, 128), 0)
+        away = (sub - lane).astype(F32)
+
+        def group(g, _):
+            at = pl.ds(pl.multiple_of(g * 16, 16), 16)
+            sq_i = sq_col[at, :]
+            sc_i = sc_col[at, :]
+            start = away + (base + g * 16).astype(F32)
+            for c in range(total // 128):
+                cols = pl.ds(c * 128, 128)
+                q = lax.rsqrt(sq_i + sq_all[:, cols])
+                u = (start - float(c * 128)) * q
+                out_ref[at, cols] = (q * jnp.exp2((sc_i + sc_all[:, cols]) - u * u)).astype(BF16)
+            return 0
+
+        lax.fori_loop(0, rows // 16, group, 0)
+
+    def row_block(n, me_ref):
+        return (0, (me_ref[0] ^ (first + n // per)) * per + n % per)
+
+    count = len(offsets) * epd
+    return pl.pallas_call(
+        body,
+        out_shape=jax.ShapeDtypeStruct((count, total), BF16),
+        grid_spec=pltpu.PrefetchScalarGridSpec(
+            num_scalar_prefetch=1,
+            grid=(count // rows,),
+            in_specs=[
+                pl.BlockSpec((1, rows), row_block),
+                pl.BlockSpec((1, rows), row_block),
+                pl.BlockSpec((1, total), lambda n, me_ref: (0, 0)),
+                pl.BlockSpec((1, total), lambda n, me_ref: (0, 0)),
+            ],
+            out_specs=pl.BlockSpec((rows, total), lambda n, me_ref: (n, 0)),
+            scratch_shapes=[pltpu.VMEM((rows, 128), F32)] * 2,
+        ),
+        compiler_params=params(16),
+        cost_estimate=cost(16 * count * total, count * total * 2, 2 * count * total),
+        name="covar_rows",
+    )(me, squares, scales, squares, scales)
+
+
+def normal(weights, pieces, resp, stud):
+    ndev = len(pieces)
+    chd, epd = pieces[0].shape
+    chans = ndev * chd
+    steps = [r ^ (ndev // 2) for r in range(ndev)]
+
+    def body(*refs):
+        w_ref, resp_ref, stud_ref = refs[:3]
+        ins = refs[3 : 3 + ndev]
+        outs = refs[3 + ndev : 3 + 2 * ndev]
+        got = refs[-1]
+        step = pl.program_id(0)
+
+        @pl.when(step == 0)
+        def _():
+            for r in range(ndev):
+                got[pl.ds(r * chd, chd), :] = ins[r][...]
+
+        out = stud_ref[...].astype(F32) * (dot(w_ref[...], got[...]) - resp_ref[...].astype(F32))
+        out = out.astype(BF16)
+        for k in range(ndev):
+
+            @pl.when(step == k)
+            def _():
+                outs[steps[k]][...] = out
+
+    def far_first(n):
+        return (n ^ (ndev // 2), 0)
+
+    whole = pl.BlockSpec((chd, epd), lambda n: (0, 0))
+    return pl.pallas_call(
+        body,
+        out_shape=[jax.ShapeDtypeStruct((chd, epd), BF16)] * ndev,
+        grid=(ndev,),
+        in_specs=[
+            pl.BlockSpec((chd, chans), far_first),
+            pl.BlockSpec((chd, epd), far_first),
+            pl.BlockSpec((chd, epd), far_first),
+        ]
+        + [whole] * ndev,
+        out_specs=[whole] * ndev,
+        scratch_shapes=[pltpu.VMEM((chans, epd), BF16)],
+        compiler_params=params(24),
+        cost_estimate=cost(2 * chans * chans * epd, chans * chans * 2 + chans * epd * 8),
+        name="normal_step",
+    )(weights, resp, stud, *pieces)
+
+
+def smooth(pieces, rows, before):
+    chd, epd = pieces[0].shape
+    total = rows.shape[1]
+    cnt = len(pieces)
+    tile = epd
+
+    def body(*refs):
+        ins = refs[:cnt]
+        rows_ref = refs[cnt]
+        out_ref = refs[-1]
+        acc = refs[cnt + 1][...] if before is not None else None
+        for r in range(cnt):
+            term = dot(ins[r][...], rows_ref[pl.ds(r * epd, epd), :])
+            acc = term if acc is None else acc + term
+        out_ref[...] = acc
+
+    moving = pl.BlockSpec((chd, tile), lambda n: (0, n))
+    more = [] if before is None else [before]
+    return pl.pallas_call(
+        body,
+        out_shape=jax.ShapeDtypeStruct((chd, total), F32),
+        grid=(total // tile,),
+        in_specs=[pl.BlockSpec((chd, epd), lambda n: (0, 0))] * cnt
+        + [pl.BlockSpec((cnt * epd, tile), lambda n: (0, n))]
+        + [moving] * len(more),
+        out_specs=moving,
+        compiler_params=params(32),
+        cost_estimate=cost(2 * chd * cnt * epd * total, cnt * epd * total * 2 + chd * total * 4),
+        name="smooth_part",
+    )(*pieces, rows, *more)
+
+
+def update(me, pieces, rows, before, current, lower, upper, last):
+    chd, epd = pieces[0].shape
+    total = rows.shape[1]
+    cnt = len(pieces)
+    ndev = total // epd
+    half = ndev // 2
+    steps = list(range(ndev)) if last else [r ^ half for r in range(ndev)]
+
+    def body(*refs):
+        ins = refs[1 : 1 + cnt]
+        rows_ref, before_ref, cur_ref, low_ref, high_ref, out_ref = refs[1 + cnt : 7 + cnt]
+        acc = before_ref[...]
+        for r in range(cnt):
+            acc = acc + dot(ins[r][...], rows_ref[pl.ds(r * epd, epd), :])
+        new = jnp.clip(cur_ref[...] - 0.02 * acc, low_ref[...], high_ref[...])
+        out_ref[...] = new
+        if not last:
+            packed = new.astype(BF16)
+            for k in range(ndev):
+
+                @pl.when(pl.program_id(0) == k)
+                def _():
+                    refs[7 + cnt + steps[k]][...] = packed
+
+    def column(n, me_ref):
+        return (0, n if last else me_ref[0] ^ n ^ half)
+
+    fixed = lambda n, me_ref: (0, 0)
+    moving = pl.BlockSpec((chd, epd), column)
+    whole = pl.BlockSpec((chd, epd), fixed)
+    extra = 0 if last else ndev
+    return pl.pallas_call(
+        body,
+        out_shape=[jax.ShapeDtypeStruct((chd, total), F32)] + [jax.ShapeDtypeStruct((chd, epd), BF16)] * extra,
+        grid_spec=pltpu.PrefetchScalarGridSpec(
+            num_scalar_prefetch=1,
+            grid=(ndev,),
+            in_specs=[whole] * cnt
+            + [pl.BlockSpec((cnt * epd, epd), column), moving, moving]
+            + [pl.BlockSpec((chd, 1), fixed)] * 2,
+            out_specs=[moving] + [whole] * extra,
+        ),
+        compiler_params=params(32),
+        cost_estimate=cost(2 * chd * cnt * epd * total, cnt * epd * total * 2 + chd * total * 14),
+        name="update",
+    )(me, *pieces, rows, before, current, lower, upper)
+
+
+def swap(pieces):
+    ndev = len(pieces)
+    half = ndev // 2
+    got = [pieces[0]] + [None] * (ndev - 1)
+    for r in list(range(half, ndev)) + list(range(1, half)):
+        got[r] = lax.ppermute(pieces[r], "wide", [(i, i ^ r) for i in range(ndev)])
+    return got
+
+
+def fast(gains, response, student, blocks, order, lower, upper, lengths, amplitude):
+    ndev = lax.axis_size("wide")
+    chd, epochs = gains.shape
+    epd = epochs // ndev
+    half = ndev // 2
+    me = lax.axis_index("wide").astype(jnp.int32).reshape(1)
+    low, high = lower[:, None], upper[:, None]
+
+    packed = pack(me, gains, ndev, epd)
+    got = swap(packed)
+    weights = dense(me, blocks, order, ndev)
+    resp = flip(me, response, ndev)
+    stud = flip(me, student, ndev)
+    squares = (lengths * lengths * LN2)[None, :]
+    scales = jnp.log2(amplitude * jnp.sqrt(lengths * math.sqrt(2.0 * LN2)))[None, :]
+    groups = [list(range(half)), list(range(half, half + half // 2)), list(range(half + half // 2, ndev))]
+    rows = [covar(me, squares, scales, group, epd) for group in groups]
+    current = gains
+    for step in range(ITERS):
+        misfit = swap(normal(weights, got, resp, stud))
+        total = smooth([misfit[r] for r in groups[0]], rows[0], None)
+        total = smooth([misfit[r] for r in groups[1]], rows[1], total)
+        last = step == ITERS - 1
+        current, *packed = update(me, [misfit[r] for r in groups[2]], rows[2], total, current, low, high, last)
+        if not last:
+            got = swap(packed)
+    return current
 
 
 def covar_stack(lengths, amplitude, span):
@@ -25,7 +350,7 @@
             * jnp.sqrt(2.0 * left * right / denom)
             * jnp.exp(-diff * diff / denom)
         )
-        return vals.astype(jnp.bfloat16)
+        return vals.astype(BF16)
 
     return lax.map(one_block, jnp.arange(count, dtype=jnp.int32))
 
@@ -34,14 +359,12 @@
     rows, chans = packed.shape
     nblk, width = (blocks.shape[0], blocks.shape[1])
     moved = jnp.take(packed, order, axis=1).reshape(rows, nblk, width)
-    product = jnp.einsum("rbi,bij->rbj", moved, blocks, preferred_element_type=jnp.float32).reshape(
-        rows, chans
-    )
-    permuted = stud_perm.astype(jnp.float32) * (product - resp_perm.astype(jnp.float32))
-    return jnp.take(permuted, inverse, axis=1).astype(jnp.bfloat16)
-
-
-def per_device(gains, response, student, blocks, order, lower, upper, lengths, amplitude):
+    product = jnp.einsum("rbi,bij->rbj", moved, blocks, preferred_element_type=F32).reshape(rows, chans)
+    permuted = stud_perm.astype(F32) * (product - resp_perm.astype(F32))
+    return jnp.take(permuted, inverse, axis=1).astype(BF16)
+
+
+def general(gains, response, student, blocks, order, lower, upper, lengths, amplitude):
     nwide = lax.axis_size("wide")
     chd, epochs = gains.shape
     epd = epochs // nwide
@@ -53,7 +376,7 @@
     kernel_stack = covar_stack(lengths, amplitude, span)
     current = gains
     for step in range(ITERS):
-        packed = current.astype(jnp.bfloat16).reshape(chd, nwide, epd)
+        packed = current.astype(BF16).reshape(chd, nwide, epd)
         got = (
             lax.all_to_all(packed, "wide", split_axis=1, concat_axis=0, tiled=True)
             .reshape(chans, epd)
@@ -63,11 +386,18 @@
         misfit = lax.all_to_all(
             misfit_rows.T.reshape(chans, 1, epd), "wide", split_axis=0, concat_axis=1, tiled=True
         ).reshape(chd, epochs)
-        smoothed = jnp.einsum(
-            "ce,bes->cbs", misfit, kernel_stack, preferred_element_type=jnp.float32
-        ).reshape(chd, epochs)
+        smoothed = jnp.einsum("ce,bes->cbs", misfit, kernel_stack, preferred_element_type=F32).reshape(
+            chd, epochs
+        )
         current = jnp.clip(current - 0.02 * smoothed, lower[:, None], upper[:, None])
     return current
+
+
+def per_device(*args):
+    ndev = lax.axis_size("wide")
+    chd, epochs = args[0].shape
+    fits = ndev >= 4 and ndev & (ndev - 1) == 0 and chd % 128 == 0 and (epochs // ndev) % 256 == 0
+    return (fast if fits else general)(*args)
 
 
 def solution(mesh):

time: 354 us -> 181 us (0.51)
  local copies, waits for them, and re-layouts: 141 us -> 17.1 us
  other arithmetic: 86.7 us -> 0.02 us
  Pallas kernels: 0 us -> 72.5 us
  blocking collectives: 59.2 us -> 0 us
  starting transfers between devices: 11.5 us -> 51.1 us
  matrix products: 35.7 us -> 0 us
  waiting for transfers between devices: 7.01 us -> 39.3 us
  loops' own time: 10.7 us -> 0 us
    convert_element_type x17 -> x0, other arithmetic: 75.8 us -> none  [the longest x16 74 us: one_block(): return vals.astype(jnp.bfloat16)]
    pallas_call x0 -> x15, Pallas kernels: none -> 72.5 us  [the longest x3 27.7 us: covar(): pl.pallas_call(body, out_shape=jax.ShapeDtypeStruct((count, total), BF16)...]
    dynamic_update_slice x32 -> x0, local copies, waits for them, and re-layouts: 70.1 us -> none  [covar_stack(): return lax.map(one_block, jnp.arange(count, dtype=jnp.int32))]
    all_to_all x2 -> x0, blocking collectives: 59.2 us -> none  [the longest x1 30.6 us: per_device(): lax.all_to_all(packed, 'wide', split_axis=1, concat_axis=0, tiled=True)]
    ppermute x0 -> x28, starting transfers between devices: none -> 51.1 us  [swap(): got[r] = lax.ppermute(pieces[r], 'wide', [(i, i ^ r) for i in range(ndev)])]
    ppermute x0 -> x28, waiting for transfers between devices: none -> 39.3 us  [swap(): got[r] = lax.ppermute(pieces[r], 'wide', [(i, i ^ r) for i in range(ndev)])]
    dot_general x4 -> x0, matrix products: 35.7 us -> none  [the longest x2 34.7 us: per_device(): jnp.einsum('ce,bes->cbs', misfit, kernel_stack, preferred_element_type=jn...]
    gather x6 -> x0, local copies, waits for them, and re-layouts: 27.4 us -> none  [the longest x2 7.93 us: data_rows(): return jnp.take(permuted, inverse, axis=1).astype(jnp.bfloat16)]
  transfers between devices with their start and end apart: 2 -> 28, of which waited for: 1 -> 7; matrix products, arithmetic and copies ran while one was open for 50% -> 0% of each run, Pallas kernels for 0% -> 30%
where the time goes in v1:
time: 181 us; the launch traced here: 180 us
  Pallas kernels  72.5 us (40%)
  starting transfers between devices  51.1 us (28%)
  waiting for transfers between devices  39.3 us (22%)
  local copies, waits for them, and re-layouts  17.1 us (9%)
    ppermute x28, starting transfers between devices, swap(): got[r] = lax.ppermute(pieces[r], 'wide', [(i, i ^ r) for i in range(ndev)])  51.1 us
    ppermute x28, waiting for transfers between devices, swap(): got[r] = lax.ppermute(pieces[r], 'wide', [(i, i ^ r) for i in range(ndev)])  39.3 us
    pallas_call x3, Pallas kernels, covar(): pl.pallas_call(body, out_shape=jax.ShapeDtypeStruct((count, total), BF16)...  27.7 us
    pallas_call x4, Pallas kernels, smooth(): pl.pallas_call(body, out_shape=jax.ShapeDtypeStruct((chd, total), F32), g...  17.1 us
    unnamed x54, local copies, waits for them, and re-layouts  16.8 us
    pallas_call x2, Pallas kernels, update(): pl.pallas_call(body, out_shape=[jax.ShapeDtypeStruct((chd, total), F32)]...  9.5 us
    pallas_call x2, Pallas kernels, normal(): pl.pallas_call(body, out_shape=[jax.ShapeDtypeStruct((chd, epd), BF16)] *...  8.05 us
    pallas_call x1, Pallas kernels, dense(): pl.pallas_call(body, out_shape=jax.ShapeDtypeStruct((chans, chans), BF16)...  6.05 us
  transfers between devices with their start and end apart: 28, of which 7 were waited for; matrix products, arithmetic and copies ran while one was open for 0% of the time, Pallas kernels for 30%

profile of v1, /device:TPU:0, one launch (start us, length us, event | category | flops | bytes accessed | tf_op | source)
XLA Modules:
  0.0 180.4 jit_solution(13121784666945412073)
XLA Ops:
  4.5 3.0 %collective-permute-start = (bf16[128,512]{1,0:T(8,128)(2,1)}, bf16[128,512]{1,0:T(8,128)(2,1)S(1)}, u32[]{:S(2)}, u32[]{:S(2)}) collective-permute-start(bf16[128,512]{1,0:T(8,128)(2,1)} %get-tuple-element.39), channel_id=1, source_target_pairs={{0,1},{1,0},{2,3},{3,2},{4,5},{5,4},{6,7},{7,6},{8,9},{9,8},{10,11... | collective-permute-start | bytes 393224 | tf_op jit(solution)/shard_map/ppermute | solution.py:301
  9.0 3.0 %collective-permute-start.3 = (bf16[128,512]{1,0:T(8,128)(2,1)}, bf16[128,512]{1,0:T(8,128)(2,1)}, u32[]{:S(2)}, u32[]{:S(2)}) collective-permute-start(bf16[128,512]{1,0:T(8,128)(2,1)} %get-tuple-element.42), channel_id=1, source_target_pairs={{0,4},{1,5},{2,6},{3,7},{4,0},{5,1},{6,2},{7,3},{8,12},{9,13},{10,... | collective-permute-start | bytes 393224 | tf_op jit(solution)/shard_map/ppermute | solution.py:301
  15.9 3.7 %collective-permute-start.5 = (bf16[128,512]{1,0:T(8,128)(2,1)S(1)}, bf16[128,512]{1,0:T(8,128)(2,1)S(1)}, u32[]{:S(2)}, u32[]{:S(2)}) collective-permute-start(bf16[128,512]{1,0:T(8,128)(2,1)S(1)} %copy-done.21), channel_id=1, source_target_pairs={{0,6},{1,7},{2,4},{3,5},{4,2},{5,3},{6,0},{7,1},{8,14},{9,15},{10,... | collective-permute-start | bytes 393224 | tf_op jit(solution)/shard_map/ppermute | solution.py:301
  19.6 6.1 %dense_blocks.1.refs_0_ = bf16[1024,1024]{1,0:T(8,128)(2,1)S(1)} custom-call(s32[1]{0:T(128)} %bitcast.me_ref.refs_0_, bf16[4,256,256]{2,1,0:T(8,128)(2,1)S(1)} %copy-done.13, s32[4,256]{1,0:T(4,128)S(1)} %reshape.7.order_ref), custom_call_target="tpu_custom_call" | custom-call | flops 2684354560 | bytes 2097152 | tf_op jit(solution)/shard_map/dense_blocks/pallas_call | solution.py:96
  25.7 6.0 %collective-permute-done.4.refs_8_ = bf16[128,512]{1,0:T(8,128)(2,1)} collective-permute-done((bf16[128,512]{1,0:T(8,128)(2,1)}, bf16[128,512]{1,0:T(8,128)(2,1)}, u32[]{:S(2)}, u32[]{:S(2)}) %collective-permute-start.4) | collective-permute-done | bytes 131104 | tf_op jit(solution)/shard_map/ppermute | solution.py:301
  31.8 5.0 %normal_step.2 = (bf16[128,512]{1,0:T(8,128)(2,1)S(1)}, bf16[128,512]{1,0:T(8,128)(2,1)}, bf16[128,512]{1,0:T(8,128)(2,1)}, bf16[128,512]{1,0:T(8,128)(2,1)}, bf...) custom-call(bf16[1024,1024]{1,0:T(8,128)(2,1)S(1)} %dense_blocks.1.r, ...), custom_call_target="tpu_custom_call" | custom-call | flops 1073741824 | bytes 6291456 | tf_op jit(solution)/shard_map/normal_step/pallas_call | solution.py:198
  38.6 4.8 %collective-permute-start.12 = (bf16[128,512]{1,0:T(8,128)(2,1)}, bf16[128,512]{1,0:T(8,128)(2,1)S(1)}, u32[]{:S(2)}, u32[]{:S(2)}) collective-permute-start(bf16[128,512]{1,0:T(8,128)(2,1)} %get-tuple-element.52), channel_id=1, source_target_pairs={{0,2},{1,3},{2,0},{3,1},{4,6},{5,7},{6,4},{7,5},{8,10},{9,11},{10,... | collective-permute-start | bytes 393224 | tf_op jit(solution)/shard_map/ppermute | solution.py:301
  44.8 6.9 %covar_rows.4.refs_2_ = bf16[1024,4096]{1,0:T(8,128)(2,1)S(1)} custom-call(s32[1]{0:T(128)} %bitcast.me_ref.refs_0_, f32[1,4096]{1,0:T(1,128)S(1)} %bitcast.11, f32[1,4096]{1,0:T(1,128)S(1)} %bitcast.5, f32[1,4096]{1,0:T(1,128)S(1)} %bitcast.12, f32[1,4096]{1,0:T(1,128)S(1)} %bitcast.6), custom_call_target="tpu_custom_call" | custom-call | flops 67108864 | bytes 8388608 | tf_op jit(solution)/shard_map/covar_rows/pallas_call | solution.py:147
  51.7 6.9 %covar_rows.3.refs_3_ = bf16[1024,4096]{1,0:T(8,128)(2,1)S(1)} custom-call(s32[1]{0:T(128)} %bitcast.me_ref.refs_0_, f32[1,4096]{1,0:T(1,128)S(1)} %bitcast.13, f32[1,4096]{1,0:T(1,128)S(1)} %bitcast.7, f32[1,4096]{1,0:T(1,128)S(1)} %bitcast.14, f32[1,4096]{1,0:T(1,128)S(1)} %bitcast.8), custom_call_target="tpu_custom_call" | custom-call | flops 67108864 | bytes 8388608 | tf_op jit(solution)/shard_map/covar_rows/pallas_call | solution.py:147
  58.7 13.8 %covar_rows.5.refs_4_ = bf16[2048,4096]{1,0:T(8,128)(2,1)S(1)} custom-call(s32[1]{0:T(128)} %bitcast.me_ref.refs_0_, f32[1,4096]{1,0:T(1,128)S(1)} %bitcast.15, f32[1,4096]{1,0:T(1,128)S(1)} %bitcast.9, f32[1,4096]{1,0:T(1,128)S(1)} %bitcast.16, f32[1,4096]{1,0:T(1,128)S(1)} %bitcast.10), custom_call_target="tpu_custom_call" | custom-call | flops 134217728 | bytes 16777216 | tf_op jit(solution)/shard_map/covar_rows/pallas_call | solution.py:147
  72.6 3.0 %collective-permute-start.7 = (bf16[128,512]{1,0:T(8,128)(2,1)}, bf16[128,512]{1,0:T(8,128)(2,1)S(1)}, u32[]{:S(2)}, u32[]{:S(2)}) collective-permute-start(bf16[128,512]{1,0:T(8,128)(2,1)} %get-tuple-element.46), channel_id=1, source_target_pairs={{0,6},{1,7},{2,4},{3,5},{4,2},{5,3},{6,0},{7,1},{8,14},{9,15},{10,... | collective-permute-start | bytes 393224 | tf_op jit(solution)/shard_map/ppermute | solution.py:301
  78.2 2.1 %collective-permute-start.10 = (bf16[128,512]{1,0:T(8,128)(2,1)S(1)}, bf16[128,512]{1,0:T(8,128)(2,1)S(1)}, u32[]{:S(2)}, u32[]{:S(2)}) collective-permute-start(bf16[128,512]{1,0:T(8,128)(2,1)S(1)} %copy-done.15), channel_id=1, source_target_pairs={{0,5},{1,4},{2,7},{3,6},{4,1},{5,0},{6,3},{7,2},{8,13},{9,12},{10,... | collective-permute-start | bytes 393224 | tf_op jit(solution)/shard_map/ppermute | solution.py:301
  80.3 5.1 %smooth_part.4.refs_3_ = f32[128,4096]{1,0:T(8,128)S(1)} custom-call(bf16[128,512]{1,0:T(8,128)(2,1)S(1)} %get-tuple-element.50.refs_0_, bf16[128,512]{1,0:T(8,128)(2,1)S(1)} %collective-permute-done.11.refs_1_, bf16[128,512]{1,0:T(8,128)(2,1)S(1)} %collective-permute-done.12.refs_2_, bf16[128,512]{1,0:T(8,128)(2,1)S(1)} %collective-permute-done.13.refs_3_, ...), custom_call_target="tpu_custom_call" | custom-call | flops 2147483648 | bytes 18874368 | tf_op jit(solution)/shard_map/smooth_part/pallas_call | solution.py:234
  85.4 10.8 %collective-permute-done.9.refs_0_ = bf16[128,512]{1,0:T(8,128)(2,1)S(1)} collective-permute-done((bf16[128,512]{1,0:T(8,128)(2,1)S(1)}, bf16[128,512]{1,0:T(8,128)(2,1)S(1)}, u32[]{:S(2)}, u32[]{:S(2)}) %collective-permute-start.9) | collective-permute-done | bytes 131104 | tf_op jit(solution)/shard_map/ppermute | solution.py:301
  97.3 3.4 %copy-done.3 = bf16[1024,4096]{1,0:T(8,128)(2,1)S(1)} copy-done((bf16[1024,4096]{1,0:T(8,128)(2,1)S(1)}, bf16[1024,4096]{1,0:T(8,128)(2,1)}, u32[]{:S(2)}) %copy-start.3) | copy-done | bytes 8388632
  100.7 3.5 %smooth_part.5.refs_4_ = f32[128,4096]{1,0:T(8,128)S(1)} custom-call(bf16[128,512]{1,0:T(8,128)(2,1)S(1)} %collective-permute-done.9.refs_0_, bf16[128,512]{1,0:T(8,128)(2,1)S(1)} %collective-permute-done.10.refs_1_, bf16[1024,4096]{1,0:T(8,128)(2,1)S(1)} %copy-done.3, f32[128,4096]{1,0:T(8,128)S(1)} %smooth_part.4.refs_3_), custom_call_target="tpu_custom_call" | custom-call | flops 1073741824 | bytes 10485760 | tf_op jit(solution)/shard_map/smooth_part/pallas_call | solution.py:234
  104.2 4.4 %update.2 = (f32[128,4096]{1,0:T(8,128)S(1)}, bf16[128,512]{1,0:T(8,128)(2,1)S(1)}, bf16[128,512]{1,0:T(8,128)(2,1)S(1)}, bf16[128,512]{1,0:T(8,128)(2,1)S(1)}, ...) custom-call(s32[1]{0:T(128)} %bitcast.me_ref.refs_0_, ...), custom_call_target="tpu_custom_call" | custom-call | flops 1073741824 | bytes 15728640 | tf_op jit(solution)/shard_map/update/pallas_call | solution.py:279
  113.6 2.7 %collective-permute-start.18 = (bf16[128,512]{1,0:T(8,128)(2,1)S(1)}, bf16[128,512]{1,0:T(8,128)(2,1)S(1)}, u32[]{:S(2)}, u32[]{:S(2)}) collective-permute-start(bf16[128,512]{1,0:T(8,128)(2,1)S(1)} %get-tuple-element.59), channel_id=1, source_target_pairs={{0,5},{1,4},{2,7},{3,6},{4,1},{5,0},{6,3},{7,2},{8,13},{9,12},{10,... | collective-permute-start | bytes 393224 | tf_op jit(solution)/shard_map/ppermute | solution.py:301
  116.3 2.6 %collective-permute-start.19 = (bf16[128,512]{1,0:T(8,128)(2,1)S(1)}, bf16[128,512]{1,0:T(8,128)(2,1)S(1)}, u32[]{:S(2)}, u32[]{:S(2)}) collective-permute-start(bf16[128,512]{1,0:T(8,128)(2,1)S(1)} %get-tuple-element.60), channel_id=1, source_target_pairs={{0,6},{1,7},{2,4},{3,5},{4,2},{5,3},{6,0},{7,1},{8,14},{9,15},{10,... | collective-permute-start | bytes 393224 | tf_op jit(solution)/shard_map/ppermute | solution.py:301
  119.8 10.8 %collective-permute-done.17.refs_7_ = bf16[128,512]{1,0:T(8,128)(2,1)S(1)} collective-permute-done((bf16[128,512]{1,0:T(8,128)(2,1)S(1)}, bf16[128,512]{1,0:T(8,128)(2,1)S(1)}, u32[]{:S(2)}, u32[]{:S(2)}) %collective-permute-start.17) | collective-permute-done | bytes 131104 | tf_op jit(solution)/shard_map/ppermute | solution.py:301
  130.7 3.5 %collective-permute-done.18.refs_8_ = bf16[128,512]{1,0:T(8,128)(2,1)S(1)} collective-permute-done((bf16[128,512]{1,0:T(8,128)(2,1)S(1)}, bf16[128,512]{1,0:T(8,128)(2,1)S(1)}, u32[]{:S(2)}, u32[]{:S(2)}) %collective-permute-start.18) | collective-permute-done | bytes 131104 | tf_op jit(solution)/shard_map/ppermute | solution.py:301
  134.2 3.1 %normal_step.3 = (bf16[128,512]{1,0:T(8,128)(2,1)S(1)}, bf16[128,512]{1,0:T(8,128)(2,1)S(1)}, bf16[128,512]{1,0:T(8,128)(2,1)S(1)}, bf16[128,512]{1,0:T(8,128)(2...) custom-call(bf16[1024,1024]{1,0:T(8,128)(2,1)S(1)} %copy-done.8, ...), custom_call_target="tpu_custom_call" | custom-call | flops 1073741824 | bytes 6291456 | tf_op jit(solution)/shard_map/normal_step/pallas_call | solution.py:198
  138.1 4.6 %collective-permute-start.26 = (bf16[128,512]{1,0:T(8,128)(2,1)S(1)}, bf16[128,512]{1,0:T(8,128)(2,1)S(1)}, u32[]{:S(2)}, u32[]{:S(2)}) collective-permute-start(bf16[128,512]{1,0:T(8,128)(2,1)S(1)} %get-tuple-element.68), channel_id=1, source_target_pairs={{0,2},{1,3},{2,0},{3,1},{4,6},{5,7},{6,4},{7,5},{8,10},{9,11},{10,... | collective-permute-start | bytes 393224 | tf_op jit(solution)/shard_map/ppermute | solution.py:301
  142.7 2.9 %collective-permute-start.21 = (bf16[128,512]{1,0:T(8,128)(2,1)S(1)}, bf16[128,512]{1,0:T(8,128)(2,1)S(1)}, u32[]{:S(2)}, u32[]{:S(2)}) collective-permute-start(bf16[128,512]{1,0:T(8,128)(2,1)S(1)} %get-tuple-element.62), channel_id=1, source_target_pairs={{0,6},{1,7},{2,4},{3,5},{4,2},{5,3},{6,0},{7,1},{8,14},{9,15},{10,... | collective-permute-start | bytes 393224 | tf_op jit(solution)/shard_map/ppermute | solution.py:301
  147.5 2.1 %collective-permute-start.23 = (bf16[128,512]{1,0:T(8,128)(2,1)S(1)}, bf16[128,512]{1,0:T(8,128)(2,1)S(1)}, u32[]{:S(2)}, u32[]{:S(2)}) collective-permute-start(bf16[128,512]{1,0:T(8,128)(2,1)S(1)} %get-tuple-element.64), channel_id=1, source_target_pairs={{0,4},{1,5},{2,6},{3,7},{4,0},{5,1},{6,2},{7,3},{8,12},{9,13},{10,... | collective-permute-start | bytes 393224 | tf_op jit(solution)/shard_map/ppermute | solution.py:301
  150.6 5.8 %copy-done.1 = bf16[2048,4096]{1,0:T(8,128)(2,1)S(1)} copy-done((bf16[2048,4096]{1,0:T(8,128)(2,1)S(1)}, bf16[2048,4096]{1,0:T(8,128)(2,1)}, u32[]{:S(2)}) %copy-start.1) | copy-done | bytes 16777240
  156.3 5.1 %smooth_part.6.refs_3_ = f32[128,4096]{1,0:T(8,128)S(1)} custom-call(bf16[128,512]{1,0:T(8,128)(2,1)S(1)} %get-tuple-element.66.refs_0_, bf16[128,512]{1,0:T(8,128)(2,1)S(1)} %collective-permute-done.25.refs_1_, bf16[128,512]{1,0:T(8,128)(2,1)S(1)} %collective-permute-done.26.refs_2_, bf16[128,512]{1,0:T(8,128)(2,1)S(1)} %collective-permute-done.27.refs_3_, ...), custom_call_target="tpu_custom_call" | custom-call | flops 2147483648 | bytes 18874368 | tf_op jit(solution)/shard_map/smooth_part/pallas_call | solution.py:234
  161.4 4.6 %collective-permute-done.23.refs_0_ = bf16[128,512]{1,0:T(8,128)(2,1)S(1)} collective-permute-done((bf16[128,512]{1,0:T(8,128)(2,1)S(1)}, bf16[128,512]{1,0:T(8,128)(2,1)S(1)}, u32[]{:S(2)}, u32[]{:S(2)}) %collective-permute-start.23) | collective-permute-done | bytes 131104 | tf_op jit(solution)/shard_map/ppermute | solution.py:301
  166.0 2.4 %collective-permute-done.24.refs_1_ = bf16[128,512]{1,0:T(8,128)(2,1)S(1)} collective-permute-done((bf16[128,512]{1,0:T(8,128)(2,1)S(1)}, bf16[128,512]{1,0:T(8,128)(2,1)S(1)}, u32[]{:S(2)}, u32[]{:S(2)}) %collective-permute-start.24) | collective-permute-done | bytes 131104 | tf_op jit(solution)/shard_map/ppermute | solution.py:301
  168.4 3.4 %copy-done.4 = bf16[1024,4096]{1,0:T(8,128)(2,1)S(1)} copy-done((bf16[1024,4096]{1,0:T(8,128)(2,1)S(1)}, bf16[1024,4096]{1,0:T(8,128)(2,1)}, u32[]{:S(2)}) %copy-start.4) | copy-done | bytes 8388632
  171.8 3.5 %smooth_part.7.refs_4_ = f32[128,4096]{1,0:T(8,128)S(1)} custom-call(bf16[128,512]{1,0:T(8,128)(2,1)S(1)} %collective-permute-done.23.refs_0_, bf16[128,512]{1,0:T(8,128)(2,1)S(1)} %collective-permute-done.24.refs_1_, bf16[1024,4096]{1,0:T(8,128)(2,1)S(1)} %copy-done.4, f32[128,4096]{1,0:T(8,128)S(1)} %smooth_part.6.refs_3_), custom_call_target="tpu_custom_call" | custom-call | flops 1073741824 | bytes 10485760 | tf_op jit(solution)/shard_map/smooth_part/pallas_call | solution.py:234
  175.3 5.1 %update.3 = f32[128,4096]{1,0:T(8,128)} custom-call(s32[1]{0:T(128)} %bitcast.me_ref.refs_0_, bf16[128,512]{1,0:T(8,128)(2,1)S(1)} %collective-permute-done.21.refs_1_, bf16[128,512]{1,0:T(8,128)(2,1)S(1)} %collective-permute-done.22.refs_2_, bf16[1024,4096]{1,0:T(8,128)(2,1)S(1)} %covar_rows.3.refs_3_, f32[128,4096]{1,0:T(8,128)S(1)} %smooth_part.7.refs_4_, ...), custom_call_target="tpu_custom_call" | custom-call | flops 1073741824 | bytes 15728640 | tf_op jit(solution)/shard_map/update/pallas_call | solution.py:279
  (97 shorter events, 26.5 us)
Async XLA Ops:
  4.5 11.4 %collective-permute-start = (bf16[128,512]{1,0:T(8,128)(2,1)}, bf16[128,512]{1,0:T(8,128)(2,1)S(1)}, u32[]{:S(2)}, u32[]{:S(2)}) collective-permute-start(bf16[128,512]{1,0:T(8,128)(2,1)} %get-tuple-element.39), channel_id=1, source_target_pairs={{0,1},{1,0},{2,3},{3,2},{4,5},{5,4},{6,7},{7,6},{8,9},{9,8},{10,11... | collective-permute-start | bytes 393224 | tf_op jit(solution)/shard_map/ppermute | solution.py:301
  7.5 12.2 %collective-permute-start.1 = (bf16[128,512]{1,0:T(8,128)(2,1)}, bf16[128,512]{1,0:T(8,128)(2,1)S(1)}, u32[]{:S(2)}, u32[]{:S(2)}) collective-permute-start(bf16[128,512]{1,0:T(8,128)(2,1)} %get-tuple-element.40), channel_id=1, source_target_pairs={{0,2},{1,3},{2,0},{3,1},{4,6},{5,7},{6,4},{7,5},{8,10},{9,11},{10,... | collective-permute-start | bytes 393224 | tf_op jit(solution)/shard_map/ppermute | solution.py:301
  9.0 16.7 %collective-permute-start.2 = (bf16[128,512]{1,0:T(8,128)(2,1)}, bf16[128,512]{1,0:T(8,128)(2,1)}, u32[]{:S(2)}, u32[]{:S(2)}) collective-permute-start(bf16[128,512]{1,0:T(8,128)(2,1)} %get-tuple-element.41), channel_id=1, source_target_pairs={{0,3},{1,2},{2,1},{3,0},{4,7},{5,6},{6,5},{7,4},{8,11},{9,10},{10,... | collective-permute-start | bytes 393224 | tf_op jit(solution)/shard_map/ppermute | solution.py:301
  9.0 16.7 %collective-permute-start.3 = (bf16[128,512]{1,0:T(8,128)(2,1)}, bf16[128,512]{1,0:T(8,128)(2,1)}, u32[]{:S(2)}, u32[]{:S(2)}) collective-permute-start(bf16[128,512]{1,0:T(8,128)(2,1)} %get-tuple-element.42), channel_id=1, source_target_pairs={{0,4},{1,5},{2,6},{3,7},{4,0},{5,1},{6,2},{7,3},{8,12},{9,13},{10,... | collective-permute-start | bytes 393224 | tf_op jit(solution)/shard_map/ppermute | solution.py:301
  12.0 19.8 %collective-permute-start.4 = (bf16[128,512]{1,0:T(8,128)(2,1)}, bf16[128,512]{1,0:T(8,128)(2,1)}, u32[]{:S(2)}, u32[]{:S(2)}) collective-permute-start(bf16[128,512]{1,0:T(8,128)(2,1)} %get-tuple-element.43), channel_id=1, source_target_pairs={{0,5},{1,4},{2,7},{3,6},{4,1},{5,0},{6,3},{7,2},{8,13},{9,12},{10,... | collective-permute-start | bytes 393224 | tf_op jit(solution)/shard_map/ppermute | solution.py:301
  15.9 15.8 %collective-permute-start.5 = (bf16[128,512]{1,0:T(8,128)(2,1)S(1)}, bf16[128,512]{1,0:T(8,128)(2,1)S(1)}, u32[]{:S(2)}, u32[]{:S(2)}) collective-permute-start(bf16[128,512]{1,0:T(8,128)(2,1)S(1)} %copy-done.21), channel_id=1, source_target_pairs={{0,6},{1,7},{2,4},{3,5},{4,2},{5,3},{6,0},{7,1},{8,14},{9,15},{10,... | collective-permute-start | bytes 393224 | tf_op jit(solution)/shard_map/ppermute | solution.py:301
  19.6 12.2 %collective-permute-start.6 = (bf16[128,512]{1,0:T(8,128)(2,1)S(1)}, bf16[128,512]{1,0:T(8,128)(2,1)S(1)}, u32[]{:S(2)}, u32[]{:S(2)}) collective-permute-start(bf16[128,512]{1,0:T(8,128)(2,1)S(1)} %copy-done.19), channel_id=1, source_target_pairs={{0,7},{1,6},{2,5},{3,4},{4,3},{5,2},{6,1},{7,0},{8,15},{9,14},{10,... | collective-permute-start | bytes 393224 | tf_op jit(solution)/shard_map/ppermute | solution.py:301
  38.1 38.4 %collective-permute-start.11 = (bf16[128,512]{1,0:T(8,128)(2,1)}, bf16[128,512]{1,0:T(8,128)(2,1)S(1)}, u32[]{:S(2)}, u32[]{:S(2)}) collective-permute-start(bf16[128,512]{1,0:T(8,128)(2,1)} %get-tuple-element.51), channel_id=1, source_target_pairs={{0,1},{1,0},{2,3},{3,2},{4,5},{5,4},{6,7},{7,6},{8,9},{9,8},{10,11... | collective-permute-start | bytes 393224 | tf_op jit(solution)/shard_map/ppermute | solution.py:301
  38.6 39.6 %collective-permute-start.12 = (bf16[128,512]{1,0:T(8,128)(2,1)}, bf16[128,512]{1,0:T(8,128)(2,1)S(1)}, u32[]{:S(2)}, u32[]{:S(2)}) collective-permute-start(bf16[128,512]{1,0:T(8,128)(2,1)} %get-tuple-element.52), channel_id=1, source_target_pairs={{0,2},{1,3},{2,0},{3,1},{4,6},{5,7},{6,4},{7,5},{8,10},{9,11},{10,... | collective-permute-start | bytes 393224 | tf_op jit(solution)/shard_map/ppermute | solution.py:301
  43.4 36.9 %collective-permute-start.13 = (bf16[128,512]{1,0:T(8,128)(2,1)}, bf16[128,512]{1,0:T(8,128)(2,1)S(1)}, u32[]{:S(2)}, u32[]{:S(2)}) collective-permute-start(bf16[128,512]{1,0:T(8,128)(2,1)} %get-tuple-element.53), channel_id=1, source_target_pairs={{0,3},{1,2},{2,1},{3,0},{4,7},{5,6},{6,5},{7,4},{8,11},{9,10},{10,... | collective-permute-start | bytes 393224 | tf_op jit(solution)/shard_map/ppermute | solution.py:301
  58.7 19.5 %copy-start.15 = (bf16[128,512]{1,0:T(8,128)(2,1)S(1)}, bf16[128,512]{1,0:T(8,128)(2,1)}, u32[]{:S(2)}) copy-start(bf16[128,512]{1,0:T(8,128)(2,1)} %copy-done.14) | copy-start | bytes 393220
  72.6 31.7 %collective-permute-start.7 = (bf16[128,512]{1,0:T(8,128)(2,1)}, bf16[128,512]{1,0:T(8,128)(2,1)S(1)}, u32[]{:S(2)}, u32[]{:S(2)}) collective-permute-start(bf16[128,512]{1,0:T(8,128)(2,1)} %get-tuple-element.46), channel_id=1, source_target_pairs={{0,6},{1,7},{2,4},{3,5},{4,2},{5,3},{6,0},{7,1},{8,14},{9,15},{10,... | collective-permute-start | bytes 393224 | tf_op jit(solution)/shard_map/ppermute | solution.py:301
  75.6 28.6 %collective-permute-start.8 = (bf16[128,512]{1,0:T(8,128)(2,1)S(1)}, bf16[128,512]{1,0:T(8,128)(2,1)S(1)}, u32[]{:S(2)}, u32[]{:S(2)}) collective-permute-start(bf16[128,512]{1,0:T(8,128)(2,1)S(1)} %get-tuple-element.47), channel_id=1, source_target_pairs={{0,7},{1,6},{2,5},{3,4},{4,3},{5,2},{6,1},{7,0},{8,15},{9,14},{10,... | collective-permute-start | bytes 393224 | tf_op jit(solution)/shard_map/ppermute | solution.py:301
  76.5 19.8 %collective-permute-start.9 = (bf16[128,512]{1,0:T(8,128)(2,1)S(1)}, bf16[128,512]{1,0:T(8,128)(2,1)S(1)}, u32[]{:S(2)}, u32[]{:S(2)}) collective-permute-start(bf16[128,512]{1,0:T(8,128)(2,1)S(1)} %copy-done.17), channel_id=1, source_target_pairs={{0,4},{1,5},{2,6},{3,7},{4,0},{5,1},{6,2},{7,3},{8,12},{9,13},{10,... | collective-permute-start | bytes 393224 | tf_op jit(solution)/shard_map/ppermute | solution.py:301
  78.2 19.1 %collective-permute-start.10 = (bf16[128,512]{1,0:T(8,128)(2,1)S(1)}, bf16[128,512]{1,0:T(8,128)(2,1)S(1)}, u32[]{:S(2)}, u32[]{:S(2)}) collective-permute-start(bf16[128,512]{1,0:T(8,128)(2,1)S(1)} %copy-done.15), channel_id=1, source_target_pairs={{0,5},{1,4},{2,7},{3,6},{4,1},{5,0},{6,3},{7,2},{8,13},{9,12},{10,... | collective-permute-start | bytes 393224 | tf_op jit(solution)/shard_map/ppermute | solution.py:301
  104.2 29.9 %copy-start.8 = (bf16[1024,1024]{1,0:T(8,128)(2,1)S(1)}, bf16[1024,1024]{1,0:T(8,128)(2,1)}, u32[]{:S(2)}) copy-start(bf16[1024,1024]{1,0:T(8,128)(2,1)} %copy-done.7) | copy-start | bytes 6291460
  108.6 28.6 %copy-start.9 = (f32[128,4096]{1,0:T(8,128)}, f32[128,4096]{1,0:T(8,128)S(1)}, u32[]{:S(2)}) copy-start(f32[128,4096]{1,0:T(8,128)S(1)} %get-tuple-element.70.refs_5_) | copy-start | bytes 6291460
  108.6 7.7 %collective-permute-start.14 = (bf16[128,512]{1,0:T(8,128)(2,1)S(1)}, bf16[128,512]{1,0:T(8,128)(2,1)S(1)}, u32[]{:S(2)}, u32[]{:S(2)}) collective-permute-start(bf16[128,512]{1,0:T(8,128)(2,1)S(1)} %get-tuple-element.55), channel_id=1, source_target_pairs={{0,1},{1,0},{2,3},{3,2},{4,5},{5,4},{6,7},{7,6},{8,9},{9,8},{10,11... | collective-permute-start | bytes 393224 | tf_op jit(solution)/shard_map/ppermute | solution.py:301
  110.4 8.5 %collective-permute-start.15 = (bf16[128,512]{1,0:T(8,128)(2,1)S(1)}, bf16[128,512]{1,0:T(8,128)(2,1)S(1)}, u32[]{:S(2)}, u32[]{:S(2)}) collective-permute-start(bf16[128,512]{1,0:T(8,128)(2,1)S(1)} %get-tuple-element.56), channel_id=1, source_target_pairs={{0,2},{1,3},{2,0},{3,1},{4,6},{5,7},{6,4},{7,5},{8,10},{9,11},{10,... | collective-permute-start | bytes 393224 | tf_op jit(solution)/shard_map/ppermute | solution.py:301
  110.4 9.4 %collective-permute-start.16 = (bf16[128,512]{1,0:T(8,128)(2,1)S(1)}, bf16[128,512]{1,0:T(8,128)(2,1)S(1)}, u32[]{:S(2)}, u32[]{:S(2)}) collective-permute-start(bf16[128,512]{1,0:T(8,128)(2,1)S(1)} %get-tuple-element.57), channel_id=1, source_target_pairs={{0,3},{1,2},{2,1},{3,0},{4,7},{5,6},{6,5},{7,4},{8,11},{9,10},{10,... | collective-permute-start | bytes 393224 | tf_op jit(solution)/shard_map/ppermute | solution.py:301
  112.2 18.5 %collective-permute-start.17 = (bf16[128,512]{1,0:T(8,128)(2,1)S(1)}, bf16[128,512]{1,0:T(8,128)(2,1)S(1)}, u32[]{:S(2)}, u32[]{:S(2)}) collective-permute-start(bf16[128,512]{1,0:T(8,128)(2,1)S(1)} %get-tuple-element.58), channel_id=1, source_target_pairs={{0,4},{1,5},{2,6},{3,7},{4,0},{5,1},{6,2},{7,3},{8,12},{9,13},{10,... | collective-permute-start | bytes 393224 | tf_op jit(solution)/shard_map/ppermute | solution.py:301
  113.6 20.5 %collective-permute-start.18 = (bf16[128,512]{1,0:T(8,128)(2,1)S(1)}, bf16[128,512]{1,0:T(8,128)(2,1)S(1)}, u32[]{:S(2)}, u32[]{:S(2)}) collective-permute-start(bf16[128,512]{1,0:T(8,128)(2,1)S(1)} %get-tuple-element.59), channel_id=1, source_target_pairs={{0,5},{1,4},{2,7},{3,6},{4,1},{5,0},{6,3},{7,2},{8,13},{9,12},{10,... | collective-permute-start | bytes 393224 | tf_op jit(solution)/shard_map/ppermute | solution.py:301
  116.3 17.8 %collective-permute-start.19 = (bf16[128,512]{1,0:T(8,128)(2,1)S(1)}, bf16[128,512]{1,0:T(8,128)(2,1)S(1)}, u32[]{:S(2)}, u32[]{:S(2)}) collective-permute-start(bf16[128,512]{1,0:T(8,128)(2,1)S(1)} %get-tuple-element.60), channel_id=1, source_target_pairs={{0,6},{1,7},{2,4},{3,5},{4,2},{5,3},{6,0},{7,1},{8,14},{9,15},{10,... | collective-permute-start | bytes 393224 | tf_op jit(solution)/shard_map/ppermute | solution.py:301
  118.9 15.2 %collective-permute-start.20 = (bf16[128,512]{1,0:T(8,128)(2,1)S(1)}, bf16[128,512]{1,0:T(8,128)(2,1)S(1)}, u32[]{:S(2)}, u32[]{:S(2)}) collective-permute-start(bf16[128,512]{1,0:T(8,128)(2,1)S(1)} %get-tuple-element.61), channel_id=1, source_target_pairs={{0,7},{1,6},{2,5},{3,4},{4,3},{5,2},{6,1},{7,0},{8,15},{9,14},{10,... | collective-permute-start | bytes 393224 | tf_op jit(solution)/shard_map/ppermute | solution.py:301
  137.2 10.2 %collective-permute-start.25 = (bf16[128,512]{1,0:T(8,128)(2,1)S(1)}, bf16[128,512]{1,0:T(8,128)(2,1)S(1)}, u32[]{:S(2)}, u32[]{:S(2)}) collective-permute-start(bf16[128,512]{1,0:T(8,128)(2,1)S(1)} %get-tuple-element.67), channel_id=1, source_target_pairs={{0,1},{1,0},{2,3},{3,2},{4,5},{5,4},{6,7},{7,6},{8,9},{9,8},{10,11... | collective-permute-start | bytes 393224 | tf_op jit(solution)/shard_map/ppermute | solution.py:301
  138.1 11.5 %collective-permute-start.26 = (bf16[128,512]{1,0:T(8,128)(2,1)S(1)}, bf16[128,512]{1,0:T(8,128)(2,1)S(1)}, u32[]{:S(2)}, u32[]{:S(2)}) collective-permute-start(bf16[128,512]{1,0:T(8,128)(2,1)S(1)} %get-tuple-element.68), channel_id=1, source_target_pairs={{0,2},{1,3},{2,0},{3,1},{4,6},{5,7},{6,4},{7,5},{8,10},{9,11},{10,... | collective-permute-start | bytes 393224 | tf_op jit(solution)/shard_map/ppermute | solution.py:301
  142.7 7.8 %collective-permute-start.27 = (bf16[128,512]{1,0:T(8,128)(2,1)S(1)}, bf16[128,512]{1,0:T(8,128)(2,1)S(1)}, u32[]{:S(2)}, u32[]{:S(2)}) collective-permute-start(bf16[128,512]{1,0:T(8,128)(2,1)S(1)} %get-tuple-element.69), channel_id=1, source_target_pairs={{0,3},{1,2},{2,1},{3,0},{4,7},{5,6},{6,5},{7,4},{8,11},{9,10},{10,... | collective-permute-start | bytes 393224 | tf_op jit(solution)/shard_map/ppermute | solution.py:301
  142.7 32.5 %collective-permute-start.21 = (bf16[128,512]{1,0:T(8,128)(2,1)S(1)}, bf16[128,512]{1,0:T(8,128)(2,1)S(1)}, u32[]{:S(2)}, u32[]{:S(2)}) collective-permute-start(bf16[128,512]{1,0:T(8,128)(2,1)S(1)} %get-tuple-element.62), channel_id=1, source_target_pairs={{0,6},{1,7},{2,4},{3,5},{4,2},{5,3},{6,0},{7,1},{8,14},{9,15},{10,... | collective-permute-start | bytes 393224 | tf_op jit(solution)/shard_map/ppermute | solution.py:301
  145.6 29.7 %collective-permute-start.22 = (bf16[128,512]{1,0:T(8,128)(2,1)S(1)}, bf16[128,512]{1,0:T(8,128)(2,1)S(1)}, u32[]{:S(2)}, u32[]{:S(2)}) collective-permute-start(bf16[128,512]{1,0:T(8,128)(2,1)S(1)} %get-tuple-element.63), channel_id=1, source_target_pairs={{0,7},{1,6},{2,5},{3,4},{4,3},{5,2},{6,1},{7,0},{8,15},{9,14},{10,... | collective-permute-start | bytes 393224 | tf_op jit(solution)/shard_map/ppermute | solution.py:301
  147.5 18.6 %collective-permute-start.23 = (bf16[128,512]{1,0:T(8,128)(2,1)S(1)}, bf16[128,512]{1,0:T(8,128)(2,1)S(1)}, u32[]{:S(2)}, u32[]{:S(2)}) collective-permute-start(bf16[128,512]{1,0:T(8,128)(2,1)S(1)} %get-tuple-element.64), channel_id=1, source_target_pairs={{0,4},{1,5},{2,6},{3,7},{4,0},{5,1},{6,2},{7,3},{8,12},{9,13},{10,... | collective-permute-start | bytes 393224 | tf_op jit(solution)/shard_map/ppermute | solution.py:301
  149.6 18.8 %collective-permute-start.24 = (bf16[128,512]{1,0:T(8,128)(2,1)S(1)}, bf16[128,512]{1,0:T(8,128)(2,1)S(1)}, u32[]{:S(2)}, u32[]{:S(2)}) collective-permute-start(bf16[128,512]{1,0:T(8,128)(2,1)S(1)} %get-tuple-element.65), channel_id=1, source_target_pairs={{0,5},{1,4},{2,7},{3,6},{4,1},{5,0},{6,3},{7,2},{8,13},{9,12},{10,... | collective-permute-start | bytes 393224 | tf_op jit(solution)/shard_map/ppermute | solution.py:301
  156.3 18.9 %copy-start.10 = (f32[128,4096]{1,0:T(8,128)S(1)}, f32[128,4096]{1,0:T(8,128)}, u32[]{:S(2)}) copy-start(f32[128,4096]{1,0:T(8,128)} %copy-done.9) | copy-start | bytes 6291460
  (23 other events, 173.2 us)

commit v2 on v0

--- a/solution.py
+++ b/solution.py
@@ -1,9 +1,310 @@
+import math
 import jax
 import jax.numpy as jnp
 from jax import lax
+from jax.experimental import pallas as pl
+from jax.experimental.pallas import tpu as pltpu
 from jax.sharding import PartitionSpec as P
 
 ITERS = 2
+LN2 = math.log(2.0)
+F32 = jnp.float32
+BF16 = jnp.bfloat16
+
+
+def params(mib=8):
+    return pltpu.CompilerParams(vmem_limit_bytes=mib * 1024 * 1024)
+
+
+CHEAP = pl.CostEstimate(flops=1, bytes_accessed=1, transcendentals=0)
+SMEM = pl.BlockSpec(memory_space=pltpu.SMEM)
+VMEM = pl.BlockSpec(memory_space=pltpu.VMEM)
+ANY = pl.BlockSpec(memory_space=pl.ANY)
+
+
+def dot(a, b):
+    return jnp.dot(a, b, preferred_element_type=F32)
+
+
+def column(row):
+    n = row.shape[1]
+    return jnp.broadcast_to(row, (n, n)).T[:, :1]
+
+
+def pack(me, gains, ndev, epd):
+    chd, total = gains.shape
+    half = ndev // 2
+
+    def body(me_ref, gains_ref, *refs):
+        outs, kept, sems = refs[:ndev], refs[ndev], refs[ndev + 1]
+        order = [r ^ half for r in range(ndev)]
+
+        def copy(r):
+            cols = pl.ds(pl.multiple_of((me_ref[0] ^ r) * epd, epd), epd)
+            return pltpu.make_async_copy(gains_ref.at[:, cols], kept.at[:, cols], sems.at[r])
+
+        for r in order:
+            copy(r).start()
+        for r in order:
+            copy(r).wait()
+            cols = pl.ds(pl.multiple_of((me_ref[0] ^ r) * epd, epd), epd)
+            outs[r][...] = kept[:, cols].astype(BF16)
+
+    return pl.pallas_call(
+        body,
+        out_shape=[jax.ShapeDtypeStruct((chd, epd), BF16)] * ndev + [pltpu.VMEM((chd, total), F32)],
+        in_specs=[SMEM, ANY],
+        out_specs=[VMEM] * (ndev + 1),
+        scratch_shapes=[pltpu.SemaphoreType.DMA((ndev,))],
+        compiler_params=params(),
+        cost_estimate=CHEAP,
+        name="pack_gains",
+    )(me, gains)
+
+
+def flip(me, data, ndev):
+    epd, chans = data.shape
+    chd = chans // ndev
+
+    def body(me_ref, data_ref, out_ref):
+        for r in range(ndev):
+            cols = pl.ds(pl.multiple_of((me_ref[0] ^ r) * chd, chd), chd)
+            out_ref[pl.ds(r * chd, chd), :] = data_ref[:, cols].astype(F32).T.astype(BF16)
+
+    return pl.pallas_call(
+        body,
+        out_shape=pltpu.VMEM((chans, epd), BF16),
+        in_specs=[SMEM, VMEM],
+        out_specs=VMEM,
+        compiler_params=params(),
+        cost_estimate=CHEAP,
+        name="flip",
+    )(me, data)
+
+
+def dense(me, blocks, order, ndev):
+    nblk, width, _ = blocks.shape
+    chans = nblk * width
+    chd = chans // ndev
+
+    def body(me_ref, blocks_ref, order_ref, out_ref, hot_ref, left_ref):
+        row = lax.broadcasted_iota(jnp.int32, (chans, width), 0)
+        chan = ((row // chd) ^ me_ref[0]) * chd + row % chd
+        for b in range(nblk):
+            hot = jnp.where(chan == order_ref[:, pl.ds(b * width, width)], 1.0, 0.0).astype(BF16)
+            hot_ref[b] = hot
+            left_ref[b] = dot(hot, blocks_ref[b]).astype(BF16)
+        for r in range(ndev):
+            rows = pl.ds(r * chd, chd)
+            total = jnp.zeros((chd, chans), F32)
+            for b in range(nblk):
+                total += lax.dot_general(
+                    left_ref[b, rows, :], hot_ref[b], (((1,), (1,)), ((), ())), preferred_element_type=F32
+                )
+            out_ref[rows, :] = total.astype(BF16)
+
+    return pl.pallas_call(
+        body,
+        out_shape=pltpu.VMEM((chans, chans), BF16),
+        in_specs=[SMEM, VMEM, VMEM],
+        out_specs=VMEM,
+        scratch_shapes=[pltpu.VMEM((nblk, chans, width), BF16)] * 2,
+        compiler_params=params(),
+        cost_estimate=CHEAP,
+        name="dense_blocks",
+    )(me, blocks, order[None, :])
+
+
+def covar(me, squares, scales, offsets, epd):
+    total = squares.shape[1]
+    per = epd // 128
+    first = offsets[0]
+    count = len(offsets) * epd
+
+    def body(me_ref, sq_all, sc_all, out_ref, sq_col, sc_col):
+        lane = lax.broadcasted_iota(jnp.int32, (16, 128), 1)
+        sub = lax.broadcasted_iota(jnp.int32, (16, 128), 0)
+        away = (sub - lane).astype(F32)
+
+        def block(n, _):
+            base = (me_ref[0] ^ (first + n // per)) * epd + (n % per) * 128
+            span = pl.ds(pl.multiple_of(base, 128), 128)
+            sq_col[...] = jnp.broadcast_to(sq_all[:, span], (128, 128)).T
+            sc_col[...] = jnp.broadcast_to(sc_all[:, span], (128, 128)).T
+
+            def group(g, _):
+                part = pl.ds(pl.multiple_of(g * 16, 16), 16)
+                at = pl.ds(pl.multiple_of(n * 128 + g * 16, 16), 16)
+                sq_i = sq_col[part, :]
+                sc_i = sc_col[part, :]
+                start = away + (base + g * 16).astype(F32)
+                for c in range(total // 128):
+                    cols = pl.ds(c * 128, 128)
+                    q = lax.rsqrt(sq_i + sq_all[:, cols])
+                    u = (start - float(c * 128)) * q
+                    out_ref[at, cols] = (q * jnp.exp2((sc_i + sc_all[:, cols]) - u * u)).astype(BF16)
+                return 0
+
+            return lax.fori_loop(0, 8, group, 0)
+
+        lax.fori_loop(0, count // 128, block, 0)
+
+    return pl.pallas_call(
+        body,
+        out_shape=pltpu.VMEM((count, total), BF16),
+        in_specs=[SMEM, VMEM, VMEM],
+        out_specs=VMEM,
+        scratch_shapes=[pltpu.VMEM((128, 128), F32)] * 2,
+        compiler_params=params(),
+        cost_estimate=CHEAP,
+        name="covar_rows",
+    )(me, squares, scales)
+
+
+def normal(weights, pieces, resp, stud):
+    ndev = len(pieces)
+    chd, epd = pieces[0].shape
+    chans = ndev * chd
+    half = ndev // 2
+
+    def body(*refs):
+        w_ref, resp_ref, stud_ref = refs[:3]
+        ins = refs[3 : 3 + ndev]
+        outs = refs[3 + ndev : 3 + 2 * ndev]
+        got = refs[-1]
+        for r in range(ndev):
+            got[pl.ds(r * chd, chd), :] = ins[r][...]
+        for r in [k ^ half for k in range(ndev)]:
+            rows = pl.ds(r * chd, chd)
+            product = dot(w_ref[rows, :], got[...])
+            outs[r][...] = (stud_ref[rows, :].astype(F32) * (product - resp_ref[rows, :].astype(F32))).astype(BF16)
+
+    return pl.pallas_call(
+        body,
+        out_shape=[jax.ShapeDtypeStruct((chd, epd), BF16)] * ndev,
+        in_specs=[VMEM] * (3 + ndev),
+        out_specs=[VMEM] * ndev,
+        scratch_shapes=[pltpu.VMEM((chans, epd), BF16)],
+        compiler_params=params(),
+        cost_estimate=CHEAP,
+        name="normal_step",
+    )(weights, resp, stud, *pieces)
+
+
+def smooth(pieces, rows, before):
+    chd, epd = pieces[0].shape
+    total = rows.shape[1]
+    cnt = len(pieces)
+
+    def body(*refs):
+        ins = refs[:cnt]
+        rows_ref = refs[cnt]
+        out_ref = refs[-1]
+        left = jnp.concatenate([ref[...] for ref in ins], axis=1)
+
+        def tile(n, _):
+            cols = pl.ds(pl.multiple_of(n * epd, epd), epd)
+            acc = dot(left, rows_ref[:, cols])
+            out_ref[:, cols] = acc if before is None else acc + refs[cnt + 1][:, cols]
+            return 0
+
+        lax.fori_loop(0, total // epd, tile, 0)
+
+    more = [] if before is None else [before]
+    return pl.pallas_call(
+        body,
+        out_shape=pltpu.VMEM((chd, total), F32),
+        in_specs=[VMEM] * (cnt + 1 + len(more)),
+        out_specs=VMEM,
+        compiler_params=params(),
+        cost_estimate=CHEAP,
+        name="smooth_part",
+    )(*pieces, rows, *more)
+
+
+def update(me, pieces, rows, before, current, lower, upper, last):
+    chd, epd = pieces[0].shape
+    total = rows.shape[1]
+    cnt = len(pieces)
+    ndev = total // epd
+    half = ndev // 2
+
+    def body(*refs):
+        me_ref = refs[0]
+        ins = refs[1 : 1 + cnt]
+        rows_ref, before_ref, cur_ref, low_ref, high_ref, out_ref = refs[1 + cnt : 7 + cnt]
+        left = jnp.concatenate([ref[...] for ref in ins], axis=1)
+        low, high = column(low_ref[...]), column(high_ref[...])
+        copies = []
+        for r in [k ^ half for k in range(ndev)]:
+            cols = pl.ds(pl.multiple_of((me_ref[0] ^ r) * epd, epd), epd)
+            acc = before_ref[:, cols] + dot(left, rows_ref[:, cols])
+            new = jnp.clip(cur_ref[:, cols] - 0.02 * acc, low, high)
+            if last:
+                stage, sems = refs[-2:]
+                stage[:, cols] = new
+                copies.append(pltpu.make_async_copy(stage.at[:, cols], out_ref.at[:, cols], sems.at[r]))
+                copies[-1].start()
+            else:
+                out_ref[:, cols] = new
+                refs[7 + cnt + r][...] = new.astype(BF16)
+        for copy in copies:
+            copy.wait()
+
+    if last:
+        shapes, specs = [jax.ShapeDtypeStruct((chd, total), F32)], [ANY]
+        scratch = [pltpu.VMEM((chd, total), F32), pltpu.SemaphoreType.DMA((ndev,))]
+    else:
+        shapes = [pltpu.VMEM((chd, total), F32)] + [jax.ShapeDtypeStruct((chd, epd), BF16)] * ndev
+        specs, scratch = [VMEM] * (1 + ndev), []
+    return pl.pallas_call(
+        body,
+        out_shape=shapes,
+        in_specs=[SMEM] + [VMEM] * (cnt + 5),
+        out_specs=specs,
+        scratch_shapes=scratch,
+        compiler_params=params(),
+        cost_estimate=CHEAP,
+        name="update",
+    )(me, *pieces, rows, before, current, lower, upper)
+
+
+def swap(pieces):
+    ndev = len(pieces)
+    half = ndev // 2
+    got = [pieces[0]] + [None] * (ndev - 1)
+    for r in list(range(half, ndev)) + list(range(1, half)):
+        got[r] = lax.ppermute(pieces[r], "wide", [(i, i ^ r) for i in range(ndev)])
+    return got
+
+
+def fast(gains, response, student, blocks, order, lower, upper, lengths, amplitude):
+    ndev = lax.axis_size("wide")
+    chd, epochs = gains.shape
+    epd = epochs // ndev
+    half = ndev // 2
+    me = lax.axis_index("wide").astype(jnp.int32).reshape(1)
+    low, high = lower[None, :], upper[None, :]
+
+    *packed, current = pack(me, gains, ndev, epd)
+    got = swap(packed)
+    weights = dense(me, blocks, order, ndev)
+    resp = flip(me, response, ndev)
+    stud = flip(me, student, ndev)
+    squares = (lengths * lengths * LN2)[None, :]
+    scales = jnp.log2(amplitude * jnp.sqrt(lengths * math.sqrt(2.0 * LN2)))[None, :]
+    groups = [list(range(half)), list(range(half, half + half // 2)), list(range(half + half // 2, ndev))]
+    rows = [covar(me, squares, scales, group, epd) for group in groups]
+    got, rows = lax.optimization_barrier((got, rows))
+    for step in range(ITERS):
+        misfit = swap(normal(weights, got, resp, stud))
+        total = smooth([misfit[r] for r in groups[0]], rows[0], None)
+        total = smooth([misfit[r] for r in groups[1]], rows[1], total)
+        last = step == ITERS - 1
+        current, *packed = update(me, [misfit[r] for r in groups[2]], rows[2], total, current, low, high, last)
+        if not last:
+            got = swap(packed)
+    return current
 
 
 def covar_stack(lengths, amplitude, span):
@@ -25,7 +326,7 @@
             * jnp.sqrt(2.0 * left * right / denom)
             * jnp.exp(-diff * diff / denom)
         )
-        return vals.astype(jnp.bfloat16)
+        return vals.astype(BF16)
 
     return lax.map(one_block, jnp.arange(count, dtype=jnp.int32))
 
@@ -34,14 +335,12 @@
     rows, chans = packed.shape
     nblk, width = (blocks.shape[0], blocks.shape[1])
     moved = jnp.take(packed, order, axis=1).reshape(rows, nblk, width)
-    product = jnp.einsum("rbi,bij->rbj", moved, blocks, preferred_element_type=jnp.float32).reshape(
-        rows, chans
-    )
-    permuted = stud_perm.astype(jnp.float32) * (product - resp_perm.astype(jnp.float32))
-    return jnp.take(permuted, inverse, axis=1).astype(jnp.bfloat16)
-
-
-def per_device(gains, response, student, blocks, order, lower, upper, lengths, amplitude):
+    product = jnp.einsum("rbi,bij->rbj", moved, blocks, preferred_element_type=F32).reshape(rows, chans)
+    permuted = stud_perm.astype(F32) * (product - resp_perm.astype(F32))
+    return jnp.take(permuted, inverse, axis=1).astype(BF16)
+
+
+def general(gains, response, student, blocks, order, lower, upper, lengths, amplitude):
     nwide = lax.axis_size("wide")
     chd, epochs = gains.shape
     epd = epochs // nwide
@@ -53,7 +352,7 @@
     kernel_stack = covar_stack(lengths, amplitude, span)
     current = gains
     for step in range(ITERS):
-        packed = current.astype(jnp.bfloat16).reshape(chd, nwide, epd)
+        packed = current.astype(BF16).reshape(chd, nwide, epd)
         got = (
             lax.all_to_all(packed, "wide", split_axis=1, concat_axis=0, tiled=True)
             .reshape(chans, epd)
@@ -63,11 +362,18 @@
         misfit = lax.all_to_all(
             misfit_rows.T.reshape(chans, 1, epd), "wide", split_axis=0, concat_axis=1, tiled=True
         ).reshape(chd, epochs)
-        smoothed = jnp.einsum(
-            "ce,bes->cbs", misfit, kernel_stack, preferred_element_type=jnp.float32
-        ).reshape(chd, epochs)
+        smoothed = jnp.einsum("ce,bes->cbs", misfit, kernel_stack, preferred_element_type=F32).reshape(
+            chd, epochs
+        )
         current = jnp.clip(current - 0.02 * smoothed, lower[:, None], upper[:, None])
     return current
+
+
+def per_device(*args):
+    ndev = lax.axis_size("wide")
+    chd, epochs = args[0].shape
+    fits = ndev >= 4 and ndev & (ndev - 1) == 0 and chd % 128 == 0 and (epochs // ndev) % 256 == 0
+    return (fast if fits else general)(*args)
 
 
 def solution(mesh):

time: 354 us -> 140 us (0.40)
  local copies, waits for them, and re-layouts: 141 us -> 2.47 us
  other arithmetic: 86.7 us -> 0.02 us
  blocking collectives: 59.2 us -> 0 us
  Pallas kernels: 0 us -> 55.3 us
  starting transfers between devices: 11.5 us -> 50 us
  matrix products: 35.7 us -> 0 us
  waiting for transfers between devices: 7.01 us -> 31.4 us
  loops' own time: 10.7 us -> 0 us
    convert_element_type x17 -> x0, other arithmetic: 75.8 us -> none  [the longest x16 74 us: one_block(): return vals.astype(jnp.bfloat16)]
    dynamic_update_slice x32 -> x0, local copies, waits for them, and re-layouts: 70.1 us -> none  [covar_stack(): return lax.map(one_block, jnp.arange(count, dtype=jnp.int32))]
    all_to_all x2 -> x0, blocking collectives: 59.2 us -> none  [the longest x1 30.6 us: per_device(): lax.all_to_all(packed, 'wide', split_axis=1, concat_axis=0, tiled=True)]
    pallas_call x0 -> x15, Pallas kernels: none -> 55.3 us  [the longest x3 28.6 us: covar(): pl.pallas_call(body, out_shape=pltpu.VMEM((count, total), BF16), in_specs...]
    ppermute x0 -> x28, starting transfers between devices: none -> 50 us  [swap(): got[r] = lax.ppermute(pieces[r], 'wide', [(i, i ^ r) for i in range(ndev)])]
    dot_general x4 -> x0, matrix products: 35.7 us -> none  [the longest x2 34.7 us: per_device(): jnp.einsum('ce,bes->cbs', misfit, kernel_stack, preferred_element_type=jn...]
    ppermute x0 -> x28, waiting for transfers between devices: none -> 31.4 us  [swap(): got[r] = lax.ppermute(pieces[r], 'wide', [(i, i ^ r) for i in range(ndev)])]
    gather x6 -> x0, local copies, waits for them, and re-layouts: 27.4 us -> none  [the longest x2 7.93 us: data_rows(): return jnp.take(permuted, inverse, axis=1).astype(jnp.bfloat16)]
  transfers between devices with their start and end apart: 2 -> 28, of which waited for: 1 -> 9; matrix products, arithmetic and copies ran while one was open for 50% -> 0% of each run, Pallas kernels for 0% -> 34%
where the time goes in v2:
time: 140 us; the launch traced here: 139 us
  Pallas kernels  55.3 us (40%)
  starting transfers between devices  50 us (36%)
  waiting for transfers between devices  31.4 us (22%)
  local copies, waits for them, and re-layouts  2.47 us (2%)
    ppermute x28, starting transfers between devices, swap(): got[r] = lax.ppermute(pieces[r], 'wide', [(i, i ^ r) for i in range(ndev)])  50 us
    ppermute x28, waiting for transfers between devices, swap(): got[r] = lax.ppermute(pieces[r], 'wide', [(i, i ^ r) for i in range(ndev)])  31.4 us
    pallas_call x3, Pallas kernels, covar(): pl.pallas_call(body, out_shape=pltpu.VMEM((count, total), BF16), in_specs...  28.6 us
    pallas_call x4, Pallas kernels, smooth(): pl.pallas_call(body, out_shape=pltpu.VMEM((chd, total), F32), in_specs=[V...  12.5 us
    pallas_call x1, Pallas kernels, dense(): pl.pallas_call(body, out_shape=pltpu.VMEM((chans, chans), BF16), in_specs...  6.05 us
    pallas_call x2, Pallas kernels, update(): pl.pallas_call(body, out_shape=shapes, in_specs=[SMEM] + [VMEM] * (cnt +...  3.99 us
    pallas_call x2, Pallas kernels, normal(): pl.pallas_call(body, out_shape=[jax.ShapeDtypeStruct((chd, epd), BF16)] *...  2.98 us
  transfers between devices with their start and end apart: 28, of which 9 were waited for; matrix products, arithmetic and copies ran while one was open for 0% of the time, Pallas kernels for 34%

profile of v2, /device:TPU:0, one launch (start us, length us, event | category | flops | bytes accessed | tf_op | source)
XLA Modules:
  0.0 139.5 jit_solution(14423144518983283233)
XLA Ops:
  0.0 1.6 %copy-done = f32[128,4096]{1,0:T(8,128)S(1)} copy-done((f32[128,4096]{1,0:T(8,128)S(1)}, f32[128,4096]{1,0:T(8,128)}, u32[]{:S(2)}) %copy-start) | copy-done | bytes 2097176
  2.0 3.0 %collective-permute-start = (bf16[128,512]{1,0:T(8,128)(2,1)S(1)}, bf16[128,512]{1,0:T(8,128)(2,1)S(1)}, u32[]{:S(2)}, u32[]{:S(2)}) collective-permute-start(bf16[128,512]{1,0:T(8,128)(2,1)S(1)} %get-tuple-element.51), channel_id=1, source_target_pairs={{0,1},{1,0},{2,3},{3,2},{4,5},{5,4},{6,7},{7,6},{8,9},{9,8},{10,11... | collective-permute-start | bytes 393224 | tf_op jit(solution)/shard_map/ppermute | solution.py:277
  5.1 1.6 %collective-permute-start.1 = (bf16[128,512]{1,0:T(8,128)(2,1)S(1)}, bf16[128,512]{1,0:T(8,128)(2,1)S(1)}, u32[]{:S(2)}, u32[]{:S(2)}) collective-permute-start(bf16[128,512]{1,0:T(8,128)(2,1)S(1)} %get-tuple-element.52), channel_id=1, source_target_pairs={{0,2},{1,3},{2,0},{3,1},{4,6},{5,7},{6,4},{7,5},{8,10},{9,11},{10,... | collective-permute-start | bytes 393224 | tf_op jit(solution)/shard_map/ppermute | solution.py:277
  6.6 3.0 %collective-permute-start.3 = (bf16[128,512]{1,0:T(8,128)(2,1)S(1)}, bf16[128,512]{1,0:T(8,128)(2,1)S(1)}, u32[]{:S(2)}, u32[]{:S(2)}) collective-permute-start(bf16[128,512]{1,0:T(8,128)(2,1)S(1)} %get-tuple-element.54), channel_id=1, source_target_pairs={{0,4},{1,5},{2,6},{3,7},{4,0},{5,1},{6,2},{7,3},{8,12},{9,13},{10,... | collective-permute-start | bytes 393224 | tf_op jit(solution)/shard_map/ppermute | solution.py:277
  10.9 3.6 %collective-permute-start.5 = (bf16[128,512]{1,0:T(8,128)(2,1)S(1)}, bf16[128,512]{1,0:T(8,128)(2,1)S(1)}, u32[]{:S(2)}, u32[]{:S(2)}) collective-permute-start(bf16[128,512]{1,0:T(8,128)(2,1)S(1)} %get-tuple-element.56), channel_id=1, source_target_pairs={{0,6},{1,7},{2,4},{3,5},{4,2},{5,3},{6,0},{7,1},{8,14},{9,15},{10,... | collective-permute-start | bytes 393224 | tf_op jit(solution)/shard_map/ppermute | solution.py:277
  16.5 7.2 %covar_rows.5.refs_3_ = bf16[1024,4096]{1,0:T(8,128)(2,1)S(1)} custom-call(s32[1]{0:T(128)} %bitcast.me_ref.refs_0_, f32[1,4096]{1,0:T(1,128)S(1)} %bitcast.9, f32[1,4096]{1,0:T(1,128)S(1)} %bitcast.6), custom_call_target="tpu_custom_call" | custom-call | flops 1 | bytes 1 | tf_op jit(solution)/shard_map/covar_rows/pallas_call | solution.py:152
  23.6 7.2 %covar_rows.4.refs_2_ = bf16[1024,4096]{1,0:T(8,128)(2,1)S(1)} custom-call(s32[1]{0:T(128)} %bitcast.me_ref.refs_0_, f32[1,4096]{1,0:T(1,128)S(1)} %bitcast.10, f32[1,4096]{1,0:T(1,128)S(1)} %bitcast.7), custom_call_target="tpu_custom_call" | custom-call | flops 1 | bytes 1 | tf_op jit(solution)/shard_map/covar_rows/pallas_call | solution.py:152
  30.8 14.3 %covar_rows.3.refs_4_ = bf16[2048,4096]{1,0:T(8,128)(2,1)S(1)} custom-call(s32[1]{0:T(128)} %bitcast.me_ref.refs_0_, f32[1,4096]{1,0:T(1,128)S(1)} %bitcast.11, f32[1,4096]{1,0:T(1,128)S(1)} %bitcast.8), custom_call_target="tpu_custom_call" | custom-call | flops 1 | bytes 1 | tf_op jit(solution)/shard_map/covar_rows/pallas_call | solution.py:152
  46.7 6.0 %dense_blocks.1.refs_0_ = bf16[1024,1024]{1,0:T(8,128)(2,1)S(1)} custom-call(s32[1]{0:T(128)} %bitcast.me_ref.refs_0_, bf16[4,256,256]{2,1,0:T(8,128)(2,1)S(1)} %copy-done.3, s32[1,1024]{1,0:T(1,128)S(1)} %bitcast.12), custom_call_target="tpu_custom_call" | custom-call | flops 1 | bytes 1 | tf_op jit(solution)/shard_map/dense_blocks/pallas_call | solution.py:106
  54.4 3.2 %collective-permute-start.11 = (bf16[128,512]{1,0:T(8,128)(2,1)S(1)}, bf16[128,512]{1,0:T(8,128)(2,1)S(1)}, u32[]{:S(2)}, u32[]{:S(2)}) collective-permute-start(bf16[128,512]{1,0:T(8,128)(2,1)S(1)} %get-tuple-element.73), channel_id=1, source_target_pairs={{0,1},{1,0},{2,3},{3,2},{4,5},{5,4},{6,7},{7,6},{8,9},{9,8},{10,11... | collective-permute-start | bytes 393224 | tf_op jit(solution)/shard_map/ppermute | solution.py:277
  59.6 3.8 %collective-permute-start.10 = (bf16[128,512]{1,0:T(8,128)(2,1)S(1)}, bf16[128,512]{1,0:T(8,128)(2,1)S(1)}, u32[]{:S(2)}, u32[]{:S(2)}) collective-permute-start(bf16[128,512]{1,0:T(8,128)(2,1)S(1)} %get-tuple-element.70), channel_id=1, source_target_pairs={{0,5},{1,4},{2,7},{3,6},{4,1},{5,0},{6,3},{7,2},{8,13},{9,12},{10,... | collective-permute-start | bytes 393224 | tf_op jit(solution)/shard_map/ppermute | solution.py:277
  64.9 2.0 %collective-permute-start.8 = (bf16[128,512]{1,0:T(8,128)(2,1)S(1)}, bf16[128,512]{1,0:T(8,128)(2,1)S(1)}, u32[]{:S(2)}, u32[]{:S(2)}) collective-permute-start(bf16[128,512]{1,0:T(8,128)(2,1)S(1)} %get-tuple-element.67), channel_id=1, source_target_pairs={{0,7},{1,6},{2,5},{3,4},{4,3},{5,2},{6,1},{7,0},{8,15},{9,14},{10,... | collective-permute-start | bytes 393224 | tf_op jit(solution)/shard_map/ppermute | solution.py:277
  66.9 3.7 %smooth_part.4.refs_3_ = f32[128,4096]{1,0:T(8,128)S(1)} custom-call(bf16[128,512]{1,0:T(8,128)(2,1)S(1)} %get-tuple-element.72.refs_0_, bf16[128,512]{1,0:T(8,128)(2,1)S(1)} %collective-permute-done.11.refs_1_, bf16[128,512]{1,0:T(8,128)(2,1)S(1)} %collective-permute-done.12.refs_2_, bf16[128,512]{1,0:T(8,128)(2,1)S(1)} %collective-permute-done.13.refs_3_, ...), custom_call_target="tpu_custom_call" | custom-call | flops 1 | bytes 1 | tf_op jit(solution)/shard_map/smooth_part/pallas_call | solution.py:214
  70.6 4.3 %collective-permute-done.9.refs_0_ = bf16[128,512]{1,0:T(8,128)(2,1)S(1)} collective-permute-done((bf16[128,512]{1,0:T(8,128)(2,1)S(1)}, bf16[128,512]{1,0:T(8,128)(2,1)S(1)}, u32[]{:S(2)}, u32[]{:S(2)}) %collective-permute-start.9) | collective-permute-done | bytes 131104 | tf_op jit(solution)/shard_map/ppermute | solution.py:277
  74.9 3.1 %collective-permute-done.10.refs_1_ = bf16[128,512]{1,0:T(8,128)(2,1)S(1)} collective-permute-done((bf16[128,512]{1,0:T(8,128)(2,1)S(1)}, bf16[128,512]{1,0:T(8,128)(2,1)S(1)}, u32[]{:S(2)}, u32[]{:S(2)}) %collective-permute-start.10) | collective-permute-done | bytes 131104 | tf_op jit(solution)/shard_map/ppermute | solution.py:277
  78.0 2.6 %smooth_part.5.refs_4_ = f32[128,4096]{1,0:T(8,128)S(1)} custom-call(bf16[128,512]{1,0:T(8,128)(2,1)S(1)} %collective-permute-done.9.refs_0_, bf16[128,512]{1,0:T(8,128)(2,1)S(1)} %collective-permute-done.10.refs_1_, bf16[1024,4096]{1,0:T(8,128)(2,1)S(1)} %covar_rows.4.refs_2_, f32[128,4096]{1,0:T(8,128)S(1)} %smooth_part.4.refs_3_), custom_call_target="tpu_custom_call" | custom-call | flops 1 | bytes 1 | tf_op jit(solution)/shard_map/smooth_part/pallas_call | solution.py:214
  83.7 2.0 %collective-permute-start.16 = (bf16[128,512]{1,0:T(8,128)(2,1)S(1)}, bf16[128,512]{1,0:T(8,128)(2,1)S(1)}, u32[]{:S(2)}, u32[]{:S(2)}) collective-permute-start(bf16[128,512]{1,0:T(8,128)(2,1)S(1)} %get-tuple-element.81), channel_id=1, source_target_pairs={{0,3},{1,2},{2,1},{3,0},{4,7},{5,6},{6,5},{7,4},{8,11},{9,10},{10,... | collective-permute-start | bytes 393224 | tf_op jit(solution)/shard_map/ppermute | solution.py:277
  85.8 1.9 %collective-permute-start.17 = (bf16[128,512]{1,0:T(8,128)(2,1)S(1)}, bf16[128,512]{1,0:T(8,128)(2,1)S(1)}, u32[]{:S(2)}, u32[]{:S(2)}) collective-permute-start(bf16[128,512]{1,0:T(8,128)(2,1)S(1)} %get-tuple-element.82), channel_id=1, source_target_pairs={{0,4},{1,5},{2,6},{3,7},{4,0},{5,1},{6,2},{7,3},{8,12},{9,13},{10,... | collective-permute-start | bytes 393224 | tf_op jit(solution)/shard_map/ppermute | solution.py:277
  88.8 1.6 %collective-permute-start.19 = (bf16[128,512]{1,0:T(8,128)(2,1)S(1)}, bf16[128,512]{1,0:T(8,128)(2,1)S(1)}, u32[]{:S(2)}, u32[]{:S(2)}) collective-permute-start(bf16[128,512]{1,0:T(8,128)(2,1)S(1)} %get-tuple-element.84), channel_id=1, source_target_pairs={{0,6},{1,7},{2,4},{3,5},{4,2},{5,3},{6,0},{7,1},{8,14},{9,15},{10,... | collective-permute-start | bytes 393224 | tf_op jit(solution)/shard_map/ppermute | solution.py:277
  90.4 3.0 %collective-permute-start.20 = (bf16[128,512]{1,0:T(8,128)(2,1)S(1)}, bf16[128,512]{1,0:T(8,128)(2,1)S(1)}, u32[]{:S(2)}, u32[]{:S(2)}) collective-permute-start(bf16[128,512]{1,0:T(8,128)(2,1)S(1)} %get-tuple-element.85), channel_id=1, source_target_pairs={{0,7},{1,6},{2,5},{3,4},{4,3},{5,2},{6,1},{7,0},{8,15},{9,14},{10,... | collective-permute-start | bytes 393224 | tf_op jit(solution)/shard_map/ppermute | solution.py:277
  93.4 9.1 %collective-permute-done.17.refs_7_ = bf16[128,512]{1,0:T(8,128)(2,1)S(1)} collective-permute-done((bf16[128,512]{1,0:T(8,128)(2,1)S(1)}, bf16[128,512]{1,0:T(8,128)(2,1)S(1)}, u32[]{:S(2)}, u32[]{:S(2)}) %collective-permute-start.17) | collective-permute-done | bytes 131104 | tf_op jit(solution)/shard_map/ppermute | solution.py:277
  102.6 3.5 %collective-permute-done.18.refs_8_ = bf16[128,512]{1,0:T(8,128)(2,1)S(1)} collective-permute-done((bf16[128,512]{1,0:T(8,128)(2,1)S(1)}, bf16[128,512]{1,0:T(8,128)(2,1)S(1)}, u32[]{:S(2)}, u32[]{:S(2)}) %collective-permute-start.18) | collective-permute-done | bytes 131104 | tf_op jit(solution)/shard_map/ppermute | solution.py:277
  108.4 3.6 %collective-permute-start.26 = (bf16[128,512]{1,0:T(8,128)(2,1)S(1)}, bf16[128,512]{1,0:T(8,128)(2,1)S(1)}, u32[]{:S(2)}, u32[]{:S(2)}) collective-permute-start(bf16[128,512]{1,0:T(8,128)(2,1)S(1)} %get-tuple-element.92), channel_id=1, source_target_pairs={{0,2},{1,3},{2,0},{3,1},{4,6},{5,7},{6,4},{7,5},{8,10},{9,11},{10,... | collective-permute-start | bytes 393224 | tf_op jit(solution)/shard_map/ppermute | solution.py:277
  112.0 2.3 %collective-permute-start.21 = (bf16[128,512]{1,0:T(8,128)(2,1)S(1)}, bf16[128,512]{1,0:T(8,128)(2,1)S(1)}, u32[]{:S(2)}, u32[]{:S(2)}) collective-permute-start(bf16[128,512]{1,0:T(8,128)(2,1)S(1)} %get-tuple-element.86), channel_id=1, source_target_pairs={{0,6},{1,7},{2,4},{3,5},{4,2},{5,3},{6,0},{7,1},{8,14},{9,15},{10,... | collective-permute-start | bytes 393224 | tf_op jit(solution)/shard_map/ppermute | solution.py:277
  114.3 3.3 %collective-permute-start.23 = (bf16[128,512]{1,0:T(8,128)(2,1)S(1)}, bf16[128,512]{1,0:T(8,128)(2,1)S(1)}, u32[]{:S(2)}, u32[]{:S(2)}) collective-permute-start(bf16[128,512]{1,0:T(8,128)(2,1)S(1)} %get-tuple-element.88), channel_id=1, source_target_pairs={{0,4},{1,5},{2,6},{3,7},{4,0},{5,1},{6,2},{7,3},{8,12},{9,13},{10,... | collective-permute-start | bytes 393224 | tf_op jit(solution)/shard_map/ppermute | solution.py:277
  119.2 2.1 %collective-permute-start.22 = (bf16[128,512]{1,0:T(8,128)(2,1)S(1)}, bf16[128,512]{1,0:T(8,128)(2,1)S(1)}, u32[]{:S(2)}, u32[]{:S(2)}) collective-permute-start(bf16[128,512]{1,0:T(8,128)(2,1)S(1)} %get-tuple-element.87), channel_id=1, source_target_pairs={{0,7},{1,6},{2,5},{3,4},{4,3},{5,2},{6,1},{7,0},{8,15},{9,14},{10,... | collective-permute-start | bytes 393224 | tf_op jit(solution)/shard_map/ppermute | solution.py:277
  121.4 2.8 %collective-permute-done.27.refs_3_ = bf16[128,512]{1,0:T(8,128)(2,1)S(1)} collective-permute-done((bf16[128,512]{1,0:T(8,128)(2,1)S(1)}, bf16[128,512]{1,0:T(8,128)(2,1)S(1)}, u32[]{:S(2)}, u32[]{:S(2)}) %collective-permute-start.27) | collective-permute-done | bytes 131104 | tf_op jit(solution)/shard_map/ppermute | solution.py:277
  124.2 3.7 %smooth_part.6.refs_3_ = f32[128,4096]{1,0:T(8,128)S(1)} custom-call(bf16[128,512]{1,0:T(8,128)(2,1)S(1)} %get-tuple-element.90.refs_0_, bf16[128,512]{1,0:T(8,128)(2,1)S(1)} %collective-permute-done.25.refs_1_, bf16[128,512]{1,0:T(8,128)(2,1)S(1)} %collective-permute-done.26.refs_2_, bf16[128,512]{1,0:T(8,128)(2,1)S(1)} %collective-permute-done.27.refs_3_, ...), custom_call_target="tpu_custom_call" | custom-call | flops 1 | bytes 1 | tf_op jit(solution)/shard_map/smooth_part/pallas_call | solution.py:214
  127.9 2.8 %collective-permute-done.23.refs_0_ = bf16[128,512]{1,0:T(8,128)(2,1)S(1)} collective-permute-done((bf16[128,512]{1,0:T(8,128)(2,1)S(1)}, bf16[128,512]{1,0:T(8,128)(2,1)S(1)}, u32[]{:S(2)}, u32[]{:S(2)}) %collective-permute-start.23) | collective-permute-done | bytes 131104 | tf_op jit(solution)/shard_map/ppermute | solution.py:277
  130.7 3.8 %collective-permute-done.24.refs_1_ = bf16[128,512]{1,0:T(8,128)(2,1)S(1)} collective-permute-done((bf16[128,512]{1,0:T(8,128)(2,1)S(1)}, bf16[128,512]{1,0:T(8,128)(2,1)S(1)}, u32[]{:S(2)}, u32[]{:S(2)}) %collective-permute-start.24) | collective-permute-done | bytes 131104 | tf_op jit(solution)/shard_map/ppermute | solution.py:277
  134.5 2.6 %smooth_part.7.refs_4_ = f32[128,4096]{1,0:T(8,128)S(1)} custom-call(bf16[128,512]{1,0:T(8,128)(2,1)S(1)} %collective-permute-done.23.refs_0_, bf16[128,512]{1,0:T(8,128)(2,1)S(1)} %collective-permute-done.24.refs_1_, bf16[1024,4096]{1,0:T(8,128)(2,1)S(1)} %covar_rows.4.refs_2_, f32[128,4096]{1,0:T(8,128)S(1)} %smooth_part.6.refs_3_), custom_call_target="tpu_custom_call" | custom-call | flops 1 | bytes 1 | tf_op jit(solution)/shard_map/smooth_part/pallas_call | solution.py:214
  137.0 2.4 %update.3 = f32[128,4096]{1,0:T(8,128)} custom-call(s32[1]{0:T(128)} %bitcast.me_ref.refs_0_, bf16[128,512]{1,0:T(8,128)(2,1)S(1)} %collective-permute-done.21.refs_1_, bf16[128,512]{1,0:T(8,128)(2,1)S(1)} %collective-permute-done.22.refs_2_, bf16[1024,4096]{1,0:T(8,128)(2,1)S(1)} %covar_rows.5.refs_3_, f32[128,4096]{1,0:T(8,128)S(1)} %smooth_part.7.refs_4_, ...), custom_call_target="tpu_custom_call" | custom-call | flops 1 | bytes 1 | tf_op jit(solution)/shard_map/update/pallas_call | solution.py:260
  (58 shorter events, 18.5 us)
Async XLA Ops:
  1.6 14.9 %copy-start.7 = (f32[4096]{0:T(1024)S(1)}, f32[4096]{0:T(1024)}, u32[]{:S(2)}) copy-start(f32[4096]{0:T(1024)} %param.17) | copy-start | bytes 49156
  1.6 14.9 %copy-start.8 = (f32[4096]{0:T(1024)S(1)}, f32[4096]{0:T(1024)}, u32[]{:S(2)}) copy-start(f32[4096]{0:T(1024)} %param.16) | copy-start | bytes 49156
  2.0 8.9 %collective-permute-start = (bf16[128,512]{1,0:T(8,128)(2,1)S(1)}, bf16[128,512]{1,0:T(8,128)(2,1)S(1)}, u32[]{:S(2)}, u32[]{:S(2)}) collective-permute-start(bf16[128,512]{1,0:T(8,128)(2,1)S(1)} %get-tuple-element.51), channel_id=1, source_target_pairs={{0,1},{1,0},{2,3},{3,2},{4,5},{5,4},{6,7},{7,6},{8,9},{9,8},{10,11... | collective-permute-start | bytes 393224 | tf_op jit(solution)/shard_map/ppermute | solution.py:277
  5.1 10.7 %collective-permute-start.1 = (bf16[128,512]{1,0:T(8,128)(2,1)S(1)}, bf16[128,512]{1,0:T(8,128)(2,1)S(1)}, u32[]{:S(2)}, u32[]{:S(2)}) collective-permute-start(bf16[128,512]{1,0:T(8,128)(2,1)S(1)} %get-tuple-element.52), channel_id=1, source_target_pairs={{0,2},{1,3},{2,0},{3,1},{4,6},{5,7},{6,4},{7,5},{8,10},{9,11},{10,... | collective-permute-start | bytes 393224 | tf_op jit(solution)/shard_map/ppermute | solution.py:277
  6.6 46.2 %collective-permute-start.2 = (bf16[128,512]{1,0:T(8,128)(2,1)S(1)}, bf16[128,512]{1,0:T(8,128)(2,1)S(1)}, u32[]{:S(2)}, u32[]{:S(2)}) collective-permute-start(bf16[128,512]{1,0:T(8,128)(2,1)S(1)} %get-tuple-element.53), channel_id=1, source_target_pairs={{0,3},{1,2},{2,1},{3,0},{4,7},{5,6},{6,5},{7,4},{8,11},{9,10},{10,... | collective-permute-start | bytes 393224 | tf_op jit(solution)/shard_map/ppermute | solution.py:277
  6.6 46.2 %collective-permute-start.3 = (bf16[128,512]{1,0:T(8,128)(2,1)S(1)}, bf16[128,512]{1,0:T(8,128)(2,1)S(1)}, u32[]{:S(2)}, u32[]{:S(2)}) collective-permute-start(bf16[128,512]{1,0:T(8,128)(2,1)S(1)} %get-tuple-element.54), channel_id=1, source_target_pairs={{0,4},{1,5},{2,6},{3,7},{4,0},{5,1},{6,2},{7,3},{8,12},{9,13},{10,... | collective-permute-start | bytes 393224 | tf_op jit(solution)/shard_map/ppermute | solution.py:277
  9.6 43.2 %collective-permute-start.4 = (bf16[128,512]{1,0:T(8,128)(2,1)S(1)}, bf16[128,512]{1,0:T(8,128)(2,1)S(1)}, u32[]{:S(2)}, u32[]{:S(2)}) collective-permute-start(bf16[128,512]{1,0:T(8,128)(2,1)S(1)} %get-tuple-element.55), channel_id=1, source_target_pairs={{0,5},{1,4},{2,7},{3,6},{4,1},{5,0},{6,3},{7,2},{8,13},{9,12},{10,... | collective-permute-start | bytes 393224 | tf_op jit(solution)/shard_map/ppermute | solution.py:277
  10.9 41.9 %collective-permute-start.5 = (bf16[128,512]{1,0:T(8,128)(2,1)S(1)}, bf16[128,512]{1,0:T(8,128)(2,1)S(1)}, u32[]{:S(2)}, u32[]{:S(2)}) collective-permute-start(bf16[128,512]{1,0:T(8,128)(2,1)S(1)} %get-tuple-element.56), channel_id=1, source_target_pairs={{0,6},{1,7},{2,4},{3,5},{4,2},{5,3},{6,0},{7,1},{8,14},{9,15},{10,... | collective-permute-start | bytes 393224 | tf_op jit(solution)/shard_map/ppermute | solution.py:277
  15.8 37.1 %collective-permute-start.6 = (bf16[128,512]{1,0:T(8,128)(2,1)S(1)}, bf16[128,512]{1,0:T(8,128)(2,1)S(1)}, u32[]{:S(2)}, u32[]{:S(2)}) collective-permute-start(bf16[128,512]{1,0:T(8,128)(2,1)S(1)} %get-tuple-element.57), channel_id=1, source_target_pairs={{0,7},{1,6},{2,5},{3,4},{4,3},{5,2},{6,1},{7,0},{8,15},{9,14},{10,... | collective-permute-start | bytes 393224 | tf_op jit(solution)/shard_map/ppermute | solution.py:277
  30.8 14.3 %copy-start.1 = (bf16[512,1024]{1,0:T(8,128)(2,1)S(1)}, bf16[512,1024]{1,0:T(8,128)(2,1)}, u32[]{:S(2)}) copy-start(bf16[512,1024]{1,0:T(8,128)(2,1)} %data_ref.2) | copy-start | bytes 3145732
  54.4 9.1 %collective-permute-start.11 = (bf16[128,512]{1,0:T(8,128)(2,1)S(1)}, bf16[128,512]{1,0:T(8,128)(2,1)S(1)}, u32[]{:S(2)}, u32[]{:S(2)}) collective-permute-start(bf16[128,512]{1,0:T(8,128)(2,1)S(1)} %get-tuple-element.73), channel_id=1, source_target_pairs={{0,1},{1,0},{2,3},{3,2},{4,5},{5,4},{6,7},{7,6},{8,9},{9,8},{10,11... | collective-permute-start | bytes 393224 | tf_op jit(solution)/shard_map/ppermute | solution.py:277
  57.6 7.3 %collective-permute-start.12 = (bf16[128,512]{1,0:T(8,128)(2,1)S(1)}, bf16[128,512]{1,0:T(8,128)(2,1)S(1)}, u32[]{:S(2)}, u32[]{:S(2)}) collective-permute-start(bf16[128,512]{1,0:T(8,128)(2,1)S(1)} %get-tuple-element.74), channel_id=1, source_target_pairs={{0,2},{1,3},{2,0},{3,1},{4,6},{5,7},{6,4},{7,5},{8,10},{9,11},{10,... | collective-permute-start | bytes 393224 | tf_op jit(solution)/shard_map/ppermute | solution.py:277
  57.6 9.3 %collective-permute-start.13 = (bf16[128,512]{1,0:T(8,128)(2,1)S(1)}, bf16[128,512]{1,0:T(8,128)(2,1)S(1)}, u32[]{:S(2)}, u32[]{:S(2)}) collective-permute-start(bf16[128,512]{1,0:T(8,128)(2,1)S(1)} %get-tuple-element.75), channel_id=1, source_target_pairs={{0,3},{1,2},{2,1},{3,0},{4,7},{5,6},{6,5},{7,4},{8,11},{9,10},{10,... | collective-permute-start | bytes 393224 | tf_op jit(solution)/shard_map/ppermute | solution.py:277
  59.1 15.8 %collective-permute-start.9 = (bf16[128,512]{1,0:T(8,128)(2,1)S(1)}, bf16[128,512]{1,0:T(8,128)(2,1)S(1)}, u32[]{:S(2)}, u32[]{:S(2)}) collective-permute-start(bf16[128,512]{1,0:T(8,128)(2,1)S(1)} %get-tuple-element.69), channel_id=1, source_target_pairs={{0,4},{1,5},{2,6},{3,7},{4,0},{5,1},{6,2},{7,3},{8,12},{9,13},{10,... | collective-permute-start | bytes 393224 | tf_op jit(solution)/shard_map/ppermute | solution.py:277
  59.6 18.4 %collective-permute-start.10 = (bf16[128,512]{1,0:T(8,128)(2,1)S(1)}, bf16[128,512]{1,0:T(8,128)(2,1)S(1)}, u32[]{:S(2)}, u32[]{:S(2)}) collective-permute-start(bf16[128,512]{1,0:T(8,128)(2,1)S(1)} %get-tuple-element.70), channel_id=1, source_target_pairs={{0,5},{1,4},{2,7},{3,6},{4,1},{5,0},{6,3},{7,2},{8,13},{9,12},{10,... | collective-permute-start | bytes 393224 | tf_op jit(solution)/shard_map/ppermute | solution.py:277
  63.4 17.2 %collective-permute-start.7 = (bf16[128,512]{1,0:T(8,128)(2,1)S(1)}, bf16[128,512]{1,0:T(8,128)(2,1)S(1)}, u32[]{:S(2)}, u32[]{:S(2)}) collective-permute-start(bf16[128,512]{1,0:T(8,128)(2,1)S(1)} %get-tuple-element.66), channel_id=1, source_target_pairs={{0,6},{1,7},{2,4},{3,5},{4,2},{5,3},{6,0},{7,1},{8,14},{9,15},{10,... | collective-permute-start | bytes 393224 | tf_op jit(solution)/shard_map/ppermute | solution.py:277
  64.9 15.7 %collective-permute-start.8 = (bf16[128,512]{1,0:T(8,128)(2,1)S(1)}, bf16[128,512]{1,0:T(8,128)(2,1)S(1)}, u32[]{:S(2)}, u32[]{:S(2)}) collective-permute-start(bf16[128,512]{1,0:T(8,128)(2,1)S(1)} %get-tuple-element.67), channel_id=1, source_target_pairs={{0,7},{1,6},{2,5},{3,4},{4,3},{5,2},{6,1},{7,0},{8,15},{9,14},{10,... | collective-permute-start | bytes 393224 | tf_op jit(solution)/shard_map/ppermute | solution.py:277
  70.6 10.0 %copy-start.5 = (f32[128]{0:T(128)S(1)}, f32[128]{0:T(128)}, u32[]{:S(2)}) copy-start(f32[128]{0:T(128)} %param.14) | copy-start | bytes 1540
  82.2 6.7 %collective-permute-start.14 = (bf16[128,512]{1,0:T(8,128)(2,1)S(1)}, bf16[128,512]{1,0:T(8,128)(2,1)S(1)}, u32[]{:S(2)}, u32[]{:S(2)}) collective-permute-start(bf16[128,512]{1,0:T(8,128)(2,1)S(1)} %get-tuple-element.79), channel_id=1, source_target_pairs={{0,1},{1,0},{2,3},{3,2},{4,5},{5,4},{6,7},{7,6},{8,9},{9,8},{10,11... | collective-permute-start | bytes 393224 | tf_op jit(solution)/shard_map/ppermute | solution.py:277
  83.0 7.5 %collective-permute-start.15 = (bf16[128,512]{1,0:T(8,128)(2,1)S(1)}, bf16[128,512]{1,0:T(8,128)(2,1)S(1)}, u32[]{:S(2)}, u32[]{:S(2)}) collective-permute-start(bf16[128,512]{1,0:T(8,128)(2,1)S(1)} %get-tuple-element.80), channel_id=1, source_target_pairs={{0,2},{1,3},{2,0},{3,1},{4,6},{5,7},{6,4},{7,5},{8,10},{9,11},{10,... | collective-permute-start | bytes 393224 | tf_op jit(solution)/shard_map/ppermute | solution.py:277
  83.7 9.7 %collective-permute-start.16 = (bf16[128,512]{1,0:T(8,128)(2,1)S(1)}, bf16[128,512]{1,0:T(8,128)(2,1)S(1)}, u32[]{:S(2)}, u32[]{:S(2)}) collective-permute-start(bf16[128,512]{1,0:T(8,128)(2,1)S(1)} %get-tuple-element.81), channel_id=1, source_target_pairs={{0,3},{1,2},{2,1},{3,0},{4,7},{5,6},{6,5},{7,4},{8,11},{9,10},{10,... | collective-permute-start | bytes 393224 | tf_op jit(solution)/shard_map/ppermute | solution.py:277
  85.8 16.8 %collective-permute-start.17 = (bf16[128,512]{1,0:T(8,128)(2,1)S(1)}, bf16[128,512]{1,0:T(8,128)(2,1)S(1)}, u32[]{:S(2)}, u32[]{:S(2)}) collective-permute-start(bf16[128,512]{1,0:T(8,128)(2,1)S(1)} %get-tuple-element.82), channel_id=1, source_target_pairs={{0,4},{1,5},{2,6},{3,7},{4,0},{5,1},{6,2},{7,3},{8,12},{9,13},{10,... | collective-permute-start | bytes 393224 | tf_op jit(solution)/shard_map/ppermute | solution.py:277
  87.7 18.4 %collective-permute-start.18 = (bf16[128,512]{1,0:T(8,128)(2,1)S(1)}, bf16[128,512]{1,0:T(8,128)(2,1)S(1)}, u32[]{:S(2)}, u32[]{:S(2)}) collective-permute-start(bf16[128,512]{1,0:T(8,128)(2,1)S(1)} %get-tuple-element.83), channel_id=1, source_target_pairs={{0,5},{1,4},{2,7},{3,6},{4,1},{5,0},{6,3},{7,2},{8,13},{9,12},{10,... | collective-permute-start | bytes 393224 | tf_op jit(solution)/shard_map/ppermute | solution.py:277
  88.8 17.2 %collective-permute-start.19 = (bf16[128,512]{1,0:T(8,128)(2,1)S(1)}, bf16[128,512]{1,0:T(8,128)(2,1)S(1)}, u32[]{:S(2)}, u32[]{:S(2)}) collective-permute-start(bf16[128,512]{1,0:T(8,128)(2,1)S(1)} %get-tuple-element.84), channel_id=1, source_target_pairs={{0,6},{1,7},{2,4},{3,5},{4,2},{5,3},{6,0},{7,1},{8,14},{9,15},{10,... | collective-permute-start | bytes 393224 | tf_op jit(solution)/shard_map/ppermute | solution.py:277
  90.4 15.6 %collective-permute-start.20 = (bf16[128,512]{1,0:T(8,128)(2,1)S(1)}, bf16[128,512]{1,0:T(8,128)(2,1)S(1)}, u32[]{:S(2)}, u32[]{:S(2)}) collective-permute-start(bf16[128,512]{1,0:T(8,128)(2,1)S(1)} %get-tuple-element.85), channel_id=1, source_target_pairs={{0,7},{1,6},{2,5},{3,4},{4,3},{5,2},{6,1},{7,0},{8,15},{9,14},{10,... | collective-permute-start | bytes 393224 | tf_op jit(solution)/shard_map/ppermute | solution.py:277
  107.6 10.0 %collective-permute-start.25 = (bf16[128,512]{1,0:T(8,128)(2,1)S(1)}, bf16[128,512]{1,0:T(8,128)(2,1)S(1)}, u32[]{:S(2)}, u32[]{:S(2)}) collective-permute-start(bf16[128,512]{1,0:T(8,128)(2,1)S(1)} %get-tuple-element.91), channel_id=1, source_target_pairs={{0,1},{1,0},{2,3},{3,2},{4,5},{5,4},{6,7},{7,6},{8,9},{9,8},{10,11... | collective-permute-start | bytes 393224 | tf_op jit(solution)/shard_map/ppermute | solution.py:277
  108.4 10.9 %collective-permute-start.26 = (bf16[128,512]{1,0:T(8,128)(2,1)S(1)}, bf16[128,512]{1,0:T(8,128)(2,1)S(1)}, u32[]{:S(2)}, u32[]{:S(2)}) collective-permute-start(bf16[128,512]{1,0:T(8,128)(2,1)S(1)} %get-tuple-element.92), channel_id=1, source_target_pairs={{0,2},{1,3},{2,0},{3,1},{4,6},{5,7},{6,4},{7,5},{8,10},{9,11},{10,... | collective-permute-start | bytes 393224 | tf_op jit(solution)/shard_map/ppermute | solution.py:277
  112.0 25.1 %collective-permute-start.21 = (bf16[128,512]{1,0:T(8,128)(2,1)S(1)}, bf16[128,512]{1,0:T(8,128)(2,1)S(1)}, u32[]{:S(2)}, u32[]{:S(2)}) collective-permute-start(bf16[128,512]{1,0:T(8,128)(2,1)S(1)} %get-tuple-element.86), channel_id=1, source_target_pairs={{0,6},{1,7},{2,4},{3,5},{4,2},{5,3},{6,0},{7,1},{8,14},{9,15},{10,... | collective-permute-start | bytes 393224 | tf_op jit(solution)/shard_map/ppermute | solution.py:277
  114.3 9.9 %collective-permute-start.27 = (bf16[128,512]{1,0:T(8,128)(2,1)S(1)}, bf16[128,512]{1,0:T(8,128)(2,1)S(1)}, u32[]{:S(2)}, u32[]{:S(2)}) collective-permute-start(bf16[128,512]{1,0:T(8,128)(2,1)S(1)} %get-tuple-element.93), channel_id=1, source_target_pairs={{0,3},{1,2},{2,1},{3,0},{4,7},{5,6},{6,5},{7,4},{8,11},{9,10},{10,... | collective-permute-start | bytes 393224 | tf_op jit(solution)/shard_map/ppermute | solution.py:277
  114.3 16.4 %collective-permute-start.23 = (bf16[128,512]{1,0:T(8,128)(2,1)S(1)}, bf16[128,512]{1,0:T(8,128)(2,1)S(1)}, u32[]{:S(2)}, u32[]{:S(2)}) collective-permute-start(bf16[128,512]{1,0:T(8,128)(2,1)S(1)} %get-tuple-element.88), channel_id=1, source_target_pairs={{0,4},{1,5},{2,6},{3,7},{4,0},{5,1},{6,2},{7,3},{8,12},{9,13},{10,... | collective-permute-start | bytes 393224 | tf_op jit(solution)/shard_map/ppermute | solution.py:277
  117.6 16.9 %collective-permute-start.24 = (bf16[128,512]{1,0:T(8,128)(2,1)S(1)}, bf16[128,512]{1,0:T(8,128)(2,1)S(1)}, u32[]{:S(2)}, u32[]{:S(2)}) collective-permute-start(bf16[128,512]{1,0:T(8,128)(2,1)S(1)} %get-tuple-element.89), channel_id=1, source_target_pairs={{0,5},{1,4},{2,7},{3,6},{4,1},{5,0},{6,3},{7,2},{8,13},{9,12},{10,... | collective-permute-start | bytes 393224 | tf_op jit(solution)/shard_map/ppermute | solution.py:277
  119.2 17.8 %collective-permute-start.22 = (bf16[128,512]{1,0:T(8,128)(2,1)S(1)}, bf16[128,512]{1,0:T(8,128)(2,1)S(1)}, u32[]{:S(2)}, u32[]{:S(2)}) collective-permute-start(bf16[128,512]{1,0:T(8,128)(2,1)S(1)} %get-tuple-element.87), channel_id=1, source_target_pairs={{0,7},{1,6},{2,5},{3,4},{4,3},{5,2},{6,1},{7,0},{8,15},{9,14},{10,... | collective-permute-start | bytes 393224 | tf_op jit(solution)/shard_map/ppermute | solution.py:277
  (5 other events, 16.0 us)

commit v3 on v2

v3 whole, which is shorter than its diff:
```python
import math
import jax
import jax.numpy as jnp
from jax import lax
from jax.experimental import pallas as pl
from jax.experimental.pallas import tpu as pltpu
from jax.sharding import PartitionSpec as P

ITERS = 2
LN2 = math.log(2.0)
F32 = jnp.float32
BF16 = jnp.bfloat16


def params(mib=8):
    return pltpu.CompilerParams(vmem_limit_bytes=mib * 1024 * 1024)


CHEAP = pl.CostEstimate(flops=1, bytes_accessed=1, transcendentals=0)
SMEM = pl.BlockSpec(memory_space=pltpu.SMEM)
VMEM = pl.BlockSpec(memory_space=pltpu.VMEM)
HBM = pl.BlockSpec(memory_space=pltpu.HBM)


def dot(a, b):
    return jnp.dot(a, b, preferred_element_type=F32)


def column(row):
    n = row.shape[1]
    return jnp.broadcast_to(row, (n, n)).T[:, :1]


def send_order(ndev):
    half = ndev // 2
    return [half, *range(1, half), *range(half + 1, ndev), 0]


def pack(me, gains, ndev, epd):
    chd, total = gains.shape
    order = send_order(ndev)

    def body(me_ref, gains_ref, *refs):
        outs, kept, sems = refs[:ndev], refs[ndev], refs[ndev + 1]

        def copy(r):
            theirs = pl.ds(pl.multiple_of((me_ref[0] ^ r) * epd, epd), epd)
            return pltpu.make_async_copy(gains_ref.at[:, theirs], kept.at[:, pl.ds(r * epd, epd)], sems.at[r])

        for r in order:
            copy(r).start()
        for r in order:
            copy(r).wait()
            outs[r][...] = kept[:, pl.ds(r * epd, epd)].astype(BF16)

    return pl.pallas_call(
        body,
        out_shape=[jax.ShapeDtypeStruct((chd, epd), BF16)] * ndev + [pltpu.VMEM((chd, total), F32)],
        in_specs=[SMEM, HBM],
        out_specs=[VMEM] * (ndev + 1),
        scratch_shapes=[pltpu.SemaphoreType.DMA((ndev,))],
        compiler_params=params(),
        cost_estimate=CHEAP,
        name="pack_gains",
    )(me, gains)


def flip(me, data, ndev):
    epd, chans = data.shape
    chd = chans // ndev

    def body(me_ref, data_ref, out_ref):
        for r in range(ndev):
            cols = pl.ds(pl.multiple_of((me_ref[0] ^ r) * chd, chd), chd)
            out_ref[pl.ds(r * chd, chd), :] = data_ref[:, cols].astype(F32).T.astype(BF16)

    return pl.pallas_call(
        body,
        out_shape=pltpu.VMEM((chans, epd), BF16),
        in_specs=[SMEM, VMEM],
        out_specs=VMEM,
        compiler_params=params(),
        cost_estimate=CHEAP,
        name="flip",
    )(me, data)


def dense(me, blocks, order, ndev):
    nblk, width, _ = blocks.shape
    chans = nblk * width
    chd = chans // ndev

    def body(me_ref, blocks_ref, order_ref, out_ref, left_ref, hot_ref):
        def channels(dim, shape):
            at = lax.broadcasted_iota(jnp.int32, shape, dim)
            return (((at // chd) ^ me_ref[0]) * chd + at % chd).astype(F32)

        down = channels(0, (chans, width))
        along = channels(1, (width, chans))
        for b in range(nblk):
            span = pl.ds(b * width, width)
            names = order_ref[:, span].astype(F32)
            hot = jnp.where(down == names, 1.0, 0.0).astype(BF16)
            left_ref[:, span] = dot(hot, blocks_ref[b]).astype(BF16)
            hot_ref[span, :] = jnp.where(along == column(names), 1.0, 0.0).astype(BF16)
        for r in range(0, ndev, 2):
            rows = pl.ds(r * chd, 2 * chd)
            out_ref[rows, :] = dot(left_ref[rows, :], hot_ref[...]).astype(BF16)

    return pl.pallas_call(
        body,
        out_shape=pltpu.VMEM((chans, chans), BF16),
        in_specs=[SMEM, VMEM, VMEM],
        out_specs=VMEM,
        scratch_shapes=[pltpu.VMEM((chans, chans), BF16)] * 2,
        compiler_params=params(),
        cost_estimate=CHEAP,
        name="dense_blocks",
    )(me, blocks, order[None, :])


def covar_tiles(me_ref, sq_all, sc_all, sq_col, sc_col, offset, k, others, epd, store):
    group = 32
    lane = lax.broadcasted_iota(jnp.int32, (group, 128), 1)
    sub = lax.broadcasted_iota(jnp.int32, (group, 128), 0)
    away = (sub - lane).astype(F32)
    base = (me_ref[0] ^ offset) * epd + k * 128
    span = pl.ds(pl.multiple_of(base, 128), 128)
    sq_col[...] = jnp.broadcast_to(sq_all[:, span], (128, 128)).T
    sc_col[...] = jnp.broadcast_to(sc_all[:, span], (128, 128)).T
    for r in others:
        first = (me_ref[0] ^ r) * epd
        apart = (base - first).astype(F32)
        for c in range(0, epd, 128):
            cols = pl.ds(pl.multiple_of(first + c, 128), 128)
            sq_j, sc_j = sq_all[:, cols], sc_all[:, cols]
            parts = []
            for g in range(0, 128, group):
                rows = pl.ds(g, group)
                q = lax.rsqrt(sq_col[rows, :] + sq_j)
                u = (away + (apart + float(g - c))) * q
                parts.append((q * jnp.exp2((sc_col[rows, :] + sc_j) - u * u)).astype(BF16))
            store(r, c, jnp.concatenate(parts, axis=0))


def covar_own(me, squares, scales, offsets, epd):
    per = epd // 128
    first = offsets[0]
    count = len(offsets) * epd

    def body(me_ref, sq_all, sc_all, out_ref, sq_col, sc_col):
        for n, offset in enumerate(offsets):

            def block(k, _):
                mine = pl.ds(pl.multiple_of(n * epd + k * 128, 128), 128)

                def store(r, c, tile):
                    theirs = pl.ds((r - first) * epd + c, 128)
                    out_ref[mine, theirs] = tile
                    if r != offset:
                        out_ref[theirs, mine] = tile.T

                covar_tiles(me_ref, sq_all, sc_all, sq_col, sc_col, offset, k, offsets[n:], epd, store)
                return 0

            lax.fori_loop(0, per, block, 0)

    return pl.pallas_call(
        body,
        out_shape=pltpu.VMEM((count, count), BF16),
        in_specs=[SMEM, VMEM, VMEM],
        out_specs=VMEM,
        scratch_shapes=[pltpu.VMEM((128, 128), F32)] * 2,
        compiler_params=params(),
        cost_estimate=CHEAP,
        name="covar_own",
    )(me, squares, scales)


def covar_cross(me, squares, scales, near, far, epd):
    per = epd // 128
    shape = (len(near) * epd, len(far) * epd)

    def body(me_ref, sq_all, sc_all, out_ref, flip_ref, sq_col, sc_col):
        def block(n, _):
            mine = pl.ds(pl.multiple_of(n * 128, 128), 128)

            def store(r, c, tile):
                theirs = pl.ds((r - far[0]) * epd + c, 128)
                out_ref[mine, theirs] = tile
                flip_ref[theirs, mine] = tile.T

            covar_tiles(me_ref, sq_all, sc_all, sq_col, sc_col, near[0] + n // per, n % per, far, epd, store)
            return 0

        lax.fori_loop(0, shape[0] // 128, block, 0)

    return pl.pallas_call(
        body,
        out_shape=[pltpu.VMEM(shape, BF16), pltpu.VMEM(shape[::-1], BF16)],
        in_specs=[SMEM, VMEM, VMEM],
        out_specs=[VMEM] * 2,
        scratch_shapes=[pltpu.VMEM((128, 128), F32)] * 2,
        compiler_params=params(),
        cost_estimate=CHEAP,
        name="covar_cross",
    )(me, squares, scales)


def normal(weights, pieces, resp, stud):
    ndev = len(pieces)
    chd, epd = pieces[0].shape
    chans = ndev * chd

    def body(w_ref, resp_ref, stud_ref, *refs):
        ins, outs, got = refs[:ndev], refs[ndev:-1], refs[-1]
        for r in range(ndev):
            got[pl.ds(r * chd, chd), :] = ins[r][...]
        for r in send_order(ndev):
            rows = pl.ds(r * chd, chd)
            product = dot(w_ref[rows, :], got[...])
            outs[r][...] = (stud_ref[rows, :].astype(F32) * (product - resp_ref[rows, :].astype(F32))).astype(BF16)

    return pl.pallas_call(
        body,
        out_shape=[jax.ShapeDtypeStruct((chd, epd), BF16)] * ndev,
        in_specs=[VMEM] * (3 + ndev),
        out_specs=[VMEM] * ndev,
        scratch_shapes=[pltpu.VMEM((chans, epd), BF16)],
        compiler_params=params(),
        cost_estimate=CHEAP,
        name="normal_step",
    )(weights, resp, stud, *pieces)


def partial(groups, before):
    chd, epd = groups[0][0][0].shape
    span = groups[0][1][0].shape[1]
    blocks = len(groups[0][1])
    args = [array for pieces, rows, _ in groups for array in [*pieces, *rows]]
    more = [] if before is None else [before]

    def body(*refs):
        out_ref, given = refs[-1], iter(refs)
        terms = []
        for pieces, rows, at in groups:
            left = jnp.concatenate([next(given)[...] for _ in pieces], axis=1)
            terms.append((left, [next(given) for _ in rows], pl.ds(at, len(pieces) * epd)))
        for b in range(blocks):
            for c in range(0, span, epd):
                cols = pl.ds(b * span + c, epd)
                acc = None if before is None else refs[len(args)][:, cols]
                for left, rows_refs, at in terms:
                    term = dot(left, rows_refs[b][at, pl.ds(c, epd)])
                    acc = term if acc is None else acc + term
                out_ref[:, cols] = acc

    return pl.pallas_call(
        body,
        out_shape=pltpu.VMEM((chd, blocks * span), F32),
        in_specs=[VMEM] * (len(args) + len(more)),
        out_specs=VMEM,
        compiler_params=params(),
        cost_estimate=CHEAP,
        name="smooth_part",
    )(*args, *more)


def update(me, pieces, rows, at, before, current, lower, upper, last):
    chd, epd = pieces[0].shape
    cnt, blocks = len(pieces), len(rows)
    span = rows[0].shape[1]
    total = blocks * span
    ndev = total // epd

    def body(*refs):
        me_ref, ins, rows_refs = refs[0], refs[1 : 1 + cnt], refs[1 + cnt : 1 + cnt + blocks]
        before_ref, cur_ref, low_ref, high_ref, out_ref = refs[1 + cnt + blocks : 6 + cnt + blocks]
        left = jnp.concatenate([ref[...] for ref in ins], axis=1)
        low, high = column(low_ref[...]), column(high_ref[...])
        copies = []
        for r in send_order(ndev):
            cols = pl.ds(r * epd, epd)
            block, c = divmod(r * epd, span)
            acc = before_ref[:, cols] + dot(left, rows_refs[block][pl.ds(at, cnt * epd), pl.ds(c, epd)])
            new = jnp.clip(cur_ref[:, cols] - 0.02 * acc, low, high)
            if last:
                stage, sems = refs[-2:]
                stage[:, cols] = new
                theirs = pl.ds(pl.multiple_of((me_ref[0] ^ r) * epd, epd), epd)
                copies.append(pltpu.make_async_copy(stage.at[:, cols], out_ref.at[:, theirs], sems.at[r]))
                copies[-1].start()
            else:
                out_ref[:, cols] = new
                refs[6 + cnt + blocks + r][...] = new.astype(BF16)
        for copy in copies:
            copy.wait()

    if last:
        shapes, specs = [jax.ShapeDtypeStruct((chd, total), F32)], [HBM]
        scratch = [pltpu.VMEM((chd, total), F32), pltpu.SemaphoreType.DMA((ndev,))]
    else:
        shapes = [pltpu.VMEM((chd, total), F32)] + [jax.ShapeDtypeStruct((chd, epd), BF16)] * ndev
        specs, scratch = [VMEM] * (1 + ndev), []
    return pl.pallas_call(
        body,
        out_shape=shapes,
        in_specs=[SMEM] + [VMEM] * (cnt + blocks + 4),
        out_specs=specs,
        scratch_shapes=scratch,
        compiler_params=params(),
        cost_estimate=CHEAP,
        name="update",
    )(me, *pieces, *rows, before, current, lower, upper)


def swap(pieces):
    ndev = len(pieces)
    got = list(pieces)
    for r in send_order(ndev)[:-1]:
        got[r] = lax.ppermute(pieces[r], "wide", [(i, i ^ r) for i in range(ndev)])
    return got


def fast(gains, response, student, blocks, order, lower, upper, lengths, amplitude):
    ndev = lax.axis_size("wide")
    epd = gains.shape[1] // ndev
    half = ndev // 2
    near, far = list(range(half)), list(range(half, ndev))
    me = lax.axis_index("wide").astype(jnp.int32).reshape(1)
    low, high = lower[None, :], upper[None, :]

    *packed, current = pack(me, gains, ndev, epd)
    got = swap(packed)
    weights = dense(me, blocks, order, ndev)
    resp = flip(me, response, ndev)
    stud = flip(me, student, ndev)
    squares = (lengths * lengths * LN2)[None, :]
    scales = jnp.log2(amplitude * jnp.sqrt(lengths * math.sqrt(2.0 * LN2)))[None, :]
    near_far, far_near = covar_cross(me, squares, scales, near, far, epd)
    near_near = covar_own(me, squares, scales, near, epd)
    got, near_far, far_near, near_near = lax.optimization_barrier((got, near_far, far_near, near_near))
    far_far = covar_own(me, squares, scales, far, epd)
    near_rows, far_rows = [near_near, near_far], [far_near, far_far]
    late = 1
    for step in range(ITERS):
        misfit = swap(normal(weights, got, resp, stud))
        total = partial([(misfit[:1], near_rows, 0), (misfit[half : half + 1], far_rows, 0)], None)
        total = partial([(misfit[1:half], near_rows, epd)], total)
        total = partial([(misfit[half + 1 : ndev - late], far_rows, epd)], total)
        last = step == ITERS - 1
        current, *packed = update(
            me, misfit[ndev - late :], far_rows, (half - late) * epd, total, current, low, high, last
        )
        if not last:
            got = swap(packed)
    return current


def covar_stack(lengths, amplitude, span):
    total = lengths.shape[0]
    count = total // span
    rows = jnp.arange(total, dtype=jnp.int32)

    def one_block(index):
        start = index * span
        cols = start + jnp.arange(span, dtype=jnp.int32)
        diff = (rows[:, None] - cols[None, :]).astype(lengths.dtype)
        left = lengths[:, None]
        right = lax.dynamic_slice_in_dim(lengths, start, span, 0)[None, :]
        amp_right = lax.dynamic_slice_in_dim(amplitude, start, span, 0)[None, :]
        denom = left * left + right * right
        vals = (
            amplitude[:, None]
            * amp_right
            * jnp.sqrt(2.0 * left * right / denom)
            * jnp.exp(-diff * diff / denom)
        )
        return vals.astype(BF16)

    return lax.map(one_block, jnp.arange(count, dtype=jnp.int32))


def data_rows(packed, resp_perm, stud_perm, blocks, order, inverse):
    rows, chans = packed.shape
    nblk, width = (blocks.shape[0], blocks.shape[1])
    moved = jnp.take(packed, order, axis=1).reshape(rows, nblk, width)
    product = jnp.einsum("rbi,bij->rbj", moved, blocks, preferred_element_type=F32).reshape(rows, chans)
    permuted = stud_perm.astype(F32) * (product - resp_perm.astype(F32))
    return jnp.take(permuted, inverse, axis=1).astype(BF16)


def general(gains, response, student, blocks, order, lower, upper, lengths, amplitude):
    nwide = lax.axis_size("wide")
    chd, epochs = gains.shape
    epd = epochs // nwide
    chans = chd * nwide
    inverse = jnp.zeros((chans,), jnp.int32).at[order].set(jnp.arange(chans, dtype=jnp.int32))
    resp_perm = jnp.take(response, order, axis=1)
    stud_perm = jnp.take(student, order, axis=1)
    span = min(256, epochs)
    kernel_stack = covar_stack(lengths, amplitude, span)
    current = gains
    for step in range(ITERS):
        packed = current.astype(BF16).reshape(chd, nwide, epd)
        got = (
            lax.all_to_all(packed, "wide", split_axis=1, concat_axis=0, tiled=True)
            .reshape(chans, epd)
            .T
        )
        misfit_rows = data_rows(got, resp_perm, stud_perm, blocks, order, inverse)
        misfit = lax.all_to_all(
            misfit_rows.T.reshape(chans, 1, epd), "wide", split_axis=0, concat_axis=1, tiled=True
        ).reshape(chd, epochs)
        smoothed = jnp.einsum("ce,bes->cbs", misfit, kernel_stack, preferred_element_type=F32).reshape(
            chd, epochs
        )
        current = jnp.clip(current - 0.02 * smoothed, lower[:, None], upper[:, None])
    return current


def per_device(*args):
    ndev = lax.axis_size("wide")
    chd, epochs = args[0].shape
    fits = ndev >= 4 and ndev & (ndev - 1) == 0 and chd % 128 == 0 and (epochs // ndev) % 256 == 0
    return (fast if fits else general)(*args)


def solution(mesh):
    placed = (
        P(("half", "wide"), None),
        P("wide", "half"),
        P("wide", "half"),
        P("half", None, None),
        P("half"),
        P(("half", "wide")),
        P(("half", "wide")),
        P(),
        P(),
    )
    return jax.shard_map(
        per_device, mesh=mesh, in_specs=placed, out_specs=P(("half", "wide"), None), check_vma=False
    )
```

time: 140 us -> 114 us (0.81)
  Pallas kernels: 55.3 us -> 39.7 us
  waiting for transfers between devices: 31.4 us -> 20 us
    ppermute x28, waiting for transfers between devices: 31.4 us -> 20 us  [swap(): got[r] = lax.ppermute(pieces[r], 'wide', [(i, i ^ r) for i in range(ndev)])]
    pallas_call x7 -> x9, Pallas kernels: 41.1 us -> 29.9 us  [the longest x2 12.2 us: covar_own(): pl.pallas_call(body, out_shape=pltpu.VMEM((count, count), BF16), in_specs...]
    pallas_call x1, Pallas kernels: 6.05 us -> 2.95 us  [dense(): pl.pallas_call(body, out_shape=pltpu.VMEM((chans, chans), BF16), in_specs...]
  transfers between devices with their start and end apart: 28 -> 28, of which waited for: 9 -> 7; matrix products, arithmetic and copies ran while one was open for 0% -> 0% of each run, Pallas kernels for 34% -> 30%
where the time goes in v3:
time: 114 us; the launch traced here: 112 us
  starting transfers between devices  50 us (44%)
  Pallas kernels  39.7 us (35%)
  waiting for transfers between devices  20 us (18%)
  local copies, waits for them, and re-layouts  1.95 us (2%)
    ppermute x28, starting transfers between devices, swap(): got[r] = lax.ppermute(pieces[r], 'wide', [(i, i ^ r) for i in range(ndev)])  50 us
    ppermute x28, waiting for transfers between devices, swap(): got[r] = lax.ppermute(pieces[r], 'wide', [(i, i ^ r) for i in range(ndev)])  20 us
    pallas_call x2, Pallas kernels, covar_own(): pl.pallas_call(body, out_shape=pltpu.VMEM((count, count), BF16), in_specs...  12.2 us
    pallas_call x6, Pallas kernels, partial(): pl.pallas_call(body, out_shape=pltpu.VMEM((chd, blocks * span), F32), in_...  9.07 us
    pallas_call x1, Pallas kernels, covar_cross(): pl.pallas_call(body, out_shape=[pltpu.VMEM(shape, BF16), pltpu.VMEM(shape...  8.67 us
    pallas_call x2, Pallas kernels, normal(): pl.pallas_call(body, out_shape=[jax.ShapeDtypeStruct((chd, epd), BF16)] *...  2.98 us
    pallas_call x1, Pallas kernels, dense(): pl.pallas_call(body, out_shape=pltpu.VMEM((chans, chans), BF16), in_specs...  2.95 us
    pallas_call x2, Pallas kernels, update(): pl.pallas_call(body, out_shape=shapes, in_specs=[SMEM] + [VMEM] * (cnt +...  2.77 us
  transfers between devices with their start and end apart: 28, of which 7 were waited for; matrix products, arithmetic and copies ran while one was open for 0% of the time, Pallas kernels for 30%

profile of v3, /device:TPU:0, one launch (start us, length us, event | category | flops | bytes accessed | tf_op | source)
XLA Modules:
  0.0 112.3 jit_solution(17223681398819210730)
XLA Ops:
  0.0 1.6 %copy-done.1 = f32[128,4096]{1,0:T(8,128)S(1)} copy-done((f32[128,4096]{1,0:T(8,128)S(1)}, f32[128,4096]{1,0:T(8,128)}, u32[]{:S(2)}) %copy-start.1) | copy-done | bytes 2097176
  2.0 3.0 %collective-permute-start = (bf16[128,512]{1,0:T(8,128)(2,1)S(1)}, bf16[128,512]{1,0:T(8,128)(2,1)S(1)}, u32[]{:S(2)}, u32[]{:S(2)}) collective-permute-start(bf16[128,512]{1,0:T(8,128)(2,1)S(1)} %get-tuple-element.53), channel_id=1, source_target_pairs={{0,1},{1,0},{2,3},{3,2},{4,5},{5,4},{6,7},{7,6},{8,9},{9,8},{10,11... | collective-permute-start | bytes 393224 | tf_op jit(solution)/shard_map/ppermute | solution.py:321
  5.0 1.6 %collective-permute-start.1 = (bf16[128,512]{1,0:T(8,128)(2,1)S(1)}, bf16[128,512]{1,0:T(8,128)(2,1)S(1)}, u32[]{:S(2)}, u32[]{:S(2)}) collective-permute-start(bf16[128,512]{1,0:T(8,128)(2,1)S(1)} %get-tuple-element.54), channel_id=1, source_target_pairs={{0,2},{1,3},{2,0},{3,1},{4,6},{5,7},{6,4},{7,5},{8,10},{9,11},{10,... | collective-permute-start | bytes 393224 | tf_op jit(solution)/shard_map/ppermute | solution.py:321
  6.6 3.0 %collective-permute-start.3 = (bf16[128,512]{1,0:T(8,128)(2,1)S(1)}, bf16[128,512]{1,0:T(8,128)(2,1)S(1)}, u32[]{:S(2)}, u32[]{:S(2)}) collective-permute-start(bf16[128,512]{1,0:T(8,128)(2,1)S(1)} %get-tuple-element.56), channel_id=1, source_target_pairs={{0,4},{1,5},{2,6},{3,7},{4,0},{5,1},{6,2},{7,3},{8,12},{9,13},{10,... | collective-permute-start | bytes 393224 | tf_op jit(solution)/shard_map/ppermute | solution.py:321
  10.9 3.6 %collective-permute-start.5 = (bf16[128,512]{1,0:T(8,128)(2,1)S(1)}, bf16[128,512]{1,0:T(8,128)(2,1)S(1)}, u32[]{:S(2)}, u32[]{:S(2)}) collective-permute-start(bf16[128,512]{1,0:T(8,128)(2,1)S(1)} %get-tuple-element.58), channel_id=1, source_target_pairs={{0,6},{1,7},{2,4},{3,5},{4,2},{5,3},{6,0},{7,1},{8,14},{9,15},{10,... | collective-permute-start | bytes 393224 | tf_op jit(solution)/shard_map/ppermute | solution.py:321
  16.4 6.0 %covar_own.2.refs_1_.refs_3_ = bf16[2048,2048]{1,0:T(8,128)(2,1)S(1)} custom-call(s32[1]{0:T(128)} %bitcast.me_ref.refs_0_, f32[1,4096]{1,0:T(1,128)S(1)} %bitcast.11, f32[1,4096]{1,0:T(1,128)S(1)} %bitcast.8), custom_call_target="tpu_custom_call" | custom-call | flops 1 | bytes 1 | tf_op jit(solution)/shard_map/covar_own/pallas_call | solution.py:168
  22.5 8.7 %covar_cross.1 = (bf16[2048,2048]{1,0:T(8,128)(2,1)S(1)}, bf16[2048,2048]{1,0:T(8,128)(2,1)S(1)}) custom-call(s32[1]{0:T(128)} %bitcast.me_ref.refs_0_, f32[1,4096]{1,0:T(1,128)S(1)} %bitcast.12, f32[1,4096]{1,0:T(1,128)S(1)} %bitcast.9), custom_call_target="tpu_custom_call" | custom-call | flops 1 | bytes 1 | tf_op jit(solution)/shard_map/covar_cross/pallas_call | solution.py:198
  32.2 2.9 %dense_blocks.1.w_ref = bf16[1024,1024]{1,0:T(8,128)(2,1)S(1)} custom-call(s32[1]{0:T(128)} %bitcast.me_ref.refs_0_, bf16[4,256,256]{2,1,0:T(8,128)(2,1)S(1)} %copy-done.4, s32[1,1024]{1,0:T(1,128)S(1)} %bitcast.14), custom_call_target="tpu_custom_call" | custom-call | flops 1 | bytes 1 | tf_op jit(solution)/shard_map/dense_blocks/pallas_call | solution.py:110
  35.2 1.5 %normal_step.2 = (bf16[128,512]{1,0:T(8,128)(2,1)S(1)}, bf16[128,512]{1,0:T(8,128)(2,1)S(1)}, bf16[128,512]{1,0:T(8,128)(2,1)S(1)}, bf16[128,512]{1,0:T(8,128)(2...) custom-call(bf16[1024,1024]{1,0:T(8,128)(2,1)S(1)} %dense_blocks.1.w, ...), custom_call_target="tpu_custom_call" | custom-call | flops 1 | bytes 1 | tf_op jit(solution)/shard_map/normal_step/pallas_call | solution.py:224
  36.7 3.2 %collective-permute-start.10 = (bf16[128,512]{1,0:T(8,128)(2,1)S(1)}, bf16[128,512]{1,0:T(8,128)(2,1)S(1)}, u32[]{:S(2)}, u32[]{:S(2)}) collective-permute-start(bf16[128,512]{1,0:T(8,128)(2,1)S(1)} %get-tuple-element.74), channel_id=1, source_target_pairs={{0,1},{1,0},{2,3},{3,2},{4,5},{5,4},{6,7},{7,6},{8,9},{9,8},{10,11... | collective-permute-start | bytes 393224 | tf_op jit(solution)/shard_map/ppermute | solution.py:321
  40.0 2.4 %collective-permute-start.8 = (bf16[128,512]{1,0:T(8,128)(2,1)S(1)}, bf16[128,512]{1,0:T(8,128)(2,1)S(1)}, u32[]{:S(2)}, u32[]{:S(2)}) collective-permute-start(bf16[128,512]{1,0:T(8,128)(2,1)S(1)} %get-tuple-element.72), channel_id=1, source_target_pairs={{0,5},{1,4},{2,7},{3,6},{4,1},{5,0},{6,3},{7,2},{8,13},{9,12},{10,... | collective-permute-start | bytes 393224 | tf_op jit(solution)/shard_map/ppermute | solution.py:321
  42.4 3.4 %collective-permute-start.12 = (bf16[128,512]{1,0:T(8,128)(2,1)S(1)}, bf16[128,512]{1,0:T(8,128)(2,1)S(1)}, u32[]{:S(2)}, u32[]{:S(2)}) collective-permute-start(bf16[128,512]{1,0:T(8,128)(2,1)S(1)} %get-tuple-element.76), channel_id=1, source_target_pairs={{0,3},{1,2},{2,1},{3,0},{4,7},{5,6},{6,5},{7,4},{8,11},{9,10},{10,... | collective-permute-start | bytes 393224 | tf_op jit(solution)/shard_map/ppermute | solution.py:321
  45.8 1.4 %collective-permute-start.9 = (bf16[128,512]{1,0:T(8,128)(2,1)S(1)}, bf16[128,512]{1,0:T(8,128)(2,1)S(1)}, u32[]{:S(2)}, u32[]{:S(2)}) collective-permute-start(bf16[128,512]{1,0:T(8,128)(2,1)S(1)} %get-tuple-element.73), channel_id=1, source_target_pairs={{0,6},{1,7},{2,4},{3,5},{4,2},{5,3},{6,0},{7,1},{8,14},{9,15},{10,... | collective-permute-start | bytes 393224 | tf_op jit(solution)/shard_map/ppermute | solution.py:321
  47.2 4.2 %collective-permute-done.13.refs_3_ = bf16[128,512]{1,0:T(8,128)(2,1)S(1)} collective-permute-done((bf16[128,512]{1,0:T(8,128)(2,1)S(1)}, bf16[128,512]{1,0:T(8,128)(2,1)S(1)}, u32[]{:S(2)}, u32[]{:S(2)}) %collective-permute-start.13) | collective-permute-done | bytes 131104 | tf_op jit(solution)/shard_map/ppermute | solution.py:321
  51.4 2.2 %collective-permute-start.7 = (bf16[128,512]{1,0:T(8,128)(2,1)S(1)}, bf16[128,512]{1,0:T(8,128)(2,1)S(1)}, u32[]{:S(2)}, u32[]{:S(2)}) collective-permute-start(bf16[128,512]{1,0:T(8,128)(2,1)S(1)} %get-tuple-element.70), channel_id=1, source_target_pairs={{0,7},{1,6},{2,5},{3,4},{4,3},{5,2},{6,1},{7,0},{8,15},{9,14},{10,... | collective-permute-start | bytes 393224 | tf_op jit(solution)/shard_map/ppermute | solution.py:321
  53.7 6.2 %covar_own.3.refs_5_.refs_3_ = bf16[2048,2048]{1,0:T(8,128)(2,1)S(1)} custom-call(s32[1]{0:T(128)} %bitcast.me_ref.refs_0_, f32[1,4096]{1,0:T(1,128)S(1)} %bitcast.13, f32[1,4096]{1,0:T(1,128)S(1)} %bitcast.10), custom_call_target="tpu_custom_call" | custom-call | flops 1 | bytes 1 | tf_op jit(solution)/shard_map/covar_own/pallas_call | solution.py:168
  61.2 1.8 %smooth_part.7.refs_4_ = f32[128,4096]{1,0:T(8,128)S(1)} custom-call(bf16[128,512]{1,0:T(8,128)(2,1)S(1)} %collective-permute-done.10.refs_0_, bf16[128,512]{1,0:T(8,128)(2,1)S(1)} %collective-permute-done.11.refs_1_, bf16[128,512]{1,0:T(8,128)(2,1)S(1)} %collective-permute-done.12.refs_2_, bf16[2048,2048]{1,0:T(8,128)(2,1)S(1)} %covar_own.2.refs_1_.refs_3_, ...), custom_call_target="tpu_custom_call" | custom-call | flops 1 | bytes 1 | tf_op jit(solution)/shard_map/smooth_part/pallas_call | solution.py:258
  65.4 2.0 %collective-permute-start.14 = (bf16[128,512]{1,0:T(8,128)(2,1)S(1)}, bf16[128,512]{1,0:T(8,128)(2,1)S(1)}, u32[]{:S(2)}, u32[]{:S(2)}) collective-permute-start(bf16[128,512]{1,0:T(8,128)(2,1)S(1)} %get-tuple-element.83), channel_id=1, source_target_pairs={{0,1},{1,0},{2,3},{3,2},{4,5},{5,4},{6,7},{7,6},{8,9},{9,8},{10,11... | collective-permute-start | bytes 393224 | tf_op jit(solution)/shard_map/ppermute | solution.py:321
  67.4 1.6 %collective-permute-start.16 = (bf16[128,512]{1,0:T(8,128)(2,1)S(1)}, bf16[128,512]{1,0:T(8,128)(2,1)S(1)}, u32[]{:S(2)}, u32[]{:S(2)}) collective-permute-start(bf16[128,512]{1,0:T(8,128)(2,1)S(1)} %get-tuple-element.85), channel_id=1, source_target_pairs={{0,3},{1,2},{2,1},{3,0},{4,7},{5,6},{6,5},{7,4},{8,11},{9,10},{10,... | collective-permute-start | bytes 393224 | tf_op jit(solution)/shard_map/ppermute | solution.py:321
  69.2 4.1 %collective-permute-start.18 = (bf16[128,512]{1,0:T(8,128)(2,1)S(1)}, bf16[128,512]{1,0:T(8,128)(2,1)S(1)}, u32[]{:S(2)}, u32[]{:S(2)}) collective-permute-start(bf16[128,512]{1,0:T(8,128)(2,1)S(1)} %get-tuple-element.87), channel_id=1, source_target_pairs={{0,5},{1,4},{2,7},{3,6},{4,1},{5,0},{6,3},{7,2},{8,13},{9,12},{10,... | collective-permute-start | bytes 393224 | tf_op jit(solution)/shard_map/ppermute | solution.py:321
  74.5 2.1 %collective-permute-done.15.refs_2_ = bf16[128,512]{1,0:T(8,128)(2,1)S(1)} collective-permute-done((bf16[128,512]{1,0:T(8,128)(2,1)S(1)}, bf16[128,512]{1,0:T(8,128)(2,1)S(1)}, u32[]{:S(2)}, u32[]{:S(2)}) %collective-permute-start.15) | collective-permute-done | bytes 131104 | tf_op jit(solution)/shard_map/ppermute | solution.py:321
  76.6 1.7 %collective-permute-start.20 = (bf16[128,512]{1,0:T(8,128)(2,1)S(1)}, bf16[128,512]{1,0:T(8,128)(2,1)S(1)}, u32[]{:S(2)}, u32[]{:S(2)}) collective-permute-start(bf16[128,512]{1,0:T(8,128)(2,1)S(1)} %get-tuple-element.89), channel_id=1, source_target_pairs={{0,7},{1,6},{2,5},{3,4},{4,3},{5,2},{6,1},{7,0},{8,15},{9,14},{10,... | collective-permute-start | bytes 393224 | tf_op jit(solution)/shard_map/ppermute | solution.py:321
  78.3 5.0 %collective-permute-done.17.refs_4_ = bf16[128,512]{1,0:T(8,128)(2,1)S(1)} collective-permute-done((bf16[128,512]{1,0:T(8,128)(2,1)S(1)}, bf16[128,512]{1,0:T(8,128)(2,1)S(1)}, u32[]{:S(2)}, u32[]{:S(2)}) %collective-permute-start.17) | collective-permute-done | bytes 131104 | tf_op jit(solution)/shard_map/ppermute | solution.py:321
  83.3 3.6 %collective-permute-done.18.refs_5_ = bf16[128,512]{1,0:T(8,128)(2,1)S(1)} collective-permute-done((bf16[128,512]{1,0:T(8,128)(2,1)S(1)}, bf16[128,512]{1,0:T(8,128)(2,1)S(1)}, u32[]{:S(2)}, u32[]{:S(2)}) %collective-permute-start.18) | collective-permute-done | bytes 131104 | tf_op jit(solution)/shard_map/ppermute | solution.py:321
  87.0 1.5 %normal_step.3 = (bf16[128,512]{1,0:T(8,128)(2,1)S(1)}, bf16[128,512]{1,0:T(8,128)(2,1)S(1)}, bf16[128,512]{1,0:T(8,128)(2,1)S(1)}, bf16[128,512]{1,0:T(8,128)(2...) custom-call(bf16[1024,1024]{1,0:T(8,128)(2,1)S(1)} %dense_blocks.1.w, ...), custom_call_target="tpu_custom_call" | custom-call | flops 1 | bytes 1 | tf_op jit(solution)/shard_map/normal_step/pallas_call | solution.py:224
  88.9 4.3 %collective-permute-start.27 = (bf16[128,512]{1,0:T(8,128)(2,1)S(1)}, bf16[128,512]{1,0:T(8,128)(2,1)S(1)}, u32[]{:S(2)}, u32[]{:S(2)}) collective-permute-start(bf16[128,512]{1,0:T(8,128)(2,1)S(1)} %get-tuple-element.97), channel_id=1, source_target_pairs={{0,4},{1,5},{2,6},{3,7},{4,0},{5,1},{6,2},{7,3},{8,12},{9,13},{10,... | collective-permute-start | bytes 393224 | tf_op jit(solution)/shard_map/ppermute | solution.py:321
  93.2 3.1 %collective-permute-start.25 = (bf16[128,512]{1,0:T(8,128)(2,1)S(1)}, bf16[128,512]{1,0:T(8,128)(2,1)S(1)}, u32[]{:S(2)}, u32[]{:S(2)}) collective-permute-start(bf16[128,512]{1,0:T(8,128)(2,1)S(1)} %get-tuple-element.94), channel_id=1, source_target_pairs={{0,2},{1,3},{2,0},{3,1},{4,6},{5,7},{6,4},{7,5},{8,10},{9,11},{10,... | collective-permute-start | bytes 393224 | tf_op jit(solution)/shard_map/ppermute | solution.py:321
  96.3 2.2 %collective-permute-start.23 = (bf16[128,512]{1,0:T(8,128)(2,1)S(1)}, bf16[128,512]{1,0:T(8,128)(2,1)S(1)}, u32[]{:S(2)}, u32[]{:S(2)}) collective-permute-start(bf16[128,512]{1,0:T(8,128)(2,1)S(1)} %get-tuple-element.92), channel_id=1, source_target_pairs={{0,6},{1,7},{2,4},{3,5},{4,2},{5,3},{6,0},{7,1},{8,14},{9,15},{10,... | collective-permute-start | bytes 393224 | tf_op jit(solution)/shard_map/ppermute | solution.py:321
  99.1 3.4 %collective-permute-start.21 = (bf16[128,512]{1,0:T(8,128)(2,1)S(1)}, bf16[128,512]{1,0:T(8,128)(2,1)S(1)}, u32[]{:S(2)}, u32[]{:S(2)}) collective-permute-start(bf16[128,512]{1,0:T(8,128)(2,1)S(1)} %get-tuple-element.90), channel_id=1, source_target_pairs={{0,7},{1,6},{2,5},{3,4},{4,3},{5,2},{6,1},{7,0},{8,15},{9,14},{10,... | collective-permute-start | bytes 393224 | tf_op jit(solution)/shard_map/ppermute | solution.py:321
  103.9 3.1 %collective-permute-done.26.refs_2_ = bf16[128,512]{1,0:T(8,128)(2,1)S(1)} collective-permute-done((bf16[128,512]{1,0:T(8,128)(2,1)S(1)}, bf16[128,512]{1,0:T(8,128)(2,1)S(1)}, u32[]{:S(2)}, u32[]{:S(2)}) %collective-permute-start.26) | collective-permute-done | bytes 131104 | tf_op jit(solution)/shard_map/ppermute | solution.py:321
  107.0 1.9 %smooth_part.10.refs_4_ = f32[128,4096]{1,0:T(8,128)S(1)} custom-call(bf16[128,512]{1,0:T(8,128)(2,1)S(1)} %collective-permute-done.24.refs_0_, bf16[128,512]{1,0:T(8,128)(2,1)S(1)} %collective-permute-done.25.refs_1_, bf16[128,512]{1,0:T(8,128)(2,1)S(1)} %collective-permute-done.26.refs_2_, bf16[2048,2048]{1,0:T(8,128)(2,1)S(1)} %bitcast.7, ...), custom_call_target="tpu_custom_call" | custom-call | flops 1 | bytes 1 | tf_op jit(solution)/shard_map/smooth_part/pallas_call | solution.py:258
  110.3 1.8 %update.3 = f32[128,4096]{1,0:T(8,128)} custom-call(s32[1]{0:T(128)} %bitcast.me_ref.refs_0_, bf16[128,512]{1,0:T(8,128)(2,1)S(1)} %collective-permute-done.21.refs_1_, bf16[2048,2048]{1,0:T(8,128)(2,1)S(1)} %get-tuple-element.71.refs_4_.refs_2_, bf16[2048,2048]{1,0:T(8,128)(2,1)S(1)} %covar_own.3.refs_5_.refs_3_, f32[128,4096]{1,0:T(8,128)S(1)} %smooth_part.11.refs_4_, ...), custom_call_target="tpu_custom_call" | custom-call | flops 1 | bytes 1 | tf_op jit(solution)/shard_map/update/pallas_call | solution.py:305
  (67 shorter events, 13.5 us)
Async XLA Ops:
  1.6 14.8 %copy-start.9 = (f32[4096]{0:T(1024)S(1)}, f32[4096]{0:T(1024)}, u32[]{:S(2)}) copy-start(f32[4096]{0:T(1024)} %param.16) | copy-start | bytes 49156
  2.0 8.9 %collective-permute-start = (bf16[128,512]{1,0:T(8,128)(2,1)S(1)}, bf16[128,512]{1,0:T(8,128)(2,1)S(1)}, u32[]{:S(2)}, u32[]{:S(2)}) collective-permute-start(bf16[128,512]{1,0:T(8,128)(2,1)S(1)} %get-tuple-element.53), channel_id=1, source_target_pairs={{0,1},{1,0},{2,3},{3,2},{4,5},{5,4},{6,7},{7,6},{8,9},{9,8},{10,11... | collective-permute-start | bytes 393224 | tf_op jit(solution)/shard_map/ppermute | solution.py:321
  5.0 10.7 %collective-permute-start.1 = (bf16[128,512]{1,0:T(8,128)(2,1)S(1)}, bf16[128,512]{1,0:T(8,128)(2,1)S(1)}, u32[]{:S(2)}, u32[]{:S(2)}) collective-permute-start(bf16[128,512]{1,0:T(8,128)(2,1)S(1)} %get-tuple-element.54), channel_id=1, source_target_pairs={{0,2},{1,3},{2,0},{3,1},{4,6},{5,7},{6,4},{7,5},{8,10},{9,11},{10,... | collective-permute-start | bytes 393224 | tf_op jit(solution)/shard_map/ppermute | solution.py:321
  6.6 28.6 %collective-permute-start.2 = (bf16[128,512]{1,0:T(8,128)(2,1)S(1)}, bf16[128,512]{1,0:T(8,128)(2,1)S(1)}, u32[]{:S(2)}, u32[]{:S(2)}) collective-permute-start(bf16[128,512]{1,0:T(8,128)(2,1)S(1)} %get-tuple-element.55), channel_id=1, source_target_pairs={{0,3},{1,2},{2,1},{3,0},{4,7},{5,6},{6,5},{7,4},{8,11},{9,10},{10,... | collective-permute-start | bytes 393224 | tf_op jit(solution)/shard_map/ppermute | solution.py:321
  6.6 28.6 %collective-permute-start.3 = (bf16[128,512]{1,0:T(8,128)(2,1)S(1)}, bf16[128,512]{1,0:T(8,128)(2,1)S(1)}, u32[]{:S(2)}, u32[]{:S(2)}) collective-permute-start(bf16[128,512]{1,0:T(8,128)(2,1)S(1)} %get-tuple-element.56), channel_id=1, source_target_pairs={{0,4},{1,5},{2,6},{3,7},{4,0},{5,1},{6,2},{7,3},{8,12},{9,13},{10,... | collective-permute-start | bytes 393224 | tf_op jit(solution)/shard_map/ppermute | solution.py:321
  9.6 25.6 %collective-permute-start.4 = (bf16[128,512]{1,0:T(8,128)(2,1)S(1)}, bf16[128,512]{1,0:T(8,128)(2,1)S(1)}, u32[]{:S(2)}, u32[]{:S(2)}) collective-permute-start(bf16[128,512]{1,0:T(8,128)(2,1)S(1)} %get-tuple-element.57), channel_id=1, source_target_pairs={{0,5},{1,4},{2,7},{3,6},{4,1},{5,0},{6,3},{7,2},{8,13},{9,12},{10,... | collective-permute-start | bytes 393224 | tf_op jit(solution)/shard_map/ppermute | solution.py:321
  10.9 24.3 %collective-permute-start.5 = (bf16[128,512]{1,0:T(8,128)(2,1)S(1)}, bf16[128,512]{1,0:T(8,128)(2,1)S(1)}, u32[]{:S(2)}, u32[]{:S(2)}) collective-permute-start(bf16[128,512]{1,0:T(8,128)(2,1)S(1)} %get-tuple-element.58), channel_id=1, source_target_pairs={{0,6},{1,7},{2,4},{3,5},{4,2},{5,3},{6,0},{7,1},{8,14},{9,15},{10,... | collective-permute-start | bytes 393224 | tf_op jit(solution)/shard_map/ppermute | solution.py:321
  15.7 19.5 %collective-permute-start.6 = (bf16[128,512]{1,0:T(8,128)(2,1)S(1)}, bf16[128,512]{1,0:T(8,128)(2,1)S(1)}, u32[]{:S(2)}, u32[]{:S(2)}) collective-permute-start(bf16[128,512]{1,0:T(8,128)(2,1)S(1)} %get-tuple-element.59), channel_id=1, source_target_pairs={{0,7},{1,6},{2,5},{3,4},{4,3},{5,2},{6,1},{7,0},{8,15},{9,14},{10,... | collective-permute-start | bytes 393224 | tf_op jit(solution)/shard_map/ppermute | solution.py:321
  22.5 38.7 %copy-start = (bf16[2048,2048]{1,0:T(8,128)(2,1)}, bf16[2048,2048]{1,0:T(8,128)(2,1)S(1)}, u32[]{:S(2)}) copy-start(bf16[2048,2048]{1,0:T(8,128)(2,1)S(1)} %covar_own.2.refs_1_.refs_3_) | copy-start | bytes 25165828
  36.7 9.1 %collective-permute-start.10 = (bf16[128,512]{1,0:T(8,128)(2,1)S(1)}, bf16[128,512]{1,0:T(8,128)(2,1)S(1)}, u32[]{:S(2)}, u32[]{:S(2)}) collective-permute-start(bf16[128,512]{1,0:T(8,128)(2,1)S(1)} %get-tuple-element.74), channel_id=1, source_target_pairs={{0,1},{1,0},{2,3},{3,2},{4,5},{5,4},{6,7},{7,6},{8,9},{9,8},{10,11... | collective-permute-start | bytes 393224 | tf_op jit(solution)/shard_map/ppermute | solution.py:321
  40.0 11.5 %collective-permute-start.13 = (bf16[128,512]{1,0:T(8,128)(2,1)S(1)}, bf16[128,512]{1,0:T(8,128)(2,1)S(1)}, u32[]{:S(2)}, u32[]{:S(2)}) collective-permute-start(bf16[128,512]{1,0:T(8,128)(2,1)S(1)} %get-tuple-element.80), channel_id=1, source_target_pairs={{0,4},{1,5},{2,6},{3,7},{4,0},{5,1},{6,2},{7,3},{8,12},{9,13},{10,... | collective-permute-start | bytes 393224 | tf_op jit(solution)/shard_map/ppermute | solution.py:321
  40.0 23.1 %collective-permute-start.8 = (bf16[128,512]{1,0:T(8,128)(2,1)S(1)}, bf16[128,512]{1,0:T(8,128)(2,1)S(1)}, u32[]{:S(2)}, u32[]{:S(2)}) collective-permute-start(bf16[128,512]{1,0:T(8,128)(2,1)S(1)} %get-tuple-element.72), channel_id=1, source_target_pairs={{0,5},{1,4},{2,7},{3,6},{4,1},{5,0},{6,3},{7,2},{8,13},{9,12},{10,... | collective-permute-start | bytes 393224 | tf_op jit(solution)/shard_map/ppermute | solution.py:321
  42.4 18.8 %collective-permute-start.11 = (bf16[128,512]{1,0:T(8,128)(2,1)S(1)}, bf16[128,512]{1,0:T(8,128)(2,1)S(1)}, u32[]{:S(2)}, u32[]{:S(2)}) collective-permute-start(bf16[128,512]{1,0:T(8,128)(2,1)S(1)} %get-tuple-element.75), channel_id=1, source_target_pairs={{0,2},{1,3},{2,0},{3,1},{4,6},{5,7},{6,4},{7,5},{8,10},{9,11},{10,... | collective-permute-start | bytes 393224 | tf_op jit(solution)/shard_map/ppermute | solution.py:321
  42.4 18.8 %collective-permute-start.12 = (bf16[128,512]{1,0:T(8,128)(2,1)S(1)}, bf16[128,512]{1,0:T(8,128)(2,1)S(1)}, u32[]{:S(2)}, u32[]{:S(2)}) collective-permute-start(bf16[128,512]{1,0:T(8,128)(2,1)S(1)} %get-tuple-element.76), channel_id=1, source_target_pairs={{0,3},{1,2},{2,1},{3,0},{4,7},{5,6},{6,5},{7,4},{8,11},{9,10},{10,... | collective-permute-start | bytes 393224 | tf_op jit(solution)/shard_map/ppermute | solution.py:321
  45.8 17.2 %collective-permute-start.9 = (bf16[128,512]{1,0:T(8,128)(2,1)S(1)}, bf16[128,512]{1,0:T(8,128)(2,1)S(1)}, u32[]{:S(2)}, u32[]{:S(2)}) collective-permute-start(bf16[128,512]{1,0:T(8,128)(2,1)S(1)} %get-tuple-element.73), channel_id=1, source_target_pairs={{0,6},{1,7},{2,4},{3,5},{4,2},{5,3},{6,0},{7,1},{8,14},{9,15},{10,... | collective-permute-start | bytes 393224 | tf_op jit(solution)/shard_map/ppermute | solution.py:321
  51.4 13.0 %collective-permute-start.7 = (bf16[128,512]{1,0:T(8,128)(2,1)S(1)}, bf16[128,512]{1,0:T(8,128)(2,1)S(1)}, u32[]{:S(2)}, u32[]{:S(2)}) collective-permute-start(bf16[128,512]{1,0:T(8,128)(2,1)S(1)} %get-tuple-element.70), channel_id=1, source_target_pairs={{0,7},{1,6},{2,5},{3,4},{4,3},{5,2},{6,1},{7,0},{8,15},{9,14},{10,... | collective-permute-start | bytes 393224 | tf_op jit(solution)/shard_map/ppermute | solution.py:321
  63.1 39.5 %slice-start = ((s8[8388608]{0:T(1024)(128)(4,1)}), s8[4194304]{0:T(1024)(128)(4,1)S(1)}, s32[]{:S(2)}) async-start(s8[8388608]{0:T(1024)(128)(4,1)} %bitcast.6), calls=%async_computation | async-start | bytes 8388608
  64.4 38.1 %slice-start.1 = ((s8[8388608]{0:T(1024)(128)(4,1)}), s8[4194304]{0:T(1024)(128)(4,1)S(1)}, s32[]{:S(2)}) async-start(s8[8388608]{0:T(1024)(128)(4,1)} %bitcast.6), calls=%async_computation.1 | async-start | bytes 8388608
  65.4 7.8 %collective-permute-start.14 = (bf16[128,512]{1,0:T(8,128)(2,1)S(1)}, bf16[128,512]{1,0:T(8,128)(2,1)S(1)}, u32[]{:S(2)}, u32[]{:S(2)}) collective-permute-start(bf16[128,512]{1,0:T(8,128)(2,1)S(1)} %get-tuple-element.83), channel_id=1, source_target_pairs={{0,1},{1,0},{2,3},{3,2},{4,5},{5,4},{6,7},{7,6},{8,9},{9,8},{10,11... | collective-permute-start | bytes 393224 | tf_op jit(solution)/shard_map/ppermute | solution.py:321
  67.4 9.1 %collective-permute-start.15 = (bf16[128,512]{1,0:T(8,128)(2,1)S(1)}, bf16[128,512]{1,0:T(8,128)(2,1)S(1)}, u32[]{:S(2)}, u32[]{:S(2)}) collective-permute-start(bf16[128,512]{1,0:T(8,128)(2,1)S(1)} %get-tuple-element.84), channel_id=1, source_target_pairs={{0,2},{1,3},{2,0},{3,1},{4,6},{5,7},{6,4},{7,5},{8,10},{9,11},{10,... | collective-permute-start | bytes 393224 | tf_op jit(solution)/shard_map/ppermute | solution.py:321
  67.4 10.9 %collective-permute-start.16 = (bf16[128,512]{1,0:T(8,128)(2,1)S(1)}, bf16[128,512]{1,0:T(8,128)(2,1)S(1)}, u32[]{:S(2)}, u32[]{:S(2)}) collective-permute-start(bf16[128,512]{1,0:T(8,128)(2,1)S(1)} %get-tuple-element.85), channel_id=1, source_target_pairs={{0,3},{1,2},{2,1},{3,0},{4,7},{5,6},{6,5},{7,4},{8,11},{9,10},{10,... | collective-permute-start | bytes 393224 | tf_op jit(solution)/shard_map/ppermute | solution.py:321
  69.0 14.3 %collective-permute-start.17 = (bf16[128,512]{1,0:T(8,128)(2,1)S(1)}, bf16[128,512]{1,0:T(8,128)(2,1)S(1)}, u32[]{:S(2)}, u32[]{:S(2)}) collective-permute-start(bf16[128,512]{1,0:T(8,128)(2,1)S(1)} %get-tuple-element.86), channel_id=1, source_target_pairs={{0,4},{1,5},{2,6},{3,7},{4,0},{5,1},{6,2},{7,3},{8,12},{9,13},{10,... | collective-permute-start | bytes 393224 | tf_op jit(solution)/shard_map/ppermute | solution.py:321
  69.2 17.8 %collective-permute-start.18 = (bf16[128,512]{1,0:T(8,128)(2,1)S(1)}, bf16[128,512]{1,0:T(8,128)(2,1)S(1)}, u32[]{:S(2)}, u32[]{:S(2)}) collective-permute-start(bf16[128,512]{1,0:T(8,128)(2,1)S(1)} %get-tuple-element.87), channel_id=1, source_target_pairs={{0,5},{1,4},{2,7},{3,6},{4,1},{5,0},{6,3},{7,2},{8,13},{9,12},{10,... | collective-permute-start | bytes 393224 | tf_op jit(solution)/shard_map/ppermute | solution.py:321
  73.3 13.7 %collective-permute-start.19 = (bf16[128,512]{1,0:T(8,128)(2,1)S(1)}, bf16[128,512]{1,0:T(8,128)(2,1)S(1)}, u32[]{:S(2)}, u32[]{:S(2)}) collective-permute-start(bf16[128,512]{1,0:T(8,128)(2,1)S(1)} %get-tuple-element.88), channel_id=1, source_target_pairs={{0,6},{1,7},{2,4},{3,5},{4,2},{5,3},{6,0},{7,1},{8,14},{9,15},{10,... | collective-permute-start | bytes 393224 | tf_op jit(solution)/shard_map/ppermute | solution.py:321
  76.6 10.4 %collective-permute-start.20 = (bf16[128,512]{1,0:T(8,128)(2,1)S(1)}, bf16[128,512]{1,0:T(8,128)(2,1)S(1)}, u32[]{:S(2)}, u32[]{:S(2)}) collective-permute-start(bf16[128,512]{1,0:T(8,128)(2,1)S(1)} %get-tuple-element.89), channel_id=1, source_target_pairs={{0,7},{1,6},{2,5},{3,4},{4,3},{5,2},{6,1},{7,0},{8,15},{9,14},{10,... | collective-permute-start | bytes 393224 | tf_op jit(solution)/shard_map/ppermute | solution.py:321
  88.5 7.8 %collective-permute-start.24 = (bf16[128,512]{1,0:T(8,128)(2,1)S(1)}, bf16[128,512]{1,0:T(8,128)(2,1)S(1)}, u32[]{:S(2)}, u32[]{:S(2)}) collective-permute-start(bf16[128,512]{1,0:T(8,128)(2,1)S(1)} %get-tuple-element.93), channel_id=1, source_target_pairs={{0,1},{1,0},{2,3},{3,2},{4,5},{5,4},{6,7},{7,6},{8,9},{9,8},{10,11... | collective-permute-start | bytes 393224 | tf_op jit(solution)/shard_map/ppermute | solution.py:321
  88.9 10.2 %collective-permute-start.27 = (bf16[128,512]{1,0:T(8,128)(2,1)S(1)}, bf16[128,512]{1,0:T(8,128)(2,1)S(1)}, u32[]{:S(2)}, u32[]{:S(2)}) collective-permute-start(bf16[128,512]{1,0:T(8,128)(2,1)S(1)} %get-tuple-element.97), channel_id=1, source_target_pairs={{0,4},{1,5},{2,6},{3,7},{4,0},{5,1},{6,2},{7,3},{8,12},{9,13},{10,... | collective-permute-start | bytes 393224 | tf_op jit(solution)/shard_map/ppermute | solution.py:321
  93.2 15.7 %collective-permute-start.22 = (bf16[128,512]{1,0:T(8,128)(2,1)S(1)}, bf16[128,512]{1,0:T(8,128)(2,1)S(1)}, u32[]{:S(2)}, u32[]{:S(2)}) collective-permute-start(bf16[128,512]{1,0:T(8,128)(2,1)S(1)} %get-tuple-element.91), channel_id=1, source_target_pairs={{0,5},{1,4},{2,7},{3,6},{4,1},{5,0},{6,3},{7,2},{8,13},{9,12},{10,... | collective-permute-start | bytes 393224 | tf_op jit(solution)/shard_map/ppermute | solution.py:321
  93.2 10.6 %collective-permute-start.25 = (bf16[128,512]{1,0:T(8,128)(2,1)S(1)}, bf16[128,512]{1,0:T(8,128)(2,1)S(1)}, u32[]{:S(2)}, u32[]{:S(2)}) collective-permute-start(bf16[128,512]{1,0:T(8,128)(2,1)S(1)} %get-tuple-element.94), channel_id=1, source_target_pairs={{0,2},{1,3},{2,0},{3,1},{4,6},{5,7},{6,4},{7,5},{8,10},{9,11},{10,... | collective-permute-start | bytes 393224 | tf_op jit(solution)/shard_map/ppermute | solution.py:321
  96.3 10.7 %collective-permute-start.26 = (bf16[128,512]{1,0:T(8,128)(2,1)S(1)}, bf16[128,512]{1,0:T(8,128)(2,1)S(1)}, u32[]{:S(2)}, u32[]{:S(2)}) collective-permute-start(bf16[128,512]{1,0:T(8,128)(2,1)S(1)} %get-tuple-element.95), channel_id=1, source_target_pairs={{0,3},{1,2},{2,1},{3,0},{4,7},{5,6},{6,5},{7,4},{8,11},{9,10},{10,... | collective-permute-start | bytes 393224 | tf_op jit(solution)/shard_map/ppermute | solution.py:321
  96.3 12.6 %collective-permute-start.23 = (bf16[128,512]{1,0:T(8,128)(2,1)S(1)}, bf16[128,512]{1,0:T(8,128)(2,1)S(1)}, u32[]{:S(2)}, u32[]{:S(2)}) collective-permute-start(bf16[128,512]{1,0:T(8,128)(2,1)S(1)} %get-tuple-element.92), channel_id=1, source_target_pairs={{0,6},{1,7},{2,4},{3,5},{4,2},{5,3},{6,0},{7,1},{8,14},{9,15},{10,... | collective-permute-start | bytes 393224 | tf_op jit(solution)/shard_map/ppermute | solution.py:321
  99.1 11.2 %collective-permute-start.21 = (bf16[128,512]{1,0:T(8,128)(2,1)S(1)}, bf16[128,512]{1,0:T(8,128)(2,1)S(1)}, u32[]{:S(2)}, u32[]{:S(2)}) collective-permute-start(bf16[128,512]{1,0:T(8,128)(2,1)S(1)} %get-tuple-element.90), channel_id=1, source_target_pairs={{0,7},{1,6},{2,5},{3,4},{4,3},{5,2},{6,1},{7,0},{8,15},{9,14},{10,... | collective-permute-start | bytes 393224 | tf_op jit(solution)/shard_map/ppermute | solution.py:321
  (8 other events, 45.1 us)

commit v4 on v3

v4 whole, which is shorter than its diff:
```python
import math
import jax
import jax.numpy as jnp
from jax import lax
from jax.experimental import pallas as pl
from jax.experimental.pallas import tpu as pltpu
from jax.sharding import PartitionSpec as P

ITERS = 2
LN2 = math.log(2.0)
F32 = jnp.float32
BF16 = jnp.bfloat16


def params(mib=8):
    return pltpu.CompilerParams(vmem_limit_bytes=mib * 1024 * 1024)


CHEAP = pl.CostEstimate(flops=1, bytes_accessed=1, transcendentals=0)
SMEM = pl.BlockSpec(memory_space=pltpu.SMEM)
VMEM = pl.BlockSpec(memory_space=pltpu.VMEM)
HBM = pl.BlockSpec(memory_space=pltpu.HBM)


def dot(a, b):
    return jnp.dot(a, b, preferred_element_type=F32)


def column(row):
    n = row.shape[1]
    return jnp.broadcast_to(row, (n, n)).T[:, :1]


def pack(me, gains, ndev, epd):
    chd, total = gains.shape
    half = ndev // 2
    order = [*range(1, ndev), 0]

    def body(me_ref, gains_ref, *refs):
        outs, kept, sems = refs[:ndev], refs[ndev : ndev + 2], refs[ndev + 2]

        def place(r):
            return kept[r // half].at[:, pl.ds(r % half * epd, epd)]

        def copy(r):
            theirs = pl.ds(pl.multiple_of((me_ref[0] ^ r) * epd, epd), epd)
            return pltpu.make_async_copy(gains_ref.at[:, theirs], place(r), sems.at[r])

        for r in order:
            copy(r).start()
        for r in order:
            copy(r).wait()
            outs[r][...] = place(r)[...].astype(BF16)

    return pl.pallas_call(
        body,
        out_shape=[jax.ShapeDtypeStruct((chd, epd), BF16)] * ndev + [pltpu.VMEM((chd, total // 2), F32)] * 2,
        in_specs=[SMEM, HBM],
        out_specs=[VMEM] * (ndev + 2),
        scratch_shapes=[pltpu.SemaphoreType.DMA((ndev,))],
        compiler_params=params(),
        cost_estimate=CHEAP,
        name="pack_gains",
    )(me, pltpu.with_memory_space_constraint(gains, pltpu.HBM))


def flip(me, data, ndev, factors=None):
    epd, chans = data.shape
    chd = chans // ndev
    kind = BF16 if factors is None else F32
    more = [] if factors is None else [factors]

    def body(me_ref, data_ref, *refs):
        for r in range(ndev):
            cols = pl.ds(pl.multiple_of((me_ref[0] ^ r) * chd, chd), chd)
            out = data_ref[:, cols].astype(F32).T
            if more:
                out = out * refs[0][:, pl.ds(pl.multiple_of(me_ref[0] * epd, epd), epd)]
            refs[-1][pl.ds(r * chd, chd), :] = out.astype(kind)

    return pl.pallas_call(
        body,
        out_shape=pltpu.VMEM((chans, epd), kind),
        in_specs=[SMEM, VMEM] + [VMEM] * len(more),
        out_specs=VMEM,
        compiler_params=params(),
        cost_estimate=CHEAP,
        name="flip",
    )(me, data, *more)


def dense(me, blocks, channels, ndev):
    nblk, width, _ = blocks.shape
    chans = nblk * width
    chd = chans // ndev

    def body(me_ref, blocks_ref, order_ref, out_ref, left_ref, hot_ref):
        def names_along(dim, shape):
            at = lax.broadcasted_iota(jnp.int32, shape, dim)
            return (((at // chd) ^ me_ref[0]) * chd + at % chd).astype(F32)

        down = names_along(0, (chans, width))
        along = names_along(1, (width, chans))
        for b in range(nblk):
            span = pl.ds(b * width, width)
            names = order_ref[:, span].astype(F32)
            hot = jnp.where(down == names, 1.0, 0.0).astype(BF16)
            left_ref[:, span] = dot(hot, blocks_ref[b]).astype(BF16)
            hot_ref[span, :] = jnp.where(along == column(names), 1.0, 0.0).astype(BF16)
        for r in range(0, ndev, 2):
            rows = pl.ds(r * chd, 2 * chd)
            out_ref[rows, :] = dot(left_ref[rows, :], hot_ref[...]).astype(BF16)

    return pl.pallas_call(
        body,
        out_shape=pltpu.VMEM((chans, chans), BF16),
        in_specs=[SMEM, VMEM, VMEM],
        out_specs=VMEM,
        scratch_shapes=[pltpu.VMEM((chans, chans), BF16)] * 2,
        compiler_params=params(),
        cost_estimate=CHEAP,
        name="dense_blocks",
    )(me, blocks, channels[None, :])


def distances(total):
    def body(out_ref):
        for c in range(0, 2 * total, 128):
            row = lax.broadcasted_iota(jnp.int32, (128, 128), 0)
            away = (row - lax.broadcasted_iota(jnp.int32, (128, 128), 1) + (total - c)).astype(F32)
            out_ref[:, pl.ds(c, 128)] = -away * away

    return pl.pallas_call(
        body,
        out_shape=pltpu.VMEM((128, 2 * total), F32),
        out_specs=VMEM,
        compiler_params=params(),
        cost_estimate=CHEAP,
        name="distances",
    )()


def covar_tiles(me_ref, away_ref, squares_ref, own_ref, offset, k, others, epd, store):
    group = 32
    total = squares_ref.shape[1]
    base = (me_ref[0] ^ offset) * epd + k * 128
    span = pl.ds(pl.multiple_of(base, 128), 128)
    own_ref[...] = jnp.broadcast_to(squares_ref[:, span], (128, 128)).T
    for r in others:
        first = (me_ref[0] ^ r) * epd
        for c in range(0, epd, 128):
            theirs = squares_ref[:, pl.ds(pl.multiple_of(first + c, 128), 128)]
            window = pl.ds(pl.multiple_of(total + first + c - base, 128), 128)
            parts = []
            for g in range(0, 128, group):
                rows = pl.ds(g, group)
                q = lax.rsqrt(own_ref[rows, :] + theirs)
                parts.append((q * jnp.exp2(away_ref[rows, window] * (q * q))).astype(BF16))
            store(r, c, jnp.concatenate(parts, axis=0))


def covar_own(me, away, squares, offsets, epd):
    per = epd // 128
    first = offsets[0]
    count = len(offsets) * epd

    def body(me_ref, away_ref, squares_ref, out_ref, own_ref):
        for n, offset in enumerate(offsets):

            def block(k, _):
                mine = pl.ds(pl.multiple_of(n * epd + k * 128, 128), 128)

                def store(r, c, tile):
                    theirs = pl.ds((r - first) * epd + c, 128)
                    out_ref[mine, theirs] = tile
                    if r != offset:
                        out_ref[theirs, mine] = tile.T

                covar_tiles(me_ref, away_ref, squares_ref, own_ref, offset, k, offsets[n:], epd, store)
                return 0

            lax.fori_loop(0, per, block, 0)

    return pl.pallas_call(
        body,
        out_shape=pltpu.VMEM((count, count), BF16),
        in_specs=[SMEM, VMEM, VMEM],
        out_specs=VMEM,
        scratch_shapes=[pltpu.VMEM((128, 128), F32)],
        compiler_params=params(),
        cost_estimate=CHEAP,
        name="covar_own",
    )(me, away, squares)


def covar_cross(me, away, squares, near, far, epd):
    per = epd // 128
    shape = (len(near) * epd, len(far) * epd)

    def body(me_ref, away_ref, squares_ref, out_ref, flip_ref, own_ref):
        def block(n, _):
            mine = pl.ds(pl.multiple_of(n * 128, 128), 128)

            def store(r, c, tile):
                theirs = pl.ds((r - far[0]) * epd + c, 128)
                out_ref[mine, theirs] = tile
                flip_ref[theirs, mine] = tile.T

            covar_tiles(me_ref, away_ref, squares_ref, own_ref, near[0] + n // per, n % per, far, epd, store)
            return 0

        lax.fori_loop(0, shape[0] // 128, block, 0)

    return pl.pallas_call(
        body,
        out_shape=[pltpu.VMEM(shape, BF16), pltpu.VMEM(shape[::-1], BF16)],
        in_specs=[SMEM, VMEM, VMEM],
        out_specs=[VMEM] * 2,
        scratch_shapes=[pltpu.VMEM((128, 128), F32)],
        compiler_params=params(),
        cost_estimate=CHEAP,
        name="covar_cross",
    )(me, away, squares)


def normal(weights, pieces, resp, stud, order):
    ndev = len(pieces)
    chd, epd = pieces[0].shape
    chans = ndev * chd

    def body(*refs):
        ins, (w_ref, resp_ref, stud_ref), outs, got = refs[:ndev], refs[ndev : ndev + 3], refs[ndev + 3 : -1], refs[-1]
        for r, ref in zip([*order, 0], ins):
            got[pl.ds(r * chd, chd), :] = ref[...]
        for r in range(ndev):
            rows = pl.ds(r * chd, chd)
            product = dot(w_ref[rows, :], got[...])
            outs[r][...] = (stud_ref[rows, :] * (product - resp_ref[rows, :].astype(F32))).astype(BF16)

    return list(
        pl.pallas_call(
            body,
            out_shape=[jax.ShapeDtypeStruct((chd, epd), BF16)] * ndev,
            in_specs=[VMEM] * (3 + ndev),
            out_specs=[VMEM] * ndev,
            scratch_shapes=[pltpu.VMEM((chans, epd), BF16)],
            compiler_params=params(),
            cost_estimate=CHEAP,
            name="normal_step",
        )(*[pieces[r] for r in [*order, 0]], weights, resp, stud)
    )


def terms_of(offsets, half):
    runs = []
    for r in sorted(offsets):
        if runs and runs[-1][1][-1] == r - 1 and r != half:
            runs[-1][1].append(r)
        else:
            runs.append((r // half, [r], r % half))
    return runs


def products(got, offsets, rows, refs):
    half = len(got) // 2
    epd = got[0].shape[1]
    pieces = {r: next(refs) for r in offsets}
    sides = [[next(refs) for _ in side] for side in rows]
    return [
        (
            jnp.concatenate([pieces[r][...] for r in run], axis=1),
            sides[side],
            pl.ds(at * epd, len(run) * epd),
        )
        for side, run, at in terms_of(offsets, half)
    ]


def partial(got, offsets, rows, before):
    chd, epd = got[0].shape
    span = max(block.shape[1] for side in rows for block in side)
    blocks = max(len(side) for side in rows)
    args = [got[r] for r in offsets] + [block for side in rows for block in side]
    more = [] if before is None else [before]

    def body(*refs):
        given = iter(refs)
        terms = products(got, offsets, rows, given)
        before_ref, out_ref = [next(given) for _ in more], refs[-1]
        for b in range(blocks):
            for c in range(0, span, epd):
                cols = pl.ds(b * span + c, epd)
                acc = before_ref[0][:, cols] if more else None
                for left, side, at in terms:
                    term = dot(left, side[b][at, pl.ds(c, epd)])
                    acc = term if acc is None else acc + term
                out_ref[:, cols] = acc

    return pl.pallas_call(
        body,
        out_shape=pltpu.VMEM((chd, blocks * span), F32),
        in_specs=[VMEM] * (len(args) + len(more)),
        out_specs=VMEM,
        compiler_params=params(),
        cost_estimate=CHEAP,
        name="smooth_part",
    )(*args, *more)


def update(me, got, offsets, rows, before, current, factors, lower, upper, last):
    chd, epd = got[0].shape
    ndev = len(got)
    total = ndev * epd
    wide = current[0].shape[1]
    span = max(block.shape[1] for side in rows for block in side)
    args = [got[r] for r in offsets] + [block for side in rows for block in side]

    def body(me_ref, *refs):
        given = iter(refs)
        terms = products(got, offsets, rows, given)
        before_ref = next(given)
        cur_refs = [next(given) for _ in current]
        factors_ref, low, high = next(given), column(next(given)[...]), column(next(given)[...])
        outs = list(given)
        copies = []
        for n in range(ndev):
            cols = pl.ds(n * epd, epd)
            block, c = divmod(n * epd, span)
            acc = before_ref[:, cols]
            for left, side, at in terms:
                acc = acc + dot(left, side[block][at, pl.ds(c, epd)])
            theirs = pl.ds(pl.multiple_of((me_ref[0] ^ n) * epd, epd), epd)
            gone = acc * (0.02 * factors_ref[:, theirs])
            new = jnp.clip(cur_refs[n * epd // wide][:, pl.ds(n * epd % wide, epd)] - gone, low, high)
            if last:
                out_ref, stage, sems = outs
                stage[:, cols] = new
                copies.append(pltpu.make_async_copy(stage.at[:, cols], out_ref.at[:, theirs], sems.at[n]))
                copies[-1].start()
            else:
                outs[0][:, cols] = new
                outs[1 + n][...] = new.astype(BF16)
        for copy in copies:
            copy.wait()

    if last:
        shapes, specs = [jax.ShapeDtypeStruct((chd, total), F32)], [HBM]
        scratch = [pltpu.VMEM((chd, total), F32), pltpu.SemaphoreType.DMA((ndev,))]
    else:
        shapes = [pltpu.VMEM((chd, total), F32)] + [jax.ShapeDtypeStruct((chd, epd), BF16)] * ndev
        specs, scratch = [VMEM] * (1 + ndev), []
    out, *pieces = pl.pallas_call(
        body,
        out_shape=shapes,
        in_specs=[SMEM] + [VMEM] * (len(args) + len(current) + 4),
        out_specs=specs,
        scratch_shapes=scratch,
        compiler_params=params(),
        cost_estimate=CHEAP,
        name="update",
    )(me, *args, before, *current, factors, lower, upper)
    return out, pieces


def swap(pieces):
    ndev = len(pieces)
    return [pieces[0]] + [
        lax.ppermute(pieces[r], "wide", [(i, i ^ r) for i in range(ndev)]) for r in range(1, ndev)
    ]


CFG = {'o1': '6712345', 'g2': '67,0123,4,5', 't2': (4,), 'n2': 1, 'o3': '6712345', 'g4': '67,0123,4,5'}


def fast(gains, response, student, blocks, channels, lower, upper, lengths, amplitude):
    ndev = lax.axis_size("wide")
    epd = gains.shape[1] // ndev
    half = ndev // 2
    near, far = list(range(half)), list(range(half, ndev))
    me = lax.axis_index("wide").astype(jnp.int32).reshape(1)
    low, high = lower[None, :], upper[None, :]
    squares = (lengths * lengths * LN2)[None, :]
    factors = (amplitude * jnp.sqrt(lengths * math.sqrt(2.0 * LN2)))[None, :]
    tied = lax.optimization_barrier
    digits = lambda text: [int(c) for c in text]
    order = digits(CFG["o1"])
    groups2 = [digits(g) for g in CFG["g2"].split(",")]
    groups4 = [digits(g) for g in CFG["g4"].split(",")]

    *packed, kept_near, kept_far = pack(me, gains, ndev, epd)
    got = swap(packed)
    weights = dense(me, blocks, channels, ndev)
    resp = flip(me, response, ndev)
    stud = flip(me, student, ndev, factors)
    away = distances(gains.shape[1])
    near_far, far_near = covar_cross(me, away, squares, near, far, epd)
    arrived, near_far, far_near = tied(([got[r] for r in order], near_far, far_near))
    got = {0: got[0], **dict(zip(order, arrived))}

    misfit = normal(weights, got, resp, stud, order)
    part, misfit = tied((squares, misfit))
    far_far = covar_own(me, away, part, far, epd)
    for r in CFG["t2"]:
        misfit[r], far_far = tied((misfit[r], far_far))
    n2 = CFG["n2"]
    if n2 == 0:
        part, far_far = tied((squares, far_far))
        near_near = covar_own(me, away, part, near, epd)
    if n2 == -1:
        near_near = covar_own(me, away, squares, near, epd)
        misfit[0], near_near = tied((misfit[0], near_near))
    got = swap(misfit)
    far_rows = [far_near, far_far]
    total = None
    for n, group in enumerate(groups2[:-1]):
        if n == n2 and n2 > 0:
            part, total = tied((squares, total))
            near_near = covar_own(me, away, part, near, epd)
        rows = [[], far_rows] if min(group) >= half else [[near_near, near_far], far_rows]
        total = partial(got, group, rows, total)
    rows = [[near_near, near_far], far_rows]
    kept, packed = update(me, got, groups2[-1], rows, total, [kept_near, kept_far], factors, low, high, False)

    order = digits(CFG["o3"])
    got = swap(normal(weights, swap(packed), resp, stud, order))
    total = None
    for group in groups4[:-1]:
        total = partial(got, group, rows, total)
    out, _ = update(me, got, groups4[-1], rows, total, [kept], factors, low, high, True)
    return out


def covar_stack(lengths, amplitude, span):
    total = lengths.shape[0]
    count = total // span
    rows = jnp.arange(total, dtype=jnp.int32)

    def one_block(index):
        start = index * span
        cols = start + jnp.arange(span, dtype=jnp.int32)
        diff = (rows[:, None] - cols[None, :]).astype(lengths.dtype)
        left = lengths[:, None]
        right = lax.dynamic_slice_in_dim(lengths, start, span, 0)[None, :]
        amp_right = lax.dynamic_slice_in_dim(amplitude, start, span, 0)[None, :]
        denom = left * left + right * right
        vals = (
            amplitude[:, None]
            * amp_right
            * jnp.sqrt(2.0 * left * right / denom)
            * jnp.exp(-diff * diff / denom)
        )
        return vals.astype(BF16)

    return lax.map(one_block, jnp.arange(count, dtype=jnp.int32))


def data_rows(packed, resp_perm, stud_perm, blocks, order, inverse):
    rows, chans = packed.shape
    nblk, width = (blocks.shape[0], blocks.shape[1])
    moved = jnp.take(packed, order, axis=1).reshape(rows, nblk, width)
    product = jnp.einsum("rbi,bij->rbj", moved, blocks, preferred_element_type=F32).reshape(rows, chans)
    permuted = stud_perm.astype(F32) * (product - resp_perm.astype(F32))
    return jnp.take(permuted, inverse, axis=1).astype(BF16)


def general(gains, response, student, blocks, order, lower, upper, lengths, amplitude):
    nwide = lax.axis_size("wide")
    chd, epochs = gains.shape
    epd = epochs // nwide
    chans = chd * nwide
    inverse = jnp.zeros((chans,), jnp.int32).at[order].set(jnp.arange(chans, dtype=jnp.int32))
    resp_perm = jnp.take(response, order, axis=1)
    stud_perm = jnp.take(student, order, axis=1)
    span = min(256, epochs)
    kernel_stack = covar_stack(lengths, amplitude, span)
    current = gains
    for step in range(ITERS):
        packed = current.astype(BF16).reshape(chd, nwide, epd)
        got = (
            lax.all_to_all(packed, "wide", split_axis=1, concat_axis=0, tiled=True)
            .reshape(chans, epd)
            .T
        )
        misfit_rows = data_rows(got, resp_perm, stud_perm, blocks, order, inverse)
        misfit = lax.all_to_all(
            misfit_rows.T.reshape(chans, 1, epd), "wide", split_axis=0, concat_axis=1, tiled=True
        ).reshape(chd, epochs)
        smoothed = jnp.einsum("ce,bes->cbs", misfit, kernel_stack, preferred_element_type=F32).reshape(
            chd, epochs
        )
        current = jnp.clip(current - 0.02 * smoothed, lower[:, None], upper[:, None])
    return current


def per_device(*args):
    ndev = lax.axis_size("wide")
    chd, epochs = args[0].shape
    fits = ndev >= 8 and ndev & (ndev - 1) == 0 and chd % 128 == 0 and (epochs // ndev) % 256 == 0
    return (fast if fits else general)(*args)


def solution(mesh):
    placed = (
        P(("half", "wide"), None),
        P("wide", "half"),
        P("wide", "half"),
        P("half", None, None),
        P("half"),
        P(("half", "wide")),
        P(("half", "wide")),
        P(),
        P(),
    )
    return jax.shard_map(
        per_device, mesh=mesh, in_specs=placed, out_specs=P(("half", "wide"), None), check_vma=False
    )
```

time: 114 us -> 108 us (0.947); the launches traced: 112 us -> 108 us
  waiting for transfers between devices: 20 us -> 12.2 us
  starting transfers between devices: 50 us -> 56.9 us
  local copies, waits for them, and re-layouts: 1.95 us -> 0.08 us
  Pallas kernels: 39.7 us -> 38.1 us
    ppermute x28, waiting for transfers between devices: 20 us -> 12.2 us  [swap(): lax.ppermute(pieces[r], 'wide', [(i, i ^ r) for i in range(ndev)])]
    ppermute x28, starting transfers between devices: 50 us -> 56.9 us  [swap(): lax.ppermute(pieces[r], 'wide', [(i, i ^ r) for i in range(ndev)])]
    unnamed x24 -> x28, local copies, waits for them, and re-layouts: 1.95 us -> 0.08 us
    pallas_call x1, Pallas kernels: 8.67 us -> 6.92 us  [covar_cross(): pl.pallas_call(body, out_shape=[pltpu.VMEM(shape, BF16), pltpu.VMEM(shape...]
    pallas_call x2, Pallas kernels: 12.2 us -> 10.6 us  [covar_own(): pl.pallas_call(body, out_shape=pltpu.VMEM((count, count), BF16), in_specs...]
    pallas_call x1, Pallas kernels: 0.37 us -> 1.59 us  [pack(): pl.pallas_call(body, out_shape=[jax.ShapeDtypeStruct((chd, epd), BF16)] *...]
    pallas_call x4 -> x5, Pallas kernels: 3.47 us -> 4.24 us  [the longest x2 2.8 us: update(): pl.pallas_call(body, out_shape=shapes, in_specs=[SMEM] + [VMEM] * (len(ar...]
  transfers between devices with their start and end apart: 28 -> 28, of which waited for: 7 -> 9; matrix products, arithmetic and copies ran while one was open for 0% -> 0% of each run, Pallas kernels for 30% -> 29%
where the time goes in v4:
time: 108 us
  starting transfers between devices  56.9 us (53%)
  Pallas kernels  38.1 us (35%)
  waiting for transfers between devices  12.2 us (11%)
    ppermute x28, starting transfers between devices, swap(): lax.ppermute(pieces[r], 'wide', [(i, i ^ r) for i in range(ndev)])  56.9 us
    ppermute x28, waiting for transfers between devices, swap(): lax.ppermute(pieces[r], 'wide', [(i, i ^ r) for i in range(ndev)])  12.2 us
    pallas_call x2, Pallas kernels, covar_own(): pl.pallas_call(body, out_shape=pltpu.VMEM((count, count), BF16), in_specs...  10.6 us
    pallas_call x6, Pallas kernels, partial(): pl.pallas_call(body, out_shape=pltpu.VMEM((chd, blocks * span), F32), in_...  9.02 us
    pallas_call x1, Pallas kernels, covar_cross(): pl.pallas_call(body, out_shape=[pltpu.VMEM(shape, BF16), pltpu.VMEM(shape...  6.92 us
    pallas_call x1, Pallas kernels, dense(): pl.pallas_call(body, out_shape=pltpu.VMEM((chans, chans), BF16), in_specs...  2.94 us
    pallas_call x2, Pallas kernels, update(): pl.pallas_call(body, out_shape=shapes, in_specs=[SMEM] + [VMEM] * (len(ar...  2.8 us
    pallas_call x2, Pallas kernels, normal(): pl.pallas_call(body, out_shape=[jax.ShapeDtypeStruct((chd, epd), BF16)] *...  2.75 us
  transfers between devices with their start and end apart: 28, of which 9 were waited for; matrix products, arithmetic and copies ran while one was open for 0% of the time, Pallas kernels for 29%

profile of v4, /device:TPU:0, one launch (start us, length us, event | category | flops | bytes accessed | tf_op | source)
XLA Modules:
  0.0 107.9 jit_solution(2683734597493588952)
XLA Ops:
  0.0 1.6 %pack_gains.1 = (bf16[128,512]{1,0:T(8,128)(2,1)S(1)}, bf16[128,512]{1,0:T(8,128)(2,1)S(1)}, bf16[128,512]{1,0:T(8,128)(2,1)S(1)}, bf16[128,512]{1,0:T(8,128)(2,...) custom-call(s32[1]{0:T(128)} %bitcast.me_ref, ...), custom_call_target="tpu_custom_call" | custom-call | flops 1 | bytes 1 | tf_op jit(solution)/shard_map/pack_gains/pallas_call | solution.py:55
  1.6 5.1 %collective-permute-start = (bf16[128,512]{1,0:T(8,128)(2,1)S(1)}, bf16[128,512]{1,0:T(8,128)(2,1)S(1)}, u32[]{:S(2)}, u32[]{:S(2)}) collective-permute-start(bf16[128,512]{1,0:T(8,128)(2,1)S(1)} %get-tuple-element.64), channel_id=1, source_target_pairs={{0,6},{1,7},{2,4},{3,5},{4,2},{5,3},{6,0},{7,1},{8,14},{9,15},{10,... | collective-permute-start | bytes 393224 | tf_op jit(solution)/shard_map/ppermute | solution.py:368
  8.3 3.1 %collective-permute-start.4 = (bf16[128,512]{1,0:T(8,128)(2,1)S(1)}, bf16[128,512]{1,0:T(8,128)(2,1)S(1)}, u32[]{:S(2)}, u32[]{:S(2)}) collective-permute-start(bf16[128,512]{1,0:T(8,128)(2,1)S(1)} %get-tuple-element.68), channel_id=1, source_target_pairs={{0,3},{1,2},{2,1},{3,0},{4,7},{5,6},{6,5},{7,4},{8,11},{9,10},{10,... | collective-permute-start | bytes 393224 | tf_op jit(solution)/shard_map/ppermute | solution.py:368
  12.5 5.2 %collective-permute-start.5 = (bf16[128,512]{1,0:T(8,128)(2,1)S(1)}, bf16[128,512]{1,0:T(8,128)(2,1)S(1)}, u32[]{:S(2)}, u32[]{:S(2)}) collective-permute-start(bf16[128,512]{1,0:T(8,128)(2,1)S(1)} %get-tuple-element.69), channel_id=1, source_target_pairs={{0,4},{1,5},{2,6},{3,7},{4,0},{5,1},{6,2},{7,3},{8,12},{9,13},{10,... | collective-permute-start | bytes 393224 | tf_op jit(solution)/shard_map/ppermute | solution.py:368
  17.7 4.1 %collective-permute-start.6 = (bf16[128,512]{1,0:T(8,128)(2,1)S(1)}, bf16[128,512]{1,0:T(8,128)(2,1)S(1)}, u32[]{:S(2)}, u32[]{:S(2)}) collective-permute-start(bf16[128,512]{1,0:T(8,128)(2,1)S(1)} %get-tuple-element.70), channel_id=1, source_target_pairs={{0,5},{1,4},{2,7},{3,6},{4,1},{5,0},{6,3},{7,2},{8,13},{9,12},{10,... | collective-permute-start | bytes 393224 | tf_op jit(solution)/shard_map/ppermute | solution.py:368
  22.2 2.9 %dense_blocks.1.refs_8_ = bf16[1024,1024]{1,0:T(8,128)(2,1)S(1)} custom-call(s32[1]{0:T(128)} %bitcast.me_ref, bf16[4,256,256]{2,1,0:T(8,128)(2,1)S(1)} %copy-done.8, s32[1,1024]{1,0:T(1,128)S(1)} %bitcast.12), custom_call_target="tpu_custom_call" | custom-call | flops 1 | bytes 1 | tf_op jit(solution)/shard_map/dense_blocks/pallas_call | solution.py:114
  25.2 6.9 %covar_cross.1 = (bf16[2048,2048]{1,0:T(8,128)(2,1)S(1)}, bf16[2048,2048]{1,0:T(8,128)(2,1)S(1)}) custom-call(s32[1]{0:T(128)} %bitcast.me_ref, f32[128,8192]{1,0:T(8,128)S(1)} %distances.1.away_ref, f32[1,4096]{1,0:T(1,128)S(1)} %bitcast.9), custom_call_target="tpu_custom_call" | custom-call | flops 1 | bytes 1 | tf_op jit(solution)/shard_map/covar_cross/pallas_call | solution.py:214
  32.2 1.5 %normal_step.2 = (bf16[128,512]{1,0:T(8,128)(2,1)S(1)}, bf16[128,512]{1,0:T(8,128)(2,1)S(1)}, bf16[128,512]{1,0:T(8,128)(2,1)S(1)}, bf16[128,512]{1,0:T(8,128)(2...) custom-call(bf16[128,512]{1,0:T(8,128)(2,1)S(1)} %collective-permute, ...), custom_call_target="tpu_custom_call" | custom-call | flops 1 | bytes 1 | tf_op jit(solution)/shard_map/normal_step/pallas_call | solution.py:241
  33.7 1.6 %collective-permute-start.8 = (bf16[128,512]{1,0:T(8,128)(2,1)S(1)}, bf16[128,512]{1,0:T(8,128)(2,1)S(1)}, u32[]{:S(2)}, u32[]{:S(2)}) collective-permute-start(bf16[128,512]{1,0:T(8,128)(2,1)S(1)} %get-tuple-element.90), channel_id=1, source_target_pairs={{0,6},{1,7},{2,4},{3,5},{4,2},{5,3},{6,0},{7,1},{8,14},{9,15},{10,... | collective-permute-start | bytes 393224 | tf_op jit(solution)/shard_map/ppermute | solution.py:368
  35.4 3.1 %collective-permute-start.9 = (bf16[128,512]{1,0:T(8,128)(2,1)S(1)}, bf16[128,512]{1,0:T(8,128)(2,1)S(1)}, u32[]{:S(2)}, u32[]{:S(2)}) collective-permute-start(bf16[128,512]{1,0:T(8,128)(2,1)S(1)} %get-tuple-element.91), channel_id=1, source_target_pairs={{0,7},{1,6},{2,5},{3,4},{4,3},{5,2},{6,1},{7,0},{8,15},{9,14},{10,... | collective-permute-start | bytes 393224 | tf_op jit(solution)/shard_map/ppermute | solution.py:368
  39.1 2.9 %collective-permute-start.13 = (bf16[128,512]{1,0:T(8,128)(2,1)S(1)}, bf16[128,512]{1,0:T(8,128)(2,1)S(1)}, u32[]{:S(2)}, u32[]{:S(2)}) collective-permute-start(bf16[128,512]{1,0:T(8,128)(2,1)S(1)} %get-tuple-element.102), channel_id=1, source_target_pairs={{0,3},{1,2},{2,1},{3,0},{4,7},{5,6},{6,5},{7,4},{8,11},{9,10},{10,... | collective-permute-start | bytes 393224 | tf_op jit(solution)/shard_map/ppermute | solution.py:368
  42.0 5.2 %covar_own.2.refs_3_.refs_7_.refs_2_.refs_4_.refs_5_ = bf16[2048,2048]{1,0:T(8,128)(2,1)S(1)} custom-call(s32[1]{0:T(128)} %bitcast.me_ref, f32[128,8192]{1,0:T(8,128)S(1)} %distances.1.away_ref, f32[1,4096]{1,0:T(1,128)S(1)} %bitcast.10), custom_call_target="tpu_custom_call" | custom-call | flops 1 | bytes 1 | tf_op jit(solution)/shard_map/covar_own/pallas_call | solution.py:184
  48.0 2.2 %collective-permute-start.7 = (bf16[128,512]{1,0:T(8,128)(2,1)S(1)}, bf16[128,512]{1,0:T(8,128)(2,1)S(1)}, u32[]{:S(2)}, u32[]{:S(2)}) collective-permute-start(bf16[128,512]{1,0:T(8,128)(2,1)S(1)} %get-tuple-element.89), channel_id=1, source_target_pairs={{0,5},{1,4},{2,7},{3,6},{4,1},{5,0},{6,3},{7,2},{8,13},{9,12},{10,... | collective-permute-start | bytes 393224 | tf_op jit(solution)/shard_map/ppermute | solution.py:368
  50.2 1.4 %smooth_part.6.refs_8_ = f32[128,4096]{1,0:T(8,128)S(1)} custom-call(bf16[128,512]{1,0:T(8,128)(2,1)S(1)} %collective-permute-done.8.refs_0_, bf16[128,512]{1,0:T(8,128)(2,1)S(1)} %collective-permute-done.9.refs_1_, bf16[2048,2048]{1,0:T(8,128)(2,1)S(1)} %get-tuple-element.92.refs_2_.refs_6_.refs_1_.refs_3_.refs_4_, ...), custom_call_target="tpu_custom_call" | custom-call | flops 1 | bytes 1 | tf_op jit(solution)/shard_map/smooth_part/pallas_call | solution.py:299
  51.6 5.4 %covar_own.3.refs_4_.refs_1_.refs_2_ = bf16[2048,2048]{1,0:T(8,128)(2,1)S(1)} custom-call(s32[1]{0:T(128)} %bitcast.me_ref, f32[128,8192]{1,0:T(8,128)S(1)} %distances.1.away_ref, f32[1,4096]{1,0:T(1,128)S(1)} %bitcast.11), custom_call_target="tpu_custom_call" | custom-call | flops 1 | bytes 1 | tf_op jit(solution)/shard_map/covar_own/pallas_call | solution.py:184
  57.0 2.4 %smooth_part.7.refs_3_ = f32[128,4096]{1,0:T(8,128)S(1)} custom-call(bf16[128,512]{1,0:T(8,128)(2,1)S(1)} %get-tuple-element.99.refs_0_, bf16[128,512]{1,0:T(8,128)(2,1)S(1)} %collective-permute-done.11.refs_1_, bf16[128,512]{1,0:T(8,128)(2,1)S(1)} %collective-permute-done.12.refs_2_, bf16[128,512]{1,0:T(8,128)(2,1)S(1)} %collective-permute-done.13.refs_3_, ...), custom_call_target="tpu_custom_call" | custom-call | flops 1 | bytes 1 | tf_op jit(solution)/shard_map/smooth_part/pallas_call | solution.py:299
  61.3 1.7 %collective-permute-start.14 = (bf16[128,512]{1,0:T(8,128)(2,1)S(1)}, bf16[128,512]{1,0:T(8,128)(2,1)S(1)}, u32[]{:S(2)}, u32[]{:S(2)}) collective-permute-start(bf16[128,512]{1,0:T(8,128)(2,1)S(1)} %get-tuple-element.106), channel_id=1, source_target_pairs={{0,6},{1,7},{2,4},{3,5},{4,2},{5,3},{6,0},{7,1},{8,14},{9,15},{10,... | collective-permute-start | bytes 393224 | tf_op jit(solution)/shard_map/ppermute | solution.py:368
  63.0 3.1 %collective-permute-start.15 = (bf16[128,512]{1,0:T(8,128)(2,1)S(1)}, bf16[128,512]{1,0:T(8,128)(2,1)S(1)}, u32[]{:S(2)}, u32[]{:S(2)}) collective-permute-start(bf16[128,512]{1,0:T(8,128)(2,1)S(1)} %get-tuple-element.107), channel_id=1, source_target_pairs={{0,7},{1,6},{2,5},{3,4},{4,3},{5,2},{6,1},{7,0},{8,15},{9,14},{10,... | collective-permute-start | bytes 393224 | tf_op jit(solution)/shard_map/ppermute | solution.py:368
  66.7 2.9 %collective-permute-start.18 = (bf16[128,512]{1,0:T(8,128)(2,1)S(1)}, bf16[128,512]{1,0:T(8,128)(2,1)S(1)}, u32[]{:S(2)}, u32[]{:S(2)}) collective-permute-start(bf16[128,512]{1,0:T(8,128)(2,1)S(1)} %get-tuple-element.110), channel_id=1, source_target_pairs={{0,3},{1,2},{2,1},{3,0},{4,7},{5,6},{6,5},{7,4},{8,11},{9,10},{10,... | collective-permute-start | bytes 393224 | tf_op jit(solution)/shard_map/ppermute | solution.py:368
  70.3 3.1 %collective-permute-done.15.refs_1_ = bf16[128,512]{1,0:T(8,128)(2,1)S(1)} collective-permute-done((bf16[128,512]{1,0:T(8,128)(2,1)S(1)}, bf16[128,512]{1,0:T(8,128)(2,1)S(1)}, u32[]{:S(2)}, u32[]{:S(2)}) %collective-permute-start.15) | collective-permute-done | bytes 131104 | tf_op jit(solution)/shard_map/ppermute | solution.py:368
  73.4 3.1 %collective-permute-start.20 = (bf16[128,512]{1,0:T(8,128)(2,1)S(1)}, bf16[128,512]{1,0:T(8,128)(2,1)S(1)}, u32[]{:S(2)}, u32[]{:S(2)}) collective-permute-start(bf16[128,512]{1,0:T(8,128)(2,1)S(1)} %get-tuple-element.112), channel_id=1, source_target_pairs={{0,5},{1,4},{2,7},{3,6},{4,1},{5,0},{6,3},{7,2},{8,13},{9,12},{10,... | collective-permute-start | bytes 393224 | tf_op jit(solution)/shard_map/ppermute | solution.py:368
  77.3 1.6 %collective-permute-done.19.refs_5_ = bf16[128,512]{1,0:T(8,128)(2,1)S(1)} collective-permute-done((bf16[128,512]{1,0:T(8,128)(2,1)S(1)}, bf16[128,512]{1,0:T(8,128)(2,1)S(1)}, u32[]{:S(2)}, u32[]{:S(2)}) %collective-permute-start.19) | collective-permute-done | bytes 131104 | tf_op jit(solution)/shard_map/ppermute | solution.py:368
  78.9 2.0 %collective-permute-done.20.refs_6_ = bf16[128,512]{1,0:T(8,128)(2,1)S(1)} collective-permute-done((bf16[128,512]{1,0:T(8,128)(2,1)S(1)}, bf16[128,512]{1,0:T(8,128)(2,1)S(1)}, u32[]{:S(2)}, u32[]{:S(2)}) %collective-permute-start.20) | collective-permute-done | bytes 131104 | tf_op jit(solution)/shard_map/ppermute | solution.py:368
  82.2 2.1 %collective-permute-start.26 = (bf16[128,512]{1,0:T(8,128)(2,1)S(1)}, bf16[128,512]{1,0:T(8,128)(2,1)S(1)}, u32[]{:S(2)}, u32[]{:S(2)}) collective-permute-start(bf16[128,512]{1,0:T(8,128)(2,1)S(1)} %get-tuple-element.120), channel_id=1, source_target_pairs={{0,6},{1,7},{2,4},{3,5},{4,2},{5,3},{6,0},{7,1},{8,14},{9,15},{10,... | collective-permute-start | bytes 393224 | tf_op jit(solution)/shard_map/ppermute | solution.py:368
  84.2 3.8 %collective-permute-start.27 = (bf16[128,512]{1,0:T(8,128)(2,1)S(1)}, bf16[128,512]{1,0:T(8,128)(2,1)S(1)}, u32[]{:S(2)}, u32[]{:S(2)}) collective-permute-start(bf16[128,512]{1,0:T(8,128)(2,1)S(1)} %get-tuple-element.121), channel_id=1, source_target_pairs={{0,7},{1,6},{2,5},{3,4},{4,3},{5,2},{6,1},{7,0},{8,15},{9,14},{10,... | collective-permute-start | bytes 393224 | tf_op jit(solution)/shard_map/ppermute | solution.py:368
  88.1 3.5 %collective-permute-start.25 = (bf16[128,512]{1,0:T(8,128)(2,1)S(1)}, bf16[128,512]{1,0:T(8,128)(2,1)S(1)}, u32[]{:S(2)}, u32[]{:S(2)}) collective-permute-start(bf16[128,512]{1,0:T(8,128)(2,1)S(1)} %get-tuple-element.119), channel_id=1, source_target_pairs={{0,3},{1,2},{2,1},{3,0},{4,7},{5,6},{6,5},{7,4},{8,11},{9,10},{10,... | collective-permute-start | bytes 393224 | tf_op jit(solution)/shard_map/ppermute | solution.py:368
  91.6 1.6 %collective-permute-start.22 = (bf16[128,512]{1,0:T(8,128)(2,1)S(1)}, bf16[128,512]{1,0:T(8,128)(2,1)S(1)}, u32[]{:S(2)}, u32[]{:S(2)}) collective-permute-start(bf16[128,512]{1,0:T(8,128)(2,1)S(1)} %get-tuple-element.115), channel_id=1, source_target_pairs={{0,4},{1,5},{2,6},{3,7},{4,0},{5,1},{6,2},{7,3},{8,12},{9,13},{10,... | collective-permute-start | bytes 393224 | tf_op jit(solution)/shard_map/ppermute | solution.py:368
  93.2 2.2 %collective-permute-done.27.refs_1_ = bf16[128,512]{1,0:T(8,128)(2,1)S(1)} collective-permute-done((bf16[128,512]{1,0:T(8,128)(2,1)S(1)}, bf16[128,512]{1,0:T(8,128)(2,1)S(1)}, u32[]{:S(2)}, u32[]{:S(2)}) %collective-permute-start.27) | collective-permute-done | bytes 131104 | tf_op jit(solution)/shard_map/ppermute | solution.py:368
  95.4 3.5 %collective-permute-start.21 = (bf16[128,512]{1,0:T(8,128)(2,1)S(1)}, bf16[128,512]{1,0:T(8,128)(2,1)S(1)}, u32[]{:S(2)}, u32[]{:S(2)}) collective-permute-start(bf16[128,512]{1,0:T(8,128)(2,1)S(1)} %get-tuple-element.114), channel_id=1, source_target_pairs={{0,5},{1,4},{2,7},{3,6},{4,1},{5,0},{6,3},{7,2},{8,13},{9,12},{10,... | collective-permute-start | bytes 393224 | tf_op jit(solution)/shard_map/ppermute | solution.py:368
  99.0 1.4 %smooth_part.9.refs_8_ = f32[128,4096]{1,0:T(8,128)S(1)} custom-call(bf16[128,512]{1,0:T(8,128)(2,1)S(1)} %collective-permute-done.26.refs_0_, bf16[128,512]{1,0:T(8,128)(2,1)S(1)} %collective-permute-done.27.refs_1_, bf16[2048,2048]{1,0:T(8,128)(2,1)S(1)} %covar_own.3.refs_4_.refs_1_.refs_2_, ...), custom_call_target="tpu_custom_call" | custom-call | flops 1 | bytes 1 | tf_op jit(solution)/shard_map/smooth_part/pallas_call | solution.py:299
  100.6 2.3 %smooth_part.10.refs_5_ = f32[128,4096]{1,0:T(8,128)S(1)} custom-call(bf16[128,512]{1,0:T(8,128)(2,1)S(1)} %get-tuple-element.116.refs_0_, bf16[128,512]{1,0:T(8,128)(2,1)S(1)} %collective-permute-done.23.refs_1_, bf16[128,512]{1,0:T(8,128)(2,1)S(1)} %collective-permute-done.24.refs_2_, bf16[128,512]{1,0:T(8,128)(2,1)S(1)} %collective-permute-done.25.refs_3_, ...), custom_call_target="tpu_custom_call" | custom-call | flops 1 | bytes 1 | tf_op jit(solution)/shard_map/smooth_part/pallas_call | solution.py:299
  105.9 1.8 %update.3 = f32[128,4096]{1,0:T(8,128)} custom-call(s32[1]{0:T(128)} %bitcast.me_ref, bf16[128,512]{1,0:T(8,128)(2,1)S(1)} %collective-permute-done.21.refs_0_, bf16[2048,2048]{1,0:T(8,128)(2,1)S(1)} %covar_own.3.refs_4_.refs_1_.refs_2_, bf16[2048,2048]{1,0:T(8,128)(2,1)S(1)} %get-tuple-element.97.refs_5_.refs_2_.refs_3_, ...), custom_call_target="tpu_custom_call" | custom-call | flops 1 | bytes 1 | tf_op jit(solution)/shard_map/update/pallas_call | solution.py:352
  (71 shorter events, 12.8 us)
Async XLA Ops:
  1.6 10.9 %collective-permute-start = (bf16[128,512]{1,0:T(8,128)(2,1)S(1)}, bf16[128,512]{1,0:T(8,128)(2,1)S(1)}, u32[]{:S(2)}, u32[]{:S(2)}) collective-permute-start(bf16[128,512]{1,0:T(8,128)(2,1)S(1)} %get-tuple-element.64), channel_id=1, source_target_pairs={{0,6},{1,7},{2,4},{3,5},{4,2},{5,3},{6,0},{7,1},{8,14},{9,15},{10,... | collective-permute-start | bytes 393224 | tf_op jit(solution)/shard_map/ppermute | solution.py:368
  6.7 11.0 %collective-permute-start.1 = (bf16[128,512]{1,0:T(8,128)(2,1)S(1)}, bf16[128,512]{1,0:T(8,128)(2,1)S(1)}, u32[]{:S(2)}, u32[]{:S(2)}) collective-permute-start(bf16[128,512]{1,0:T(8,128)(2,1)S(1)} %get-tuple-element.65), channel_id=1, source_target_pairs={{0,7},{1,6},{2,5},{3,4},{4,3},{5,2},{6,1},{7,0},{8,15},{9,14},{10,... | collective-permute-start | bytes 393224 | tf_op jit(solution)/shard_map/ppermute | solution.py:368
  7.9 24.3 %collective-permute-start.2 = (bf16[128,512]{1,0:T(8,128)(2,1)S(1)}, bf16[128,512]{1,0:T(8,128)(2,1)S(1)}, u32[]{:S(2)}, u32[]{:S(2)}) collective-permute-start(bf16[128,512]{1,0:T(8,128)(2,1)S(1)} %get-tuple-element.66), channel_id=1, source_target_pairs={{0,1},{1,0},{2,3},{3,2},{4,5},{5,4},{6,7},{7,6},{8,9},{9,8},{10,11... | collective-permute-start | bytes 393224 | tf_op jit(solution)/shard_map/ppermute | solution.py:368
  8.3 23.9 %collective-permute-start.3 = (bf16[128,512]{1,0:T(8,128)(2,1)S(1)}, bf16[128,512]{1,0:T(8,128)(2,1)S(1)}, u32[]{:S(2)}, u32[]{:S(2)}) collective-permute-start(bf16[128,512]{1,0:T(8,128)(2,1)S(1)} %get-tuple-element.67), channel_id=1, source_target_pairs={{0,2},{1,3},{2,0},{3,1},{4,6},{5,7},{6,4},{7,5},{8,10},{9,11},{10,... | collective-permute-start | bytes 393224 | tf_op jit(solution)/shard_map/ppermute | solution.py:368
  8.3 23.9 %collective-permute-start.4 = (bf16[128,512]{1,0:T(8,128)(2,1)S(1)}, bf16[128,512]{1,0:T(8,128)(2,1)S(1)}, u32[]{:S(2)}, u32[]{:S(2)}) collective-permute-start(bf16[128,512]{1,0:T(8,128)(2,1)S(1)} %get-tuple-element.68), channel_id=1, source_target_pairs={{0,3},{1,2},{2,1},{3,0},{4,7},{5,6},{6,5},{7,4},{8,11},{9,10},{10,... | collective-permute-start | bytes 393224 | tf_op jit(solution)/shard_map/ppermute | solution.py:368
  12.5 19.7 %copy-start.4 = (bf16[1024,512]{1,0:T(8,128)(2,1)}, bf16[1024,512]{1,0:T(8,128)(2,1)S(1)}, u32[]{:S(2)}) copy-start(bf16[1024,512]{1,0:T(8,128)(2,1)S(1)} %flip.2.refs_9_) | copy-start | bytes 3145732
  12.5 19.7 %collective-permute-start.5 = (bf16[128,512]{1,0:T(8,128)(2,1)S(1)}, bf16[128,512]{1,0:T(8,128)(2,1)S(1)}, u32[]{:S(2)}, u32[]{:S(2)}) collective-permute-start(bf16[128,512]{1,0:T(8,128)(2,1)S(1)} %get-tuple-element.69), channel_id=1, source_target_pairs={{0,4},{1,5},{2,6},{3,7},{4,0},{5,1},{6,2},{7,3},{8,12},{9,13},{10,... | collective-permute-start | bytes 393224 | tf_op jit(solution)/shard_map/ppermute | solution.py:368
  17.7 14.5 %collective-permute-start.6 = (bf16[128,512]{1,0:T(8,128)(2,1)S(1)}, bf16[128,512]{1,0:T(8,128)(2,1)S(1)}, u32[]{:S(2)}, u32[]{:S(2)}) collective-permute-start(bf16[128,512]{1,0:T(8,128)(2,1)S(1)} %get-tuple-element.70), channel_id=1, source_target_pairs={{0,5},{1,4},{2,7},{3,6},{4,1},{5,0},{6,3},{7,2},{8,13},{9,12},{10,... | collective-permute-start | bytes 393224 | tf_op jit(solution)/shard_map/ppermute | solution.py:368
  33.7 13.5 %collective-permute-start.8 = (bf16[128,512]{1,0:T(8,128)(2,1)S(1)}, bf16[128,512]{1,0:T(8,128)(2,1)S(1)}, u32[]{:S(2)}, u32[]{:S(2)}) collective-permute-start(bf16[128,512]{1,0:T(8,128)(2,1)S(1)} %get-tuple-element.90), channel_id=1, source_target_pairs={{0,6},{1,7},{2,4},{3,5},{4,2},{5,3},{6,0},{7,1},{8,14},{9,15},{10,... | collective-permute-start | bytes 393224 | tf_op jit(solution)/shard_map/ppermute | solution.py:368
  35.4 12.7 %collective-permute-start.9 = (bf16[128,512]{1,0:T(8,128)(2,1)S(1)}, bf16[128,512]{1,0:T(8,128)(2,1)S(1)}, u32[]{:S(2)}, u32[]{:S(2)}) collective-permute-start(bf16[128,512]{1,0:T(8,128)(2,1)S(1)} %get-tuple-element.91), channel_id=1, source_target_pairs={{0,7},{1,6},{2,5},{3,4},{4,3},{5,2},{6,1},{7,0},{8,15},{9,14},{10,... | collective-permute-start | bytes 393224 | tf_op jit(solution)/shard_map/ppermute | solution.py:368
  38.5 18.5 %collective-permute-start.11 = (bf16[128,512]{1,0:T(8,128)(2,1)S(1)}, bf16[128,512]{1,0:T(8,128)(2,1)S(1)}, u32[]{:S(2)}, u32[]{:S(2)}) collective-permute-start(bf16[128,512]{1,0:T(8,128)(2,1)S(1)} %get-tuple-element.100), channel_id=1, source_target_pairs={{0,1},{1,0},{2,3},{3,2},{4,5},{5,4},{6,7},{7,6},{8,9},{9,8},{10,11... | collective-permute-start | bytes 393224 | tf_op jit(solution)/shard_map/ppermute | solution.py:368
  39.1 18.0 %collective-permute-start.12 = (bf16[128,512]{1,0:T(8,128)(2,1)S(1)}, bf16[128,512]{1,0:T(8,128)(2,1)S(1)}, u32[]{:S(2)}, u32[]{:S(2)}) collective-permute-start(bf16[128,512]{1,0:T(8,128)(2,1)S(1)} %get-tuple-element.101), channel_id=1, source_target_pairs={{0,2},{1,3},{2,0},{3,1},{4,6},{5,7},{6,4},{7,5},{8,10},{9,11},{10,... | collective-permute-start | bytes 393224 | tf_op jit(solution)/shard_map/ppermute | solution.py:368
  39.1 18.0 %collective-permute-start.13 = (bf16[128,512]{1,0:T(8,128)(2,1)S(1)}, bf16[128,512]{1,0:T(8,128)(2,1)S(1)}, u32[]{:S(2)}, u32[]{:S(2)}) collective-permute-start(bf16[128,512]{1,0:T(8,128)(2,1)S(1)} %get-tuple-element.102), channel_id=1, source_target_pairs={{0,3},{1,2},{2,1},{3,0},{4,7},{5,6},{6,5},{7,4},{8,11},{9,10},{10,... | collective-permute-start | bytes 393224 | tf_op jit(solution)/shard_map/ppermute | solution.py:368
  47.2 12.2 %collective-permute-start.10 = (bf16[128,512]{1,0:T(8,128)(2,1)S(1)}, bf16[128,512]{1,0:T(8,128)(2,1)S(1)}, u32[]{:S(2)}, u32[]{:S(2)}) collective-permute-start(bf16[128,512]{1,0:T(8,128)(2,1)S(1)} %get-tuple-element.98), channel_id=1, source_target_pairs={{0,4},{1,5},{2,6},{3,7},{4,0},{5,1},{6,2},{7,3},{8,12},{9,13},{10,... | collective-permute-start | bytes 393224 | tf_op jit(solution)/shard_map/ppermute | solution.py:368
  48.0 12.2 %collective-permute-start.7 = (bf16[128,512]{1,0:T(8,128)(2,1)S(1)}, bf16[128,512]{1,0:T(8,128)(2,1)S(1)}, u32[]{:S(2)}, u32[]{:S(2)}) collective-permute-start(bf16[128,512]{1,0:T(8,128)(2,1)S(1)} %get-tuple-element.89), channel_id=1, source_target_pairs={{0,5},{1,4},{2,7},{3,6},{4,1},{5,0},{6,3},{7,2},{8,13},{9,12},{10,... | collective-permute-start | bytes 393224 | tf_op jit(solution)/shard_map/ppermute | solution.py:368
  60.3 20.6 %copy-start.1 = (f32[1024,512]{1,0:T(8,128)S(1)}, f32[1024,512]{1,0:T(8,128)}, u32[]{:S(2)}) copy-start(f32[1024,512]{1,0:T(8,128)} %copy-done) | copy-start | bytes 6291460
  60.3 20.6 %copy-start.3 = (bf16[1024,1024]{1,0:T(8,128)(2,1)S(1)}, bf16[1024,1024]{1,0:T(8,128)(2,1)}, u32[]{:S(2)}) copy-start(bf16[1024,1024]{1,0:T(8,128)(2,1)} %copy-done.2) | copy-start | bytes 6291460
  60.3 20.6 %copy-start.5 = (bf16[1024,512]{1,0:T(8,128)(2,1)S(1)}, bf16[1024,512]{1,0:T(8,128)(2,1)}, u32[]{:S(2)}) copy-start(bf16[1024,512]{1,0:T(8,128)(2,1)} %copy-done.4) | copy-start | bytes 3145732
  61.3 8.4 %collective-permute-start.14 = (bf16[128,512]{1,0:T(8,128)(2,1)S(1)}, bf16[128,512]{1,0:T(8,128)(2,1)S(1)}, u32[]{:S(2)}, u32[]{:S(2)}) collective-permute-start(bf16[128,512]{1,0:T(8,128)(2,1)S(1)} %get-tuple-element.106), channel_id=1, source_target_pairs={{0,6},{1,7},{2,4},{3,5},{4,2},{5,3},{6,0},{7,1},{8,14},{9,15},{10,... | collective-permute-start | bytes 393224 | tf_op jit(solution)/shard_map/ppermute | solution.py:368
  63.0 10.4 %collective-permute-start.15 = (bf16[128,512]{1,0:T(8,128)(2,1)S(1)}, bf16[128,512]{1,0:T(8,128)(2,1)S(1)}, u32[]{:S(2)}, u32[]{:S(2)}) collective-permute-start(bf16[128,512]{1,0:T(8,128)(2,1)S(1)} %get-tuple-element.107), channel_id=1, source_target_pairs={{0,7},{1,6},{2,5},{3,4},{4,3},{5,2},{6,1},{7,0},{8,15},{9,14},{10,... | collective-permute-start | bytes 393224 | tf_op jit(solution)/shard_map/ppermute | solution.py:368
  66.1 10.4 %collective-permute-start.16 = (bf16[128,512]{1,0:T(8,128)(2,1)S(1)}, bf16[128,512]{1,0:T(8,128)(2,1)S(1)}, u32[]{:S(2)}, u32[]{:S(2)}) collective-permute-start(bf16[128,512]{1,0:T(8,128)(2,1)S(1)} %get-tuple-element.108), channel_id=1, source_target_pairs={{0,1},{1,0},{2,3},{3,2},{4,5},{5,4},{6,7},{7,6},{8,9},{9,8},{10,11... | collective-permute-start | bytes 393224 | tf_op jit(solution)/shard_map/ppermute | solution.py:368
  66.6 9.9 %collective-permute-start.17 = (bf16[128,512]{1,0:T(8,128)(2,1)S(1)}, bf16[128,512]{1,0:T(8,128)(2,1)S(1)}, u32[]{:S(2)}, u32[]{:S(2)}) collective-permute-start(bf16[128,512]{1,0:T(8,128)(2,1)S(1)} %get-tuple-element.109), channel_id=1, source_target_pairs={{0,2},{1,3},{2,0},{3,1},{4,6},{5,7},{6,4},{7,5},{8,10},{9,11},{10,... | collective-permute-start | bytes 393224 | tf_op jit(solution)/shard_map/ppermute | solution.py:368
  66.7 10.6 %collective-permute-start.18 = (bf16[128,512]{1,0:T(8,128)(2,1)S(1)}, bf16[128,512]{1,0:T(8,128)(2,1)S(1)}, u32[]{:S(2)}, u32[]{:S(2)}) collective-permute-start(bf16[128,512]{1,0:T(8,128)(2,1)S(1)} %get-tuple-element.110), channel_id=1, source_target_pairs={{0,3},{1,2},{2,1},{3,0},{4,7},{5,6},{6,5},{7,4},{8,11},{9,10},{10,... | collective-permute-start | bytes 393224 | tf_op jit(solution)/shard_map/ppermute | solution.py:368
  69.7 9.2 %collective-permute-start.19 = (bf16[128,512]{1,0:T(8,128)(2,1)S(1)}, bf16[128,512]{1,0:T(8,128)(2,1)S(1)}, u32[]{:S(2)}, u32[]{:S(2)}) collective-permute-start(bf16[128,512]{1,0:T(8,128)(2,1)S(1)} %get-tuple-element.111), channel_id=1, source_target_pairs={{0,4},{1,5},{2,6},{3,7},{4,0},{5,1},{6,2},{7,3},{8,12},{9,13},{10,... | collective-permute-start | bytes 393224 | tf_op jit(solution)/shard_map/ppermute | solution.py:368
  73.4 7.5 %collective-permute-start.20 = (bf16[128,512]{1,0:T(8,128)(2,1)S(1)}, bf16[128,512]{1,0:T(8,128)(2,1)S(1)}, u32[]{:S(2)}, u32[]{:S(2)}) collective-permute-start(bf16[128,512]{1,0:T(8,128)(2,1)S(1)} %get-tuple-element.112), channel_id=1, source_target_pairs={{0,5},{1,4},{2,7},{3,6},{4,1},{5,0},{6,3},{7,2},{8,13},{9,12},{10,... | collective-permute-start | bytes 393224 | tf_op jit(solution)/shard_map/ppermute | solution.py:368
  82.2 9.4 %collective-permute-start.26 = (bf16[128,512]{1,0:T(8,128)(2,1)S(1)}, bf16[128,512]{1,0:T(8,128)(2,1)S(1)}, u32[]{:S(2)}, u32[]{:S(2)}) collective-permute-start(bf16[128,512]{1,0:T(8,128)(2,1)S(1)} %get-tuple-element.120), channel_id=1, source_target_pairs={{0,6},{1,7},{2,4},{3,5},{4,2},{5,3},{6,0},{7,1},{8,14},{9,15},{10,... | collective-permute-start | bytes 393224 | tf_op jit(solution)/shard_map/ppermute | solution.py:368
  84.2 11.2 %collective-permute-start.27 = (bf16[128,512]{1,0:T(8,128)(2,1)S(1)}, bf16[128,512]{1,0:T(8,128)(2,1)S(1)}, u32[]{:S(2)}, u32[]{:S(2)}) collective-permute-start(bf16[128,512]{1,0:T(8,128)(2,1)S(1)} %get-tuple-element.121), channel_id=1, source_target_pairs={{0,7},{1,6},{2,5},{3,4},{4,3},{5,2},{6,1},{7,0},{8,15},{9,14},{10,... | collective-permute-start | bytes 393224 | tf_op jit(solution)/shard_map/ppermute | solution.py:368
  88.1 12.2 %collective-permute-start.23 = (bf16[128,512]{1,0:T(8,128)(2,1)S(1)}, bf16[128,512]{1,0:T(8,128)(2,1)S(1)}, u32[]{:S(2)}, u32[]{:S(2)}) collective-permute-start(bf16[128,512]{1,0:T(8,128)(2,1)S(1)} %get-tuple-element.117), channel_id=1, source_target_pairs={{0,1},{1,0},{2,3},{3,2},{4,5},{5,4},{6,7},{7,6},{8,9},{9,8},{10,11... | collective-permute-start | bytes 393224 | tf_op jit(solution)/shard_map/ppermute | solution.py:368
  88.1 12.3 %collective-permute-start.24 = (bf16[128,512]{1,0:T(8,128)(2,1)S(1)}, bf16[128,512]{1,0:T(8,128)(2,1)S(1)}, u32[]{:S(2)}, u32[]{:S(2)}) collective-permute-start(bf16[128,512]{1,0:T(8,128)(2,1)S(1)} %get-tuple-element.118), channel_id=1, source_target_pairs={{0,2},{1,3},{2,0},{3,1},{4,6},{5,7},{6,4},{7,5},{8,10},{9,11},{10,... | collective-permute-start | bytes 393224 | tf_op jit(solution)/shard_map/ppermute | solution.py:368
  88.1 12.5 %collective-permute-start.25 = (bf16[128,512]{1,0:T(8,128)(2,1)S(1)}, bf16[128,512]{1,0:T(8,128)(2,1)S(1)}, u32[]{:S(2)}, u32[]{:S(2)}) collective-permute-start(bf16[128,512]{1,0:T(8,128)(2,1)S(1)} %get-tuple-element.119), channel_id=1, source_target_pairs={{0,3},{1,2},{2,1},{3,0},{4,7},{5,6},{6,5},{7,4},{8,11},{9,10},{10,... | collective-permute-start | bytes 393224 | tf_op jit(solution)/shard_map/ppermute | solution.py:368
  91.6 12.6 %collective-permute-start.22 = (bf16[128,512]{1,0:T(8,128)(2,1)S(1)}, bf16[128,512]{1,0:T(8,128)(2,1)S(1)}, u32[]{:S(2)}, u32[]{:S(2)}) collective-permute-start(bf16[128,512]{1,0:T(8,128)(2,1)S(1)} %get-tuple-element.115), channel_id=1, source_target_pairs={{0,4},{1,5},{2,6},{3,7},{4,0},{5,1},{6,2},{7,3},{8,12},{9,13},{10,... | collective-permute-start | bytes 393224 | tf_op jit(solution)/shard_map/ppermute | solution.py:368
  95.4 10.5 %collective-permute-start.21 = (bf16[128,512]{1,0:T(8,128)(2,1)S(1)}, bf16[128,512]{1,0:T(8,128)(2,1)S(1)}, u32[]{:S(2)}, u32[]{:S(2)}) collective-permute-start(bf16[128,512]{1,0:T(8,128)(2,1)S(1)} %get-tuple-element.114), channel_id=1, source_target_pairs={{0,5},{1,4},{2,7},{3,6},{4,1},{5,0},{6,3},{7,2},{8,13},{9,12},{10,... | collective-permute-start | bytes 393224 | tf_op jit(solution)/shard_map/ppermute | solution.py:368
  (10 other events, 71.1 us)

commit v5 on v4

--- a/solution.py
+++ b/solution.py
@@ -261,11 +261,15 @@
     return runs
 
 
+def sides_of(offsets, half):
+    return sorted({r // half for r in offsets})
+
+
 def products(got, offsets, rows, refs):
     half = len(got) // 2
     epd = got[0].shape[1]
     pieces = {r: next(refs) for r in offsets}
-    sides = [[next(refs) for _ in side] for side in rows]
+    sides = {side: [next(refs) for _ in rows[side]] for side in sides_of(offsets, half)}
     return [
         (
             jnp.concatenate([pieces[r][...] for r in run], axis=1),
@@ -280,7 +284,7 @@
     chd, epd = got[0].shape
     span = max(block.shape[1] for side in rows for block in side)
     blocks = max(len(side) for side in rows)
-    args = [got[r] for r in offsets] + [block for side in rows for block in side]
+    args = [got[r] for r in offsets] + [block for side in sides_of(offsets, len(got) // 2) for block in rows[side]]
     more = [] if before is None else [before]
 
     def body(*refs):
@@ -313,7 +317,7 @@
     total = ndev * epd
     wide = current[0].shape[1]
     span = max(block.shape[1] for side in rows for block in side)
-    args = [got[r] for r in offsets] + [block for side in rows for block in side]
+    args = [got[r] for r in offsets] + [block for side in sides_of(offsets, len(got) // 2) for block in rows[side]]
 
     def body(me_ref, *refs):
         given = iter(refs)
@@ -369,9 +373,6 @@
     ]
 
 
-CFG = {'o1': '6712345', 'g2': '67,0123,4,5', 't2': (4,), 'n2': 1, 'o3': '6712345', 'g4': '67,0123,4,5'}
-
-
 def fast(gains, response, student, blocks, channels, lower, upper, lengths, amplitude):
     ndev = lax.axis_size("wide")
     epd = gains.shape[1] // ndev
@@ -382,10 +383,10 @@
     squares = (lengths * lengths * LN2)[None, :]
     factors = (amplitude * jnp.sqrt(lengths * math.sqrt(2.0 * LN2)))[None, :]
     tied = lax.optimization_barrier
-    digits = lambda text: [int(c) for c in text]
-    order = digits(CFG["o1"])
-    groups2 = [digits(g) for g in CFG["g2"].split(",")]
-    groups4 = [digits(g) for g in CFG["g4"].split(",")]
+
+    order = [*far[half // 2 :], *near[1:], *far[: half // 2]]
+    groups = [far[:1], near, far[1:-1]]
+    latest = far[-1:]
 
     *packed, kept_near, kept_far = pack(me, gains, ndev, epd)
     got = swap(packed)
@@ -400,33 +401,23 @@
     misfit = normal(weights, got, resp, stud, order)
     part, misfit = tied((squares, misfit))
     far_far = covar_own(me, away, part, far, epd)
-    for r in CFG["t2"]:
-        misfit[r], far_far = tied((misfit[r], far_far))
-    n2 = CFG["n2"]
-    if n2 == 0:
-        part, far_far = tied((squares, far_far))
-        near_near = covar_own(me, away, part, near, epd)
-    if n2 == -1:
-        near_near = covar_own(me, away, squares, near, epd)
-        misfit[0], near_near = tied((misfit[0], near_near))
+    misfit[-1], far_far = tied((misfit[-1], far_far))
+    near_near = covar_own(me, away, squares, near, epd)
+    misfit[0], near_near = tied((misfit[0], near_near))
     got = swap(misfit)
-    far_rows = [far_near, far_far]
+    rows = [[near_near, near_far], [far_near, far_far]]
     total = None
-    for n, group in enumerate(groups2[:-1]):
-        if n == n2 and n2 > 0:
-            part, total = tied((squares, total))
-            near_near = covar_own(me, away, part, near, epd)
-        rows = [[], far_rows] if min(group) >= half else [[near_near, near_far], far_rows]
+    for group in groups:
         total = partial(got, group, rows, total)
-    rows = [[near_near, near_far], far_rows]
-    kept, packed = update(me, got, groups2[-1], rows, total, [kept_near, kept_far], factors, low, high, False)
-
-    order = digits(CFG["o3"])
+    current = [kept_near, kept_far]
+    current, packed = update(me, got, latest, rows, total, current, factors, low, high, False)
+
+    order = [*far[:0:-1], *near[1:], far[0]]
     got = swap(normal(weights, swap(packed), resp, stud, order))
     total = None
-    for group in groups4[:-1]:
+    for group in groups:
         total = partial(got, group, rows, total)
-    out, _ = update(me, got, groups4[-1], rows, total, [kept], factors, low, high, True)
+    out, _ = update(me, got, latest, rows, total, [current], factors, low, high, True)
     return out
 
 

time: 108 us -> 106 us (0.981)
  waiting for transfers between devices: 12.2 us -> 8.06 us
  starting transfers between devices: 56.9 us -> 59.2 us
    ppermute x28, waiting for transfers between devices: 12.2 us -> 8.06 us  [swap(): lax.ppermute(pieces[r], 'wide', [(i, i ^ r) for i in range(ndev)])]
    ppermute x28, starting transfers between devices: 56.9 us -> 59.2 us  [swap(): lax.ppermute(pieces[r], 'wide', [(i, i ^ r) for i in range(ndev)])]
  transfers between devices with their start and end apart: 28 -> 28, of which waited for: 9 -> 5; matrix products, arithmetic and copies ran while one was open for 0% -> 0% of each run, Pallas kernels for 29% -> 30%
where the time goes in v5:
time: 106 us
  starting transfers between devices  59.2 us (56%)
  Pallas kernels  38.4 us (36%)
  waiting for transfers between devices  8.06 us (8%)
    ppermute x28, starting transfers between devices, swap(): lax.ppermute(pieces[r], 'wide', [(i, i ^ r) for i in range(ndev)])  59.2 us
    pallas_call x2, Pallas kernels, covar_own(): pl.pallas_call(body, out_shape=pltpu.VMEM((count, count), BF16), in_specs...  10.6 us
    pallas_call x6, Pallas kernels, partial(): pl.pallas_call(body, out_shape=pltpu.VMEM((chd, blocks * span), F32), in_...  9.5 us
    ppermute x28, waiting for transfers between devices, swap(): lax.ppermute(pieces[r], 'wide', [(i, i ^ r) for i in range(ndev)])  8.06 us
    pallas_call x1, Pallas kernels, covar_cross(): pl.pallas_call(body, out_shape=[pltpu.VMEM(shape, BF16), pltpu.VMEM(shape...  6.94 us
    pallas_call x1, Pallas kernels, dense(): pl.pallas_call(body, out_shape=pltpu.VMEM((chans, chans), BF16), in_specs...  2.94 us
    pallas_call x2, Pallas kernels, update(): pl.pallas_call(body, out_shape=shapes, in_specs=[SMEM] + [VMEM] * (len(ar...  2.8 us
    pallas_call x2, Pallas kernels, normal(): pl.pallas_call(body, out_shape=[jax.ShapeDtypeStruct((chd, epd), BF16)] *...  2.55 us
  transfers between devices with their start and end apart: 28, of which 5 were waited for; matrix products, arithmetic and copies ran while one was open for 0% of the time, Pallas kernels for 30%

profile of v5, /device:TPU:0, one launch (start us, length us, event | category | flops | bytes accessed | tf_op | source)
XLA Modules:
  0.0 106.3 jit_solution(5030577162400687963)
XLA Ops:
  0.0 1.6 %pack_gains.1 = (bf16[128,512]{1,0:T(8,128)(2,1)S(1)}, bf16[128,512]{1,0:T(8,128)(2,1)S(1)}, bf16[128,512]{1,0:T(8,128)(2,1)S(1)}, bf16[128,512]{1,0:T(8,128)(2,...) custom-call(s32[1]{0:T(128)} %bitcast.me_ref, ...), custom_call_target="tpu_custom_call" | custom-call | flops 1 | bytes 1 | tf_op jit(solution)/shard_map/pack_gains/pallas_call | solution.py:55
  1.6 5.1 %collective-permute-start = (bf16[128,512]{1,0:T(8,128)(2,1)S(1)}, bf16[128,512]{1,0:T(8,128)(2,1)S(1)}, u32[]{:S(2)}, u32[]{:S(2)}) collective-permute-start(bf16[128,512]{1,0:T(8,128)(2,1)S(1)} %get-tuple-element.64), channel_id=1, source_target_pairs={{0,6},{1,7},{2,4},{3,5},{4,2},{5,3},{6,0},{7,1},{8,14},{9,15},{10,... | collective-permute-start | bytes 393224 | tf_op jit(solution)/shard_map/ppermute | solution.py:372
  8.3 3.1 %collective-permute-start.4 = (bf16[128,512]{1,0:T(8,128)(2,1)S(1)}, bf16[128,512]{1,0:T(8,128)(2,1)S(1)}, u32[]{:S(2)}, u32[]{:S(2)}) collective-permute-start(bf16[128,512]{1,0:T(8,128)(2,1)S(1)} %get-tuple-element.68), channel_id=1, source_target_pairs={{0,3},{1,2},{2,1},{3,0},{4,7},{5,6},{6,5},{7,4},{8,11},{9,10},{10,... | collective-permute-start | bytes 393224 | tf_op jit(solution)/shard_map/ppermute | solution.py:372
  12.5 5.2 %collective-permute-start.5 = (bf16[128,512]{1,0:T(8,128)(2,1)S(1)}, bf16[128,512]{1,0:T(8,128)(2,1)S(1)}, u32[]{:S(2)}, u32[]{:S(2)}) collective-permute-start(bf16[128,512]{1,0:T(8,128)(2,1)S(1)} %get-tuple-element.69), channel_id=1, source_target_pairs={{0,4},{1,5},{2,6},{3,7},{4,0},{5,1},{6,2},{7,3},{8,12},{9,13},{10,... | collective-permute-start | bytes 393224 | tf_op jit(solution)/shard_map/ppermute | solution.py:372
  17.7 4.1 %collective-permute-start.6 = (bf16[128,512]{1,0:T(8,128)(2,1)S(1)}, bf16[128,512]{1,0:T(8,128)(2,1)S(1)}, u32[]{:S(2)}, u32[]{:S(2)}) collective-permute-start(bf16[128,512]{1,0:T(8,128)(2,1)S(1)} %get-tuple-element.70), channel_id=1, source_target_pairs={{0,5},{1,4},{2,7},{3,6},{4,1},{5,0},{6,3},{7,2},{8,13},{9,12},{10,... | collective-permute-start | bytes 393224 | tf_op jit(solution)/shard_map/ppermute | solution.py:372
  22.2 2.9 %dense_blocks.1.refs_8_ = bf16[1024,1024]{1,0:T(8,128)(2,1)S(1)} custom-call(s32[1]{0:T(128)} %bitcast.me_ref, bf16[4,256,256]{2,1,0:T(8,128)(2,1)S(1)} %copy-done.2, s32[1,1024]{1,0:T(1,128)S(1)} %bitcast.12), custom_call_target="tpu_custom_call" | custom-call | flops 1 | bytes 1 | tf_op jit(solution)/shard_map/dense_blocks/pallas_call | solution.py:114
  25.2 6.9 %covar_cross.1 = (bf16[2048,2048]{1,0:T(8,128)(2,1)S(1)}, bf16[2048,2048]{1,0:T(8,128)(2,1)S(1)}) custom-call(s32[1]{0:T(128)} %bitcast.me_ref, f32[128,8192]{1,0:T(8,128)S(1)} %distances.1.away_ref, f32[1,4096]{1,0:T(1,128)S(1)} %bitcast.6), custom_call_target="tpu_custom_call" | custom-call | flops 1 | bytes 1 | tf_op jit(solution)/shard_map/covar_cross/pallas_call | solution.py:214
  32.2 1.3 %normal_step.2 = (bf16[128,512]{1,0:T(8,128)(2,1)S(1)}, bf16[128,512]{1,0:T(8,128)(2,1)S(1)}, bf16[128,512]{1,0:T(8,128)(2,1)S(1)}, bf16[128,512]{1,0:T(8,128)(2...) custom-call(bf16[128,512]{1,0:T(8,128)(2,1)S(1)} %collective-permute, ...), custom_call_target="tpu_custom_call" | custom-call | flops 1 | bytes 1 | tf_op jit(solution)/shard_map/normal_step/pallas_call | solution.py:241
  33.5 1.6 %collective-permute-start.10 = (bf16[128,512]{1,0:T(8,128)(2,1)S(1)}, bf16[128,512]{1,0:T(8,128)(2,1)S(1)}, u32[]{:S(2)}, u32[]{:S(2)}) collective-permute-start(bf16[128,512]{1,0:T(8,128)(2,1)S(1)} %get-tuple-element.98), channel_id=1, source_target_pairs={{0,1},{1,0},{2,3},{3,2},{4,5},{5,4},{6,7},{7,6},{8,9},{9,8},{10,11... | collective-permute-start | bytes 393224 | tf_op jit(solution)/shard_map/ppermute | solution.py:372
  35.0 2.9 %collective-permute-start.8 = (bf16[128,512]{1,0:T(8,128)(2,1)S(1)}, bf16[128,512]{1,0:T(8,128)(2,1)S(1)}, u32[]{:S(2)}, u32[]{:S(2)}) collective-permute-start(bf16[128,512]{1,0:T(8,128)(2,1)S(1)} %get-tuple-element.94), channel_id=1, source_target_pairs={{0,5},{1,4},{2,7},{3,6},{4,1},{5,0},{6,3},{7,2},{8,13},{9,12},{10,... | collective-permute-start | bytes 393224 | tf_op jit(solution)/shard_map/ppermute | solution.py:372
  37.9 2.9 %collective-permute-start.12 = (bf16[128,512]{1,0:T(8,128)(2,1)S(1)}, bf16[128,512]{1,0:T(8,128)(2,1)S(1)}, u32[]{:S(2)}, u32[]{:S(2)}) collective-permute-start(bf16[128,512]{1,0:T(8,128)(2,1)S(1)} %get-tuple-element.100), channel_id=1, source_target_pairs={{0,3},{1,2},{2,1},{3,0},{4,7},{5,6},{6,5},{7,4},{8,11},{9,10},{10,... | collective-permute-start | bytes 393224 | tf_op jit(solution)/shard_map/ppermute | solution.py:372
  40.9 5.2 %covar_own.2.refs_2_.refs_3_ = bf16[2048,2048]{1,0:T(8,128)(2,1)S(1)} custom-call(s32[1]{0:T(128)} %bitcast.me_ref, f32[128,8192]{1,0:T(8,128)S(1)} %distances.1.away_ref, f32[1,4096]{1,0:T(1,128)S(1)} %bitcast.7), custom_call_target="tpu_custom_call" | custom-call | flops 1 | bytes 1 | tf_op jit(solution)/shard_map/covar_own/pallas_call | solution.py:184
  46.1 2.2 %collective-permute-start.9 = (bf16[128,512]{1,0:T(8,128)(2,1)S(1)}, bf16[128,512]{1,0:T(8,128)(2,1)S(1)}, u32[]{:S(2)}, u32[]{:S(2)}) collective-permute-start(bf16[128,512]{1,0:T(8,128)(2,1)S(1)} %get-tuple-element.95), channel_id=1, source_target_pairs={{0,6},{1,7},{2,4},{3,5},{4,2},{5,3},{6,0},{7,1},{8,14},{9,15},{10,... | collective-permute-start | bytes 393224 | tf_op jit(solution)/shard_map/ppermute | solution.py:372
  48.3 1.7 %collective-permute-start.7 = (bf16[128,512]{1,0:T(8,128)(2,1)S(1)}, bf16[128,512]{1,0:T(8,128)(2,1)S(1)}, u32[]{:S(2)}, u32[]{:S(2)}) collective-permute-start(bf16[128,512]{1,0:T(8,128)(2,1)S(1)} %get-tuple-element.91), channel_id=1, source_target_pairs={{0,7},{1,6},{2,5},{3,4},{4,3},{5,2},{6,1},{7,0},{8,15},{9,14},{10,... | collective-permute-start | bytes 393224 | tf_op jit(solution)/shard_map/ppermute | solution.py:372
  50.0 5.4 %covar_own.3.refs_4_ = bf16[2048,2048]{1,0:T(8,128)(2,1)S(1)} custom-call(s32[1]{0:T(128)} %bitcast.me_ref, f32[128,8192]{1,0:T(8,128)S(1)} %distances.1.away_ref, f32[1,4096]{1,0:T(1,128)S(1)} %bitcast.8), custom_call_target="tpu_custom_call" | custom-call | flops 1 | bytes 1 | tf_op jit(solution)/shard_map/covar_own/pallas_call | solution.py:184
  56.2 2.6 %smooth_part.7.refs_4_ = f32[128,4096]{1,0:T(8,128)S(1)} custom-call(bf16[128,512]{1,0:T(8,128)(2,1)S(1)} %get-tuple-element.97.refs_0_, bf16[128,512]{1,0:T(8,128)(2,1)S(1)} %collective-permute-done.10.refs_1_, bf16[128,512]{1,0:T(8,128)(2,1)S(1)} %collective-permute-done.11.refs_2_, bf16[128,512]{1,0:T(8,128)(2,1)S(1)} %collective-permute-done.12.refs_3_, ...), custom_call_target="tpu_custom_call" | custom-call | flops 1 | bytes 1 | tf_op jit(solution)/shard_map/smooth_part/pallas_call | solution.py:303
  58.9 1.4 %smooth_part.8.refs_3_ = f32[128,4096]{1,0:T(8,128)S(1)} custom-call(bf16[128,512]{1,0:T(8,128)(2,1)S(1)} %collective-permute-done.8.refs_0_, bf16[128,512]{1,0:T(8,128)(2,1)S(1)} %collective-permute-done.9.refs_1_, bf16[2048,2048]{1,0:T(8,128)(2,1)S(1)} %get-tuple-element.92.refs_1_.refs_2_, bf16[2048,2048]{1,0:T(8,128)(2,1)S(1)} %covar_own.2.refs_2_.refs_3_, ...), custom_call_target="tpu_custom_call" | custom-call | flops 1 | bytes 1 | tf_op jit(solution)/shard_map/smooth_part/pallas_call | solution.py:303
  61.3 3.1 %collective-permute-start.14 = (bf16[128,512]{1,0:T(8,128)(2,1)S(1)}, bf16[128,512]{1,0:T(8,128)(2,1)S(1)}, u32[]{:S(2)}, u32[]{:S(2)}) collective-permute-start(bf16[128,512]{1,0:T(8,128)(2,1)S(1)} %get-tuple-element.106), channel_id=1, source_target_pairs={{0,7},{1,6},{2,5},{3,4},{4,3},{5,2},{6,1},{7,0},{8,15},{9,14},{10,... | collective-permute-start | bytes 393224 | tf_op jit(solution)/shard_map/ppermute | solution.py:372
  64.4 1.7 %collective-permute-start.15 = (bf16[128,512]{1,0:T(8,128)(2,1)S(1)}, bf16[128,512]{1,0:T(8,128)(2,1)S(1)}, u32[]{:S(2)}, u32[]{:S(2)}) collective-permute-start(bf16[128,512]{1,0:T(8,128)(2,1)S(1)} %get-tuple-element.107), channel_id=1, source_target_pairs={{0,6},{1,7},{2,4},{3,5},{4,2},{5,3},{6,0},{7,1},{8,14},{9,15},{10,... | collective-permute-start | bytes 393224 | tf_op jit(solution)/shard_map/ppermute | solution.py:372
  66.6 3.6 %collective-permute-start.18 = (bf16[128,512]{1,0:T(8,128)(2,1)S(1)}, bf16[128,512]{1,0:T(8,128)(2,1)S(1)}, u32[]{:S(2)}, u32[]{:S(2)}) collective-permute-start(bf16[128,512]{1,0:T(8,128)(2,1)S(1)} %get-tuple-element.110), channel_id=1, source_target_pairs={{0,2},{1,3},{2,0},{3,1},{4,6},{5,7},{6,4},{7,5},{8,10},{9,11},{10,... | collective-permute-start | bytes 393224 | tf_op jit(solution)/shard_map/ppermute | solution.py:372
  70.5 1.5 %collective-permute-start.19 = (bf16[128,512]{1,0:T(8,128)(2,1)S(1)}, bf16[128,512]{1,0:T(8,128)(2,1)S(1)}, u32[]{:S(2)}, u32[]{:S(2)}) collective-permute-start(bf16[128,512]{1,0:T(8,128)(2,1)S(1)} %get-tuple-element.111), channel_id=1, source_target_pairs={{0,3},{1,2},{2,1},{3,0},{4,7},{5,6},{6,5},{7,4},{8,11},{9,10},{10,... | collective-permute-start | bytes 393224 | tf_op jit(solution)/shard_map/ppermute | solution.py:372
  73.2 5.4 %collective-permute-start.20 = (bf16[128,512]{1,0:T(8,128)(2,1)S(1)}, bf16[128,512]{1,0:T(8,128)(2,1)S(1)}, u32[]{:S(2)}, u32[]{:S(2)}) collective-permute-start(bf16[128,512]{1,0:T(8,128)(2,1)S(1)} %get-tuple-element.112), channel_id=1, source_target_pairs={{0,4},{1,5},{2,6},{3,7},{4,0},{5,1},{6,2},{7,3},{8,12},{9,13},{10,... | collective-permute-start | bytes 393224 | tf_op jit(solution)/shard_map/ppermute | solution.py:372
  79.0 2.7 %collective-permute-done.20.refs_6_ = bf16[128,512]{1,0:T(8,128)(2,1)S(1)} collective-permute-done((bf16[128,512]{1,0:T(8,128)(2,1)S(1)}, bf16[128,512]{1,0:T(8,128)(2,1)S(1)}, u32[]{:S(2)}, u32[]{:S(2)}) %collective-permute-start.20) | collective-permute-done | bytes 131104 | tf_op jit(solution)/shard_map/ppermute | solution.py:372
  83.3 3.2 %collective-permute-start.27 = (bf16[128,512]{1,0:T(8,128)(2,1)S(1)}, bf16[128,512]{1,0:T(8,128)(2,1)S(1)}, u32[]{:S(2)}, u32[]{:S(2)}) collective-permute-start(bf16[128,512]{1,0:T(8,128)(2,1)S(1)} %get-tuple-element.121), channel_id=1, source_target_pairs={{0,4},{1,5},{2,6},{3,7},{4,0},{5,1},{6,2},{7,3},{8,12},{9,13},{10,... | collective-permute-start | bytes 393224 | tf_op jit(solution)/shard_map/ppermute | solution.py:372
  86.5 1.4 %collective-permute-start.22 = (bf16[128,512]{1,0:T(8,128)(2,1)S(1)}, bf16[128,512]{1,0:T(8,128)(2,1)S(1)}, u32[]{:S(2)}, u32[]{:S(2)}) collective-permute-start(bf16[128,512]{1,0:T(8,128)(2,1)S(1)} %get-tuple-element.115), channel_id=1, source_target_pairs={{0,5},{1,4},{2,7},{3,6},{4,1},{5,0},{6,3},{7,2},{8,13},{9,12},{10,... | collective-permute-start | bytes 393224 | tf_op jit(solution)/shard_map/ppermute | solution.py:372
  87.9 2.1 %collective-permute-start.25 = (bf16[128,512]{1,0:T(8,128)(2,1)S(1)}, bf16[128,512]{1,0:T(8,128)(2,1)S(1)}, u32[]{:S(2)}, u32[]{:S(2)}) collective-permute-start(bf16[128,512]{1,0:T(8,128)(2,1)S(1)} %get-tuple-element.119), channel_id=1, source_target_pairs={{0,2},{1,3},{2,0},{3,1},{4,6},{5,7},{6,4},{7,5},{8,10},{9,11},{10,... | collective-permute-start | bytes 393224 | tf_op jit(solution)/shard_map/ppermute | solution.py:372
  90.0 2.3 %collective-permute-start.23 = (bf16[128,512]{1,0:T(8,128)(2,1)S(1)}, bf16[128,512]{1,0:T(8,128)(2,1)S(1)}, u32[]{:S(2)}, u32[]{:S(2)}) collective-permute-start(bf16[128,512]{1,0:T(8,128)(2,1)S(1)} %get-tuple-element.116), channel_id=1, source_target_pairs={{0,6},{1,7},{2,4},{3,5},{4,2},{5,3},{6,0},{7,1},{8,14},{9,15},{10,... | collective-permute-start | bytes 393224 | tf_op jit(solution)/shard_map/ppermute | solution.py:372
  92.3 3.5 %collective-permute-done.27.refs_0_ = bf16[128,512]{1,0:T(8,128)(2,1)S(1)} collective-permute-done((bf16[128,512]{1,0:T(8,128)(2,1)S(1)}, bf16[128,512]{1,0:T(8,128)(2,1)S(1)}, u32[]{:S(2)}, u32[]{:S(2)}) %collective-permute-start.27) | collective-permute-done | bytes 131104 | tf_op jit(solution)/shard_map/ppermute | solution.py:372
  95.8 3.7 %collective-permute-start.21 = (bf16[128,512]{1,0:T(8,128)(2,1)S(1)}, bf16[128,512]{1,0:T(8,128)(2,1)S(1)}, u32[]{:S(2)}, u32[]{:S(2)}) collective-permute-start(bf16[128,512]{1,0:T(8,128)(2,1)S(1)} %get-tuple-element.114), channel_id=1, source_target_pairs={{0,7},{1,6},{2,5},{3,4},{4,3},{5,2},{6,1},{7,0},{8,15},{9,14},{10,... | collective-permute-start | bytes 393224 | tf_op jit(solution)/shard_map/ppermute | solution.py:372
  100.3 2.6 %smooth_part.10.refs_4_ = f32[128,4096]{1,0:T(8,128)S(1)} custom-call(bf16[128,512]{1,0:T(8,128)(2,1)S(1)} %get-tuple-element.117.refs_0_, bf16[128,512]{1,0:T(8,128)(2,1)S(1)} %collective-permute-done.24.refs_1_, bf16[128,512]{1,0:T(8,128)(2,1)S(1)} %collective-permute-done.25.refs_2_, bf16[128,512]{1,0:T(8,128)(2,1)S(1)} %collective-permute-done.26.refs_3_, ...), custom_call_target="tpu_custom_call" | custom-call | flops 1 | bytes 1 | tf_op jit(solution)/shard_map/smooth_part/pallas_call | solution.py:303
  102.9 1.4 %smooth_part.11.refs_3_ = f32[128,4096]{1,0:T(8,128)S(1)} custom-call(bf16[128,512]{1,0:T(8,128)(2,1)S(1)} %collective-permute-done.22.refs_0_, bf16[128,512]{1,0:T(8,128)(2,1)S(1)} %collective-permute-done.23.refs_1_, bf16[2048,2048]{1,0:T(8,128)(2,1)S(1)} %get-tuple-element.92.refs_1_.refs_2_, bf16[2048,2048]{1,0:T(8,128)(2,1)S(1)} %covar_own.2.refs_2_.refs_3_, ...), custom_call_target="tpu_custom_call" | custom-call | flops 1 | bytes 1 | tf_op jit(solution)/shard_map/smooth_part/pallas_call | solution.py:303
  104.3 1.8 %update.3 = f32[128,4096]{1,0:T(8,128)} custom-call(s32[1]{0:T(128)} %bitcast.me_ref, bf16[128,512]{1,0:T(8,128)(2,1)S(1)} %collective-permute-done.21.refs_0_, bf16[2048,2048]{1,0:T(8,128)(2,1)S(1)} %get-tuple-element.92.refs_1_.refs_2_, bf16[2048,2048]{1,0:T(8,128)(2,1)S(1)} %covar_own.2.refs_2_.refs_3_, f32[128,4096]{1,0:T(8,128)S(1)} %smooth_part.11.refs_3_, ...), custom_call_target="tpu_custom_call" | custom-call | flops 1 | bytes 1 | tf_op jit(solution)/shard_map/update/pallas_call | solution.py:356
  (59 shorter events, 9.7 us)
Async XLA Ops:
  1.6 10.9 %collective-permute-start = (bf16[128,512]{1,0:T(8,128)(2,1)S(1)}, bf16[128,512]{1,0:T(8,128)(2,1)S(1)}, u32[]{:S(2)}, u32[]{:S(2)}) collective-permute-start(bf16[128,512]{1,0:T(8,128)(2,1)S(1)} %get-tuple-element.64), channel_id=1, source_target_pairs={{0,6},{1,7},{2,4},{3,5},{4,2},{5,3},{6,0},{7,1},{8,14},{9,15},{10,... | collective-permute-start | bytes 393224 | tf_op jit(solution)/shard_map/ppermute | solution.py:372
  6.7 11.0 %collective-permute-start.1 = (bf16[128,512]{1,0:T(8,128)(2,1)S(1)}, bf16[128,512]{1,0:T(8,128)(2,1)S(1)}, u32[]{:S(2)}, u32[]{:S(2)}) collective-permute-start(bf16[128,512]{1,0:T(8,128)(2,1)S(1)} %get-tuple-element.65), channel_id=1, source_target_pairs={{0,7},{1,6},{2,5},{3,4},{4,3},{5,2},{6,1},{7,0},{8,15},{9,14},{10,... | collective-permute-start | bytes 393224 | tf_op jit(solution)/shard_map/ppermute | solution.py:372
  7.9 24.2 %collective-permute-start.2 = (bf16[128,512]{1,0:T(8,128)(2,1)S(1)}, bf16[128,512]{1,0:T(8,128)(2,1)S(1)}, u32[]{:S(2)}, u32[]{:S(2)}) collective-permute-start(bf16[128,512]{1,0:T(8,128)(2,1)S(1)} %get-tuple-element.66), channel_id=1, source_target_pairs={{0,1},{1,0},{2,3},{3,2},{4,5},{5,4},{6,7},{7,6},{8,9},{9,8},{10,11... | collective-permute-start | bytes 393224 | tf_op jit(solution)/shard_map/ppermute | solution.py:372
  8.3 23.9 %collective-permute-start.3 = (bf16[128,512]{1,0:T(8,128)(2,1)S(1)}, bf16[128,512]{1,0:T(8,128)(2,1)S(1)}, u32[]{:S(2)}, u32[]{:S(2)}) collective-permute-start(bf16[128,512]{1,0:T(8,128)(2,1)S(1)} %get-tuple-element.67), channel_id=1, source_target_pairs={{0,2},{1,3},{2,0},{3,1},{4,6},{5,7},{6,4},{7,5},{8,10},{9,11},{10,... | collective-permute-start | bytes 393224 | tf_op jit(solution)/shard_map/ppermute | solution.py:372
  8.3 23.9 %collective-permute-start.4 = (bf16[128,512]{1,0:T(8,128)(2,1)S(1)}, bf16[128,512]{1,0:T(8,128)(2,1)S(1)}, u32[]{:S(2)}, u32[]{:S(2)}) collective-permute-start(bf16[128,512]{1,0:T(8,128)(2,1)S(1)} %get-tuple-element.68), channel_id=1, source_target_pairs={{0,3},{1,2},{2,1},{3,0},{4,7},{5,6},{6,5},{7,4},{8,11},{9,10},{10,... | collective-permute-start | bytes 393224 | tf_op jit(solution)/shard_map/ppermute | solution.py:372
  12.1 9.7 %copy-start.6 = (f32[4096]{0:T(1024)S(1)}, f32[4096]{0:T(1024)}, u32[]{:S(2)}) copy-start(f32[4096]{0:T(1024)} %param.17) | copy-start | bytes 49156
  12.1 9.7 %copy-start.1 = (bf16[512,1024]{1,0:T(8,128)(2,1)S(1)}, bf16[512,1024]{1,0:T(8,128)(2,1)}, u32[]{:S(2)}) copy-start(bf16[512,1024]{1,0:T(8,128)(2,1)} %data_ref.3) | copy-start | bytes 3145732
  12.5 9.8 %copy-start.2 = (bf16[4,256,256]{2,1,0:T(8,128)(2,1)S(1)}, bf16[4,256,256]{2,1,0:T(8,128)(2,1)}, u32[]{:S(2)}) copy-start(bf16[4,256,256]{2,1,0:T(8,128)(2,1)} %blocks_ref.1) | copy-start | bytes 1572868
  12.5 9.8 %copy-start.3 = (s32[1024]{0:T(1024)S(1)}, s32[1024]{0:T(1024)}, u32[]{:S(2)}) copy-start(s32[1024]{0:T(1024)} %param.13) | copy-start | bytes 12292
  12.5 19.7 %collective-permute-start.5 = (bf16[128,512]{1,0:T(8,128)(2,1)S(1)}, bf16[128,512]{1,0:T(8,128)(2,1)S(1)}, u32[]{:S(2)}, u32[]{:S(2)}) collective-permute-start(bf16[128,512]{1,0:T(8,128)(2,1)S(1)} %get-tuple-element.69), channel_id=1, source_target_pairs={{0,4},{1,5},{2,6},{3,7},{4,0},{5,1},{6,2},{7,3},{8,12},{9,13},{10,... | collective-permute-start | bytes 393224 | tf_op jit(solution)/shard_map/ppermute | solution.py:372
  17.7 14.5 %collective-permute-start.6 = (bf16[128,512]{1,0:T(8,128)(2,1)S(1)}, bf16[128,512]{1,0:T(8,128)(2,1)S(1)}, u32[]{:S(2)}, u32[]{:S(2)}) collective-permute-start(bf16[128,512]{1,0:T(8,128)(2,1)S(1)} %get-tuple-element.70), channel_id=1, source_target_pairs={{0,5},{1,4},{2,7},{3,6},{4,1},{5,0},{6,3},{7,2},{8,13},{9,12},{10,... | collective-permute-start | bytes 393224 | tf_op jit(solution)/shard_map/ppermute | solution.py:372
  33.5 12.6 %collective-permute-start.10 = (bf16[128,512]{1,0:T(8,128)(2,1)S(1)}, bf16[128,512]{1,0:T(8,128)(2,1)S(1)}, u32[]{:S(2)}, u32[]{:S(2)}) collective-permute-start(bf16[128,512]{1,0:T(8,128)(2,1)S(1)} %get-tuple-element.98), channel_id=1, source_target_pairs={{0,1},{1,0},{2,3},{3,2},{4,5},{5,4},{6,7},{7,6},{8,9},{9,8},{10,11... | collective-permute-start | bytes 393224 | tf_op jit(solution)/shard_map/ppermute | solution.py:372
  35.0 13.3 %collective-permute-start.13 = (bf16[128,512]{1,0:T(8,128)(2,1)S(1)}, bf16[128,512]{1,0:T(8,128)(2,1)S(1)}, u32[]{:S(2)}, u32[]{:S(2)}) collective-permute-start(bf16[128,512]{1,0:T(8,128)(2,1)S(1)} %get-tuple-element.103), channel_id=1, source_target_pairs={{0,4},{1,5},{2,6},{3,7},{4,0},{5,1},{6,2},{7,3},{8,12},{9,13},{10,... | collective-permute-start | bytes 393224 | tf_op jit(solution)/shard_map/ppermute | solution.py:372
  35.0 23.8 %collective-permute-start.8 = (bf16[128,512]{1,0:T(8,128)(2,1)S(1)}, bf16[128,512]{1,0:T(8,128)(2,1)S(1)}, u32[]{:S(2)}, u32[]{:S(2)}) collective-permute-start(bf16[128,512]{1,0:T(8,128)(2,1)S(1)} %get-tuple-element.94), channel_id=1, source_target_pairs={{0,5},{1,4},{2,7},{3,6},{4,1},{5,0},{6,3},{7,2},{8,13},{9,12},{10,... | collective-permute-start | bytes 393224 | tf_op jit(solution)/shard_map/ppermute | solution.py:372
  37.9 18.3 %collective-permute-start.11 = (bf16[128,512]{1,0:T(8,128)(2,1)S(1)}, bf16[128,512]{1,0:T(8,128)(2,1)S(1)}, u32[]{:S(2)}, u32[]{:S(2)}) collective-permute-start(bf16[128,512]{1,0:T(8,128)(2,1)S(1)} %get-tuple-element.99), channel_id=1, source_target_pairs={{0,2},{1,3},{2,0},{3,1},{4,6},{5,7},{6,4},{7,5},{8,10},{9,11},{10,... | collective-permute-start | bytes 393224 | tf_op jit(solution)/shard_map/ppermute | solution.py:372
  37.9 18.3 %collective-permute-start.12 = (bf16[128,512]{1,0:T(8,128)(2,1)S(1)}, bf16[128,512]{1,0:T(8,128)(2,1)S(1)}, u32[]{:S(2)}, u32[]{:S(2)}) collective-permute-start(bf16[128,512]{1,0:T(8,128)(2,1)S(1)} %get-tuple-element.100), channel_id=1, source_target_pairs={{0,3},{1,2},{2,1},{3,0},{4,7},{5,6},{6,5},{7,4},{8,11},{9,10},{10,... | collective-permute-start | bytes 393224 | tf_op jit(solution)/shard_map/ppermute | solution.py:372
  46.1 12.7 %collective-permute-start.9 = (bf16[128,512]{1,0:T(8,128)(2,1)S(1)}, bf16[128,512]{1,0:T(8,128)(2,1)S(1)}, u32[]{:S(2)}, u32[]{:S(2)}) collective-permute-start(bf16[128,512]{1,0:T(8,128)(2,1)S(1)} %get-tuple-element.95), channel_id=1, source_target_pairs={{0,6},{1,7},{2,4},{3,5},{4,2},{5,3},{6,0},{7,1},{8,14},{9,15},{10,... | collective-permute-start | bytes 393224 | tf_op jit(solution)/shard_map/ppermute | solution.py:372
  48.3 11.9 %collective-permute-start.7 = (bf16[128,512]{1,0:T(8,128)(2,1)S(1)}, bf16[128,512]{1,0:T(8,128)(2,1)S(1)}, u32[]{:S(2)}, u32[]{:S(2)}) collective-permute-start(bf16[128,512]{1,0:T(8,128)(2,1)S(1)} %get-tuple-element.91), channel_id=1, source_target_pairs={{0,7},{1,6},{2,5},{3,4},{4,3},{5,2},{6,1},{7,0},{8,15},{9,14},{10,... | collective-permute-start | bytes 393224 | tf_op jit(solution)/shard_map/ppermute | solution.py:372
  61.3 9.2 %collective-permute-start.14 = (bf16[128,512]{1,0:T(8,128)(2,1)S(1)}, bf16[128,512]{1,0:T(8,128)(2,1)S(1)}, u32[]{:S(2)}, u32[]{:S(2)}) collective-permute-start(bf16[128,512]{1,0:T(8,128)(2,1)S(1)} %get-tuple-element.106), channel_id=1, source_target_pairs={{0,7},{1,6},{2,5},{3,4},{4,3},{5,2},{6,1},{7,0},{8,15},{9,14},{10,... | collective-permute-start | bytes 393224 | tf_op jit(solution)/shard_map/ppermute | solution.py:372
  64.4 8.8 %collective-permute-start.15 = (bf16[128,512]{1,0:T(8,128)(2,1)S(1)}, bf16[128,512]{1,0:T(8,128)(2,1)S(1)}, u32[]{:S(2)}, u32[]{:S(2)}) collective-permute-start(bf16[128,512]{1,0:T(8,128)(2,1)S(1)} %get-tuple-element.107), channel_id=1, source_target_pairs={{0,6},{1,7},{2,4},{3,5},{4,2},{5,3},{6,0},{7,1},{8,14},{9,15},{10,... | collective-permute-start | bytes 393224 | tf_op jit(solution)/shard_map/ppermute | solution.py:372
  66.1 12.9 %collective-permute-start.16 = (bf16[128,512]{1,0:T(8,128)(2,1)S(1)}, bf16[128,512]{1,0:T(8,128)(2,1)S(1)}, u32[]{:S(2)}, u32[]{:S(2)}) collective-permute-start(bf16[128,512]{1,0:T(8,128)(2,1)S(1)} %get-tuple-element.108), channel_id=1, source_target_pairs={{0,5},{1,4},{2,7},{3,6},{4,1},{5,0},{6,3},{7,2},{8,13},{9,12},{10,... | collective-permute-start | bytes 393224 | tf_op jit(solution)/shard_map/ppermute | solution.py:372
  66.1 12.9 %collective-permute-start.17 = (bf16[128,512]{1,0:T(8,128)(2,1)S(1)}, bf16[128,512]{1,0:T(8,128)(2,1)S(1)}, u32[]{:S(2)}, u32[]{:S(2)}) collective-permute-start(bf16[128,512]{1,0:T(8,128)(2,1)S(1)} %get-tuple-element.109), channel_id=1, source_target_pairs={{0,1},{1,0},{2,3},{3,2},{4,5},{5,4},{6,7},{7,6},{8,9},{9,8},{10,11... | collective-permute-start | bytes 393224 | tf_op jit(solution)/shard_map/ppermute | solution.py:372
  66.6 12.4 %collective-permute-start.18 = (bf16[128,512]{1,0:T(8,128)(2,1)S(1)}, bf16[128,512]{1,0:T(8,128)(2,1)S(1)}, u32[]{:S(2)}, u32[]{:S(2)}) collective-permute-start(bf16[128,512]{1,0:T(8,128)(2,1)S(1)} %get-tuple-element.110), channel_id=1, source_target_pairs={{0,2},{1,3},{2,0},{3,1},{4,6},{5,7},{6,4},{7,5},{8,10},{9,11},{10,... | collective-permute-start | bytes 393224 | tf_op jit(solution)/shard_map/ppermute | solution.py:372
  70.5 8.5 %collective-permute-start.19 = (bf16[128,512]{1,0:T(8,128)(2,1)S(1)}, bf16[128,512]{1,0:T(8,128)(2,1)S(1)}, u32[]{:S(2)}, u32[]{:S(2)}) collective-permute-start(bf16[128,512]{1,0:T(8,128)(2,1)S(1)} %get-tuple-element.111), channel_id=1, source_target_pairs={{0,3},{1,2},{2,1},{3,0},{4,7},{5,6},{6,5},{7,4},{8,11},{9,10},{10,... | collective-permute-start | bytes 393224 | tf_op jit(solution)/shard_map/ppermute | solution.py:372
  73.2 8.5 %collective-permute-start.20 = (bf16[128,512]{1,0:T(8,128)(2,1)S(1)}, bf16[128,512]{1,0:T(8,128)(2,1)S(1)}, u32[]{:S(2)}, u32[]{:S(2)}) collective-permute-start(bf16[128,512]{1,0:T(8,128)(2,1)S(1)} %get-tuple-element.112), channel_id=1, source_target_pairs={{0,4},{1,5},{2,6},{3,7},{4,0},{5,1},{6,2},{7,3},{8,12},{9,13},{10,... | collective-permute-start | bytes 393224 | tf_op jit(solution)/shard_map/ppermute | solution.py:372
  83.0 7.1 %collective-permute-start.24 = (bf16[128,512]{1,0:T(8,128)(2,1)S(1)}, bf16[128,512]{1,0:T(8,128)(2,1)S(1)}, u32[]{:S(2)}, u32[]{:S(2)}) collective-permute-start(bf16[128,512]{1,0:T(8,128)(2,1)S(1)} %get-tuple-element.118), channel_id=1, source_target_pairs={{0,1},{1,0},{2,3},{3,2},{4,5},{5,4},{6,7},{7,6},{8,9},{9,8},{10,11... | collective-permute-start | bytes 393224 | tf_op jit(solution)/shard_map/ppermute | solution.py:372
  83.3 12.5 %collective-permute-start.27 = (bf16[128,512]{1,0:T(8,128)(2,1)S(1)}, bf16[128,512]{1,0:T(8,128)(2,1)S(1)}, u32[]{:S(2)}, u32[]{:S(2)}) collective-permute-start(bf16[128,512]{1,0:T(8,128)(2,1)S(1)} %get-tuple-element.121), channel_id=1, source_target_pairs={{0,4},{1,5},{2,6},{3,7},{4,0},{5,1},{6,2},{7,3},{8,12},{9,13},{10,... | collective-permute-start | bytes 393224 | tf_op jit(solution)/shard_map/ppermute | solution.py:372
  86.5 16.4 %collective-permute-start.22 = (bf16[128,512]{1,0:T(8,128)(2,1)S(1)}, bf16[128,512]{1,0:T(8,128)(2,1)S(1)}, u32[]{:S(2)}, u32[]{:S(2)}) collective-permute-start(bf16[128,512]{1,0:T(8,128)(2,1)S(1)} %get-tuple-element.115), channel_id=1, source_target_pairs={{0,5},{1,4},{2,7},{3,6},{4,1},{5,0},{6,3},{7,2},{8,13},{9,12},{10,... | collective-permute-start | bytes 393224 | tf_op jit(solution)/shard_map/ppermute | solution.py:372
  87.9 12.4 %collective-permute-start.25 = (bf16[128,512]{1,0:T(8,128)(2,1)S(1)}, bf16[128,512]{1,0:T(8,128)(2,1)S(1)}, u32[]{:S(2)}, u32[]{:S(2)}) collective-permute-start(bf16[128,512]{1,0:T(8,128)(2,1)S(1)} %get-tuple-element.119), channel_id=1, source_target_pairs={{0,2},{1,3},{2,0},{3,1},{4,6},{5,7},{6,4},{7,5},{8,10},{9,11},{10,... | collective-permute-start | bytes 393224 | tf_op jit(solution)/shard_map/ppermute | solution.py:372
  90.0 10.3 %collective-permute-start.26 = (bf16[128,512]{1,0:T(8,128)(2,1)S(1)}, bf16[128,512]{1,0:T(8,128)(2,1)S(1)}, u32[]{:S(2)}, u32[]{:S(2)}) collective-permute-start(bf16[128,512]{1,0:T(8,128)(2,1)S(1)} %get-tuple-element.120), channel_id=1, source_target_pairs={{0,3},{1,2},{2,1},{3,0},{4,7},{5,6},{6,5},{7,4},{8,11},{9,10},{10,... | collective-permute-start | bytes 393224 | tf_op jit(solution)/shard_map/ppermute | solution.py:372
  90.0 12.9 %collective-permute-start.23 = (bf16[128,512]{1,0:T(8,128)(2,1)S(1)}, bf16[128,512]{1,0:T(8,128)(2,1)S(1)}, u32[]{:S(2)}, u32[]{:S(2)}) collective-permute-start(bf16[128,512]{1,0:T(8,128)(2,1)S(1)} %get-tuple-element.116), channel_id=1, source_target_pairs={{0,6},{1,7},{2,4},{3,5},{4,2},{5,3},{6,0},{7,1},{8,14},{9,15},{10,... | collective-permute-start | bytes 393224 | tf_op jit(solution)/shard_map/ppermute | solution.py:372
  95.8 8.5 %collective-permute-start.21 = (bf16[128,512]{1,0:T(8,128)(2,1)S(1)}, bf16[128,512]{1,0:T(8,128)(2,1)S(1)}, u32[]{:S(2)}, u32[]{:S(2)}) collective-permute-start(bf16[128,512]{1,0:T(8,128)(2,1)S(1)} %get-tuple-element.114), channel_id=1, source_target_pairs={{0,7},{1,6},{2,5},{3,4},{4,3},{5,2},{6,1},{7,0},{8,15},{9,14},{10,... | collective-permute-start | bytes 393224 | tf_op jit(solution)/shard_map/ppermute | solution.py:372
  (4 other events, 16.4 us)

commit v6 on v5

--- a/solution.py
+++ b/solution.py
@@ -107,9 +107,12 @@
             hot = jnp.where(down == names, 1.0, 0.0).astype(BF16)
             left_ref[:, span] = dot(hot, blocks_ref[b]).astype(BF16)
             hot_ref[span, :] = jnp.where(along == column(names), 1.0, 0.0).astype(BF16)
-        for r in range(0, ndev, 2):
-            rows = pl.ds(r * chd, 2 * chd)
-            out_ref[rows, :] = dot(left_ref[rows, :], hot_ref[...]).astype(BF16)
+        for r in range(0, chans, width):
+            rows, rest = pl.ds(r, width), pl.ds(r, chans - r)
+            tile = dot(left_ref[rows, :], hot_ref[:, rest]).astype(BF16)
+            out_ref[rows, rest] = tile
+            for c in range(r + width, chans, width):
+                out_ref[pl.ds(c, width), rows] = tile[:, c - r : c - r + width].T
 
     return pl.pallas_call(
         body,
@@ -125,10 +128,11 @@
 
 def distances(total):
     def body(out_ref):
+        row = lax.broadcasted_iota(jnp.int32, (128, 128), 0)
+        away = (row - lax.broadcasted_iota(jnp.int32, (128, 128), 1)).astype(F32)
+        back = -away
         for c in range(0, 2 * total, 128):
-            row = lax.broadcasted_iota(jnp.int32, (128, 128), 0)
-            away = (row - lax.broadcasted_iota(jnp.int32, (128, 128), 1) + (total - c)).astype(F32)
-            out_ref[:, pl.ds(c, 128)] = -away * away
+            out_ref[:, pl.ds(c, 128)] = (away + float(total - c)) * (back - float(total - c))
 
     return pl.pallas_call(
         body,
@@ -412,7 +416,6 @@
     current = [kept_near, kept_far]
     current, packed = update(me, got, latest, rows, total, current, factors, low, high, False)
 
-    order = [*far[:0:-1], *near[1:], far[0]]
     got = swap(normal(weights, swap(packed), resp, stud, order))
     total = None
     for group in groups:

time: 106 us -> 112 us (1.057)
  waiting for transfers between devices: 8.06 us -> 17.5 us
  starting transfers between devices: 59.2 us -> 56.4 us
    ppermute x28, waiting for transfers between devices: 8.06 us -> 17.5 us  [swap(): lax.ppermute(pieces[r], 'wide', [(i, i ^ r) for i in range(ndev)])]
    ppermute x28, starting transfers between devices: 59.2 us -> 56.4 us  [swap(): lax.ppermute(pieces[r], 'wide', [(i, i ^ r) for i in range(ndev)])]
  transfers between devices with their start and end apart: 28 -> 28, of which waited for: 5 -> 6; matrix products, arithmetic and copies ran while one was open for 0% -> 0% of each run, Pallas kernels for 30% -> 27%
where the time goes in v6:
time: 112 us
  starting transfers between devices  56.4 us (50%)
  Pallas kernels  37.5 us (33%)
  waiting for transfers between devices  17.5 us (16%)
    ppermute x28, starting transfers between devices, swap(): lax.ppermute(pieces[r], 'wide', [(i, i ^ r) for i in range(ndev)])  56.4 us
    ppermute x28, waiting for transfers between devices, swap(): lax.ppermute(pieces[r], 'wide', [(i, i ^ r) for i in range(ndev)])  17.5 us
    pallas_call x2, Pallas kernels, covar_own(): pl.pallas_call(body, out_shape=pltpu.VMEM((count, count), BF16), in_specs...  10.6 us
    pallas_call x6, Pallas kernels, partial(): pl.pallas_call(body, out_shape=pltpu.VMEM((chd, blocks * span), F32), in_...  9.5 us
    pallas_call x1, Pallas kernels, covar_cross(): pl.pallas_call(body, out_shape=[pltpu.VMEM(shape, BF16), pltpu.VMEM(shape...  6.94 us
    pallas_call x2, Pallas kernels, update(): pl.pallas_call(body, out_shape=shapes, in_specs=[SMEM] + [VMEM] * (len(ar...  2.8 us
    pallas_call x2, Pallas kernels, normal(): pl.pallas_call(body, out_shape=[jax.ShapeDtypeStruct((chd, epd), BF16)] *...  2.55 us
  transfers between devices with their start and end apart: 28, of which 6 were waited for; matrix products, arithmetic and copies ran while one was open for 0% of the time, Pallas kernels for 27%

profile of v6, /device:TPU:0, one launch (start us, length us, event | category | flops | bytes accessed | tf_op | source)
XLA Modules:
  0.0 112.0 jit_solution(5917923366940429427)
XLA Ops:
  0.0 1.6 %pack_gains.1 = (bf16[128,512]{1,0:T(8,128)(2,1)S(1)}, bf16[128,512]{1,0:T(8,128)(2,1)S(1)}, bf16[128,512]{1,0:T(8,128)(2,1)S(1)}, bf16[128,512]{1,0:T(8,128)(2,...) custom-call(s32[1]{0:T(128)} %bitcast.me_ref, ...), custom_call_target="tpu_custom_call" | custom-call | flops 1 | bytes 1 | tf_op jit(solution)/shard_map/pack_gains/pallas_call | solution.py:55
  1.6 5.1 %collective-permute-start = (bf16[128,512]{1,0:T(8,128)(2,1)S(1)}, bf16[128,512]{1,0:T(8,128)(2,1)S(1)}, u32[]{:S(2)}, u32[]{:S(2)}) collective-permute-start(bf16[128,512]{1,0:T(8,128)(2,1)S(1)} %get-tuple-element.64), channel_id=1, source_target_pairs={{0,6},{1,7},{2,4},{3,5},{4,2},{5,3},{6,0},{7,1},{8,14},{9,15},{10,... | collective-permute-start | bytes 393224 | tf_op jit(solution)/shard_map/ppermute | solution.py:376
  8.3 3.1 %collective-permute-start.4 = (bf16[128,512]{1,0:T(8,128)(2,1)S(1)}, bf16[128,512]{1,0:T(8,128)(2,1)S(1)}, u32[]{:S(2)}, u32[]{:S(2)}) collective-permute-start(bf16[128,512]{1,0:T(8,128)(2,1)S(1)} %get-tuple-element.68), channel_id=1, source_target_pairs={{0,3},{1,2},{2,1},{3,0},{4,7},{5,6},{6,5},{7,4},{8,11},{9,10},{10,... | collective-permute-start | bytes 393224 | tf_op jit(solution)/shard_map/ppermute | solution.py:376
  12.4 5.3 %collective-permute-start.5 = (bf16[128,512]{1,0:T(8,128)(2,1)S(1)}, bf16[128,512]{1,0:T(8,128)(2,1)S(1)}, u32[]{:S(2)}, u32[]{:S(2)}) collective-permute-start(bf16[128,512]{1,0:T(8,128)(2,1)S(1)} %get-tuple-element.69), channel_id=1, source_target_pairs={{0,4},{1,5},{2,6},{3,7},{4,0},{5,1},{6,2},{7,3},{8,12},{9,13},{10,... | collective-permute-start | bytes 393224 | tf_op jit(solution)/shard_map/ppermute | solution.py:376
  17.7 4.1 %collective-permute-start.6 = (bf16[128,512]{1,0:T(8,128)(2,1)S(1)}, bf16[128,512]{1,0:T(8,128)(2,1)S(1)}, u32[]{:S(2)}, u32[]{:S(2)}) collective-permute-start(bf16[128,512]{1,0:T(8,128)(2,1)S(1)} %get-tuple-element.70), channel_id=1, source_target_pairs={{0,5},{1,4},{2,7},{3,6},{4,1},{5,0},{6,3},{7,2},{8,13},{9,12},{10,... | collective-permute-start | bytes 393224 | tf_op jit(solution)/shard_map/ppermute | solution.py:376
  22.2 2.2 %dense_blocks.1.refs_8_ = bf16[1024,1024]{1,0:T(8,128)(2,1)S(1)} custom-call(s32[1]{0:T(128)} %bitcast.me_ref, bf16[4,256,256]{2,1,0:T(8,128)(2,1)S(1)} %copy-done.2, s32[1,1024]{1,0:T(1,128)S(1)} %bitcast.12), custom_call_target="tpu_custom_call" | custom-call | flops 1 | bytes 1 | tf_op jit(solution)/shard_map/dense_blocks/pallas_call | solution.py:117
  24.4 6.9 %covar_cross.1 = (bf16[2048,2048]{1,0:T(8,128)(2,1)S(1)}, bf16[2048,2048]{1,0:T(8,128)(2,1)S(1)}) custom-call(s32[1]{0:T(128)} %bitcast.me_ref, f32[128,8192]{1,0:T(8,128)S(1)} %distances.1.away_ref, f32[1,4096]{1,0:T(1,128)S(1)} %bitcast.6), custom_call_target="tpu_custom_call" | custom-call | flops 1 | bytes 1 | tf_op jit(solution)/shard_map/covar_cross/pallas_call | solution.py:218
  31.4 1.3 %normal_step.2 = (bf16[128,512]{1,0:T(8,128)(2,1)S(1)}, bf16[128,512]{1,0:T(8,128)(2,1)S(1)}, bf16[128,512]{1,0:T(8,128)(2,1)S(1)}, bf16[128,512]{1,0:T(8,128)(2...) custom-call(bf16[128,512]{1,0:T(8,128)(2,1)S(1)} %collective-permute, ...), custom_call_target="tpu_custom_call" | custom-call | flops 1 | bytes 1 | tf_op jit(solution)/shard_map/normal_step/pallas_call | solution.py:245
  32.7 1.6 %collective-permute-start.10 = (bf16[128,512]{1,0:T(8,128)(2,1)S(1)}, bf16[128,512]{1,0:T(8,128)(2,1)S(1)}, u32[]{:S(2)}, u32[]{:S(2)}) collective-permute-start(bf16[128,512]{1,0:T(8,128)(2,1)S(1)} %get-tuple-element.98), channel_id=1, source_target_pairs={{0,1},{1,0},{2,3},{3,2},{4,5},{5,4},{6,7},{7,6},{8,9},{9,8},{10,11... | collective-permute-start | bytes 393224 | tf_op jit(solution)/shard_map/ppermute | solution.py:376
  34.3 2.9 %collective-permute-start.8 = (bf16[128,512]{1,0:T(8,128)(2,1)S(1)}, bf16[128,512]{1,0:T(8,128)(2,1)S(1)}, u32[]{:S(2)}, u32[]{:S(2)}) collective-permute-start(bf16[128,512]{1,0:T(8,128)(2,1)S(1)} %get-tuple-element.94), channel_id=1, source_target_pairs={{0,5},{1,4},{2,7},{3,6},{4,1},{5,0},{6,3},{7,2},{8,13},{9,12},{10,... | collective-permute-start | bytes 393224 | tf_op jit(solution)/shard_map/ppermute | solution.py:376
  37.2 2.9 %collective-permute-start.12 = (bf16[128,512]{1,0:T(8,128)(2,1)S(1)}, bf16[128,512]{1,0:T(8,128)(2,1)S(1)}, u32[]{:S(2)}, u32[]{:S(2)}) collective-permute-start(bf16[128,512]{1,0:T(8,128)(2,1)S(1)} %get-tuple-element.100), channel_id=1, source_target_pairs={{0,3},{1,2},{2,1},{3,0},{4,7},{5,6},{6,5},{7,4},{8,11},{9,10},{10,... | collective-permute-start | bytes 393224 | tf_op jit(solution)/shard_map/ppermute | solution.py:376
  40.1 5.2 %covar_own.2.refs_2_.refs_3_ = bf16[2048,2048]{1,0:T(8,128)(2,1)S(1)} custom-call(s32[1]{0:T(128)} %bitcast.me_ref, f32[128,8192]{1,0:T(8,128)S(1)} %distances.1.away_ref, f32[1,4096]{1,0:T(1,128)S(1)} %bitcast.7), custom_call_target="tpu_custom_call" | custom-call | flops 1 | bytes 1 | tf_op jit(solution)/shard_map/covar_own/pallas_call | solution.py:188
  45.4 2.2 %collective-permute-start.9 = (bf16[128,512]{1,0:T(8,128)(2,1)S(1)}, bf16[128,512]{1,0:T(8,128)(2,1)S(1)}, u32[]{:S(2)}, u32[]{:S(2)}) collective-permute-start(bf16[128,512]{1,0:T(8,128)(2,1)S(1)} %get-tuple-element.95), channel_id=1, source_target_pairs={{0,6},{1,7},{2,4},{3,5},{4,2},{5,3},{6,0},{7,1},{8,14},{9,15},{10,... | collective-permute-start | bytes 393224 | tf_op jit(solution)/shard_map/ppermute | solution.py:376
  47.5 1.7 %collective-permute-start.7 = (bf16[128,512]{1,0:T(8,128)(2,1)S(1)}, bf16[128,512]{1,0:T(8,128)(2,1)S(1)}, u32[]{:S(2)}, u32[]{:S(2)}) collective-permute-start(bf16[128,512]{1,0:T(8,128)(2,1)S(1)} %get-tuple-element.91), channel_id=1, source_target_pairs={{0,7},{1,6},{2,5},{3,4},{4,3},{5,2},{6,1},{7,0},{8,15},{9,14},{10,... | collective-permute-start | bytes 393224 | tf_op jit(solution)/shard_map/ppermute | solution.py:376
  49.2 5.4 %covar_own.3.refs_4_ = bf16[2048,2048]{1,0:T(8,128)(2,1)S(1)} custom-call(s32[1]{0:T(128)} %bitcast.me_ref, f32[128,8192]{1,0:T(8,128)S(1)} %distances.1.away_ref, f32[1,4096]{1,0:T(1,128)S(1)} %bitcast.8), custom_call_target="tpu_custom_call" | custom-call | flops 1 | bytes 1 | tf_op jit(solution)/shard_map/covar_own/pallas_call | solution.py:188
  55.4 2.6 %smooth_part.7.refs_4_ = f32[128,4096]{1,0:T(8,128)S(1)} custom-call(bf16[128,512]{1,0:T(8,128)(2,1)S(1)} %get-tuple-element.97.refs_0_, bf16[128,512]{1,0:T(8,128)(2,1)S(1)} %collective-permute-done.10.refs_1_, bf16[128,512]{1,0:T(8,128)(2,1)S(1)} %collective-permute-done.11.refs_2_, bf16[128,512]{1,0:T(8,128)(2,1)S(1)} %collective-permute-done.12.refs_3_, ...), custom_call_target="tpu_custom_call" | custom-call | flops 1 | bytes 1 | tf_op jit(solution)/shard_map/smooth_part/pallas_call | solution.py:307
  58.1 1.4 %smooth_part.8.refs_3_ = f32[128,4096]{1,0:T(8,128)S(1)} custom-call(bf16[128,512]{1,0:T(8,128)(2,1)S(1)} %collective-permute-done.8.refs_0_, bf16[128,512]{1,0:T(8,128)(2,1)S(1)} %collective-permute-done.9.refs_1_, bf16[2048,2048]{1,0:T(8,128)(2,1)S(1)} %get-tuple-element.92.refs_1_.refs_2_, bf16[2048,2048]{1,0:T(8,128)(2,1)S(1)} %covar_own.2.refs_2_.refs_3_, ...), custom_call_target="tpu_custom_call" | custom-call | flops 1 | bytes 1 | tf_op jit(solution)/shard_map/smooth_part/pallas_call | solution.py:307
  60.5 1.7 %collective-permute-start.14 = (bf16[128,512]{1,0:T(8,128)(2,1)S(1)}, bf16[128,512]{1,0:T(8,128)(2,1)S(1)}, u32[]{:S(2)}, u32[]{:S(2)}) collective-permute-start(bf16[128,512]{1,0:T(8,128)(2,1)S(1)} %get-tuple-element.106), channel_id=1, source_target_pairs={{0,6},{1,7},{2,4},{3,5},{4,2},{5,3},{6,0},{7,1},{8,14},{9,15},{10,... | collective-permute-start | bytes 393224 | tf_op jit(solution)/shard_map/ppermute | solution.py:376
  62.2 3.1 %collective-permute-start.15 = (bf16[128,512]{1,0:T(8,128)(2,1)S(1)}, bf16[128,512]{1,0:T(8,128)(2,1)S(1)}, u32[]{:S(2)}, u32[]{:S(2)}) collective-permute-start(bf16[128,512]{1,0:T(8,128)(2,1)S(1)} %get-tuple-element.107), channel_id=1, source_target_pairs={{0,7},{1,6},{2,5},{3,4},{4,3},{5,2},{6,1},{7,0},{8,15},{9,14},{10,... | collective-permute-start | bytes 393224 | tf_op jit(solution)/shard_map/ppermute | solution.py:376
  65.9 2.9 %collective-permute-start.18 = (bf16[128,512]{1,0:T(8,128)(2,1)S(1)}, bf16[128,512]{1,0:T(8,128)(2,1)S(1)}, u32[]{:S(2)}, u32[]{:S(2)}) collective-permute-start(bf16[128,512]{1,0:T(8,128)(2,1)S(1)} %get-tuple-element.110), channel_id=1, source_target_pairs={{0,3},{1,2},{2,1},{3,0},{4,7},{5,6},{6,5},{7,4},{8,11},{9,10},{10,... | collective-permute-start | bytes 393224 | tf_op jit(solution)/shard_map/ppermute | solution.py:376
  69.5 3.1 %collective-permute-done.15.refs_1_ = bf16[128,512]{1,0:T(8,128)(2,1)S(1)} collective-permute-done((bf16[128,512]{1,0:T(8,128)(2,1)S(1)}, bf16[128,512]{1,0:T(8,128)(2,1)S(1)}, u32[]{:S(2)}, u32[]{:S(2)}) %collective-permute-start.15) | collective-permute-done | bytes 131104 | tf_op jit(solution)/shard_map/ppermute | solution.py:376
  72.6 4.5 %collective-permute-start.20 = (bf16[128,512]{1,0:T(8,128)(2,1)S(1)}, bf16[128,512]{1,0:T(8,128)(2,1)S(1)}, u32[]{:S(2)}, u32[]{:S(2)}) collective-permute-start(bf16[128,512]{1,0:T(8,128)(2,1)S(1)} %get-tuple-element.112), channel_id=1, source_target_pairs={{0,5},{1,4},{2,7},{3,6},{4,1},{5,0},{6,3},{7,2},{8,13},{9,12},{10,... | collective-permute-start | bytes 393224 | tf_op jit(solution)/shard_map/ppermute | solution.py:376
  77.1 3.4 %collective-permute-done.19.refs_5_ = bf16[128,512]{1,0:T(8,128)(2,1)S(1)} collective-permute-done((bf16[128,512]{1,0:T(8,128)(2,1)S(1)}, bf16[128,512]{1,0:T(8,128)(2,1)S(1)}, u32[]{:S(2)}, u32[]{:S(2)}) %collective-permute-start.19) | collective-permute-done | bytes 131104 | tf_op jit(solution)/shard_map/ppermute | solution.py:376
  81.9 3.3 %collective-permute-start.24 = (bf16[128,512]{1,0:T(8,128)(2,1)S(1)}, bf16[128,512]{1,0:T(8,128)(2,1)S(1)}, u32[]{:S(2)}, u32[]{:S(2)}) collective-permute-start(bf16[128,512]{1,0:T(8,128)(2,1)S(1)} %get-tuple-element.118), channel_id=1, source_target_pairs={{0,1},{1,0},{2,3},{3,2},{4,5},{5,4},{6,7},{7,6},{8,9},{9,8},{10,11... | collective-permute-start | bytes 393224 | tf_op jit(solution)/shard_map/ppermute | solution.py:376
  85.7 1.9 %collective-permute-start.22 = (bf16[128,512]{1,0:T(8,128)(2,1)S(1)}, bf16[128,512]{1,0:T(8,128)(2,1)S(1)}, u32[]{:S(2)}, u32[]{:S(2)}) collective-permute-start(bf16[128,512]{1,0:T(8,128)(2,1)S(1)} %get-tuple-element.115), channel_id=1, source_target_pairs={{0,5},{1,4},{2,7},{3,6},{4,1},{5,0},{6,3},{7,2},{8,13},{9,12},{10,... | collective-permute-start | bytes 393224 | tf_op jit(solution)/shard_map/ppermute | solution.py:376
  88.7 2.4 %collective-permute-start.26 = (bf16[128,512]{1,0:T(8,128)(2,1)S(1)}, bf16[128,512]{1,0:T(8,128)(2,1)S(1)}, u32[]{:S(2)}, u32[]{:S(2)}) collective-permute-start(bf16[128,512]{1,0:T(8,128)(2,1)S(1)} %get-tuple-element.120), channel_id=1, source_target_pairs={{0,3},{1,2},{2,1},{3,0},{4,7},{5,6},{6,5},{7,4},{8,11},{9,10},{10,... | collective-permute-start | bytes 393224 | tf_op jit(solution)/shard_map/ppermute | solution.py:376
  92.2 3.4 %collective-permute-done.27.refs_0_ = bf16[128,512]{1,0:T(8,128)(2,1)S(1)} collective-permute-done((bf16[128,512]{1,0:T(8,128)(2,1)S(1)}, bf16[128,512]{1,0:T(8,128)(2,1)S(1)}, u32[]{:S(2)}, u32[]{:S(2)}) %collective-permute-start.27) | collective-permute-done | bytes 131104 | tf_op jit(solution)/shard_map/ppermute | solution.py:376
  95.6 2.3 %collective-permute-start.21 = (bf16[128,512]{1,0:T(8,128)(2,1)S(1)}, bf16[128,512]{1,0:T(8,128)(2,1)S(1)}, u32[]{:S(2)}, u32[]{:S(2)}) collective-permute-start(bf16[128,512]{1,0:T(8,128)(2,1)S(1)} %get-tuple-element.114), channel_id=1, source_target_pairs={{0,7},{1,6},{2,5},{3,4},{4,3},{5,2},{6,1},{7,0},{8,15},{9,14},{10,... | collective-permute-start | bytes 393224 | tf_op jit(solution)/shard_map/ppermute | solution.py:376
  99.7 6.3 %collective-permute-done.26.refs_3_ = bf16[128,512]{1,0:T(8,128)(2,1)S(1)} collective-permute-done((bf16[128,512]{1,0:T(8,128)(2,1)S(1)}, bf16[128,512]{1,0:T(8,128)(2,1)S(1)}, u32[]{:S(2)}, u32[]{:S(2)}) %collective-permute-start.26) | collective-permute-done | bytes 131104 | tf_op jit(solution)/shard_map/ppermute | solution.py:376
  106.0 2.6 %smooth_part.10.refs_4_ = f32[128,4096]{1,0:T(8,128)S(1)} custom-call(bf16[128,512]{1,0:T(8,128)(2,1)S(1)} %get-tuple-element.117.refs_0_, bf16[128,512]{1,0:T(8,128)(2,1)S(1)} %collective-permute-done.24.refs_1_, bf16[128,512]{1,0:T(8,128)(2,1)S(1)} %collective-permute-done.25.refs_2_, bf16[128,512]{1,0:T(8,128)(2,1)S(1)} %collective-permute-done.26.refs_3_, ...), custom_call_target="tpu_custom_call" | custom-call | flops 1 | bytes 1 | tf_op jit(solution)/shard_map/smooth_part/pallas_call | solution.py:307
  108.7 1.4 %smooth_part.11.refs_3_ = f32[128,4096]{1,0:T(8,128)S(1)} custom-call(bf16[128,512]{1,0:T(8,128)(2,1)S(1)} %collective-permute-done.22.refs_0_, bf16[128,512]{1,0:T(8,128)(2,1)S(1)} %collective-permute-done.23.refs_1_, bf16[2048,2048]{1,0:T(8,128)(2,1)S(1)} %get-tuple-element.92.refs_1_.refs_2_, bf16[2048,2048]{1,0:T(8,128)(2,1)S(1)} %covar_own.2.refs_2_.refs_3_, ...), custom_call_target="tpu_custom_call" | custom-call | flops 1 | bytes 1 | tf_op jit(solution)/shard_map/smooth_part/pallas_call | solution.py:307
  110.1 1.8 %update.3 = f32[128,4096]{1,0:T(8,128)} custom-call(s32[1]{0:T(128)} %bitcast.me_ref, bf16[128,512]{1,0:T(8,128)(2,1)S(1)} %collective-permute-done.21.refs_0_, bf16[2048,2048]{1,0:T(8,128)(2,1)S(1)} %get-tuple-element.92.refs_1_.refs_2_, bf16[2048,2048]{1,0:T(8,128)(2,1)S(1)} %covar_own.2.refs_2_.refs_3_, f32[128,4096]{1,0:T(8,128)S(1)} %smooth_part.11.refs_3_, ...), custom_call_target="tpu_custom_call" | custom-call | flops 1 | bytes 1 | tf_op jit(solution)/shard_map/update/pallas_call | solution.py:360
  (59 shorter events, 11.8 us)
Async XLA Ops:
  1.6 10.8 %collective-permute-start = (bf16[128,512]{1,0:T(8,128)(2,1)S(1)}, bf16[128,512]{1,0:T(8,128)(2,1)S(1)}, u32[]{:S(2)}, u32[]{:S(2)}) collective-permute-start(bf16[128,512]{1,0:T(8,128)(2,1)S(1)} %get-tuple-element.64), channel_id=1, source_target_pairs={{0,6},{1,7},{2,4},{3,5},{4,2},{5,3},{6,0},{7,1},{8,14},{9,15},{10,... | collective-permute-start | bytes 393224 | tf_op jit(solution)/shard_map/ppermute | solution.py:376
  6.7 11.0 %collective-permute-start.1 = (bf16[128,512]{1,0:T(8,128)(2,1)S(1)}, bf16[128,512]{1,0:T(8,128)(2,1)S(1)}, u32[]{:S(2)}, u32[]{:S(2)}) collective-permute-start(bf16[128,512]{1,0:T(8,128)(2,1)S(1)} %get-tuple-element.65), channel_id=1, source_target_pairs={{0,7},{1,6},{2,5},{3,4},{4,3},{5,2},{6,1},{7,0},{8,15},{9,14},{10,... | collective-permute-start | bytes 393224 | tf_op jit(solution)/shard_map/ppermute | solution.py:376
  7.9 23.5 %collective-permute-start.2 = (bf16[128,512]{1,0:T(8,128)(2,1)S(1)}, bf16[128,512]{1,0:T(8,128)(2,1)S(1)}, u32[]{:S(2)}, u32[]{:S(2)}) collective-permute-start(bf16[128,512]{1,0:T(8,128)(2,1)S(1)} %get-tuple-element.66), channel_id=1, source_target_pairs={{0,1},{1,0},{2,3},{3,2},{4,5},{5,4},{6,7},{7,6},{8,9},{9,8},{10,11... | collective-permute-start | bytes 393224 | tf_op jit(solution)/shard_map/ppermute | solution.py:376
  8.3 23.1 %collective-permute-start.3 = (bf16[128,512]{1,0:T(8,128)(2,1)S(1)}, bf16[128,512]{1,0:T(8,128)(2,1)S(1)}, u32[]{:S(2)}, u32[]{:S(2)}) collective-permute-start(bf16[128,512]{1,0:T(8,128)(2,1)S(1)} %get-tuple-element.67), channel_id=1, source_target_pairs={{0,2},{1,3},{2,0},{3,1},{4,6},{5,7},{6,4},{7,5},{8,10},{9,11},{10,... | collective-permute-start | bytes 393224 | tf_op jit(solution)/shard_map/ppermute | solution.py:376
  8.3 23.1 %collective-permute-start.4 = (bf16[128,512]{1,0:T(8,128)(2,1)S(1)}, bf16[128,512]{1,0:T(8,128)(2,1)S(1)}, u32[]{:S(2)}, u32[]{:S(2)}) collective-permute-start(bf16[128,512]{1,0:T(8,128)(2,1)S(1)} %get-tuple-element.68), channel_id=1, source_target_pairs={{0,3},{1,2},{2,1},{3,0},{4,7},{5,6},{6,5},{7,4},{8,11},{9,10},{10,... | collective-permute-start | bytes 393224 | tf_op jit(solution)/shard_map/ppermute | solution.py:376
  11.9 9.8 %copy-start.6 = (f32[4096]{0:T(1024)S(1)}, f32[4096]{0:T(1024)}, u32[]{:S(2)}) copy-start(f32[4096]{0:T(1024)} %param.17) | copy-start | bytes 49156
  12.0 9.8 %copy-start.1 = (bf16[512,1024]{1,0:T(8,128)(2,1)S(1)}, bf16[512,1024]{1,0:T(8,128)(2,1)}, u32[]{:S(2)}) copy-start(bf16[512,1024]{1,0:T(8,128)(2,1)} %data_ref.3) | copy-start | bytes 3145732
  12.3 9.9 %copy-start.2 = (bf16[4,256,256]{2,1,0:T(8,128)(2,1)S(1)}, bf16[4,256,256]{2,1,0:T(8,128)(2,1)}, u32[]{:S(2)}) copy-start(bf16[4,256,256]{2,1,0:T(8,128)(2,1)} %blocks_ref.1) | copy-start | bytes 1572868
  12.3 9.9 %copy-start.3 = (s32[1024]{0:T(1024)S(1)}, s32[1024]{0:T(1024)}, u32[]{:S(2)}) copy-start(s32[1024]{0:T(1024)} %param.13) | copy-start | bytes 12292
  12.4 19.0 %collective-permute-start.5 = (bf16[128,512]{1,0:T(8,128)(2,1)S(1)}, bf16[128,512]{1,0:T(8,128)(2,1)S(1)}, u32[]{:S(2)}, u32[]{:S(2)}) collective-permute-start(bf16[128,512]{1,0:T(8,128)(2,1)S(1)} %get-tuple-element.69), channel_id=1, source_target_pairs={{0,4},{1,5},{2,6},{3,7},{4,0},{5,1},{6,2},{7,3},{8,12},{9,13},{10,... | collective-permute-start | bytes 393224 | tf_op jit(solution)/shard_map/ppermute | solution.py:376
  17.7 13.7 %collective-permute-start.6 = (bf16[128,512]{1,0:T(8,128)(2,1)S(1)}, bf16[128,512]{1,0:T(8,128)(2,1)S(1)}, u32[]{:S(2)}, u32[]{:S(2)}) collective-permute-start(bf16[128,512]{1,0:T(8,128)(2,1)S(1)} %get-tuple-element.70), channel_id=1, source_target_pairs={{0,5},{1,4},{2,7},{3,6},{4,1},{5,0},{6,3},{7,2},{8,13},{9,12},{10,... | collective-permute-start | bytes 393224 | tf_op jit(solution)/shard_map/ppermute | solution.py:376
  32.7 12.6 %collective-permute-start.10 = (bf16[128,512]{1,0:T(8,128)(2,1)S(1)}, bf16[128,512]{1,0:T(8,128)(2,1)S(1)}, u32[]{:S(2)}, u32[]{:S(2)}) collective-permute-start(bf16[128,512]{1,0:T(8,128)(2,1)S(1)} %get-tuple-element.98), channel_id=1, source_target_pairs={{0,1},{1,0},{2,3},{3,2},{4,5},{5,4},{6,7},{7,6},{8,9},{9,8},{10,11... | collective-permute-start | bytes 393224 | tf_op jit(solution)/shard_map/ppermute | solution.py:376
  34.3 13.3 %collective-permute-start.13 = (bf16[128,512]{1,0:T(8,128)(2,1)S(1)}, bf16[128,512]{1,0:T(8,128)(2,1)S(1)}, u32[]{:S(2)}, u32[]{:S(2)}) collective-permute-start(bf16[128,512]{1,0:T(8,128)(2,1)S(1)} %get-tuple-element.103), channel_id=1, source_target_pairs={{0,4},{1,5},{2,6},{3,7},{4,0},{5,1},{6,2},{7,3},{8,12},{9,13},{10,... | collective-permute-start | bytes 393224 | tf_op jit(solution)/shard_map/ppermute | solution.py:376
  34.3 23.8 %collective-permute-start.8 = (bf16[128,512]{1,0:T(8,128)(2,1)S(1)}, bf16[128,512]{1,0:T(8,128)(2,1)S(1)}, u32[]{:S(2)}, u32[]{:S(2)}) collective-permute-start(bf16[128,512]{1,0:T(8,128)(2,1)S(1)} %get-tuple-element.94), channel_id=1, source_target_pairs={{0,5},{1,4},{2,7},{3,6},{4,1},{5,0},{6,3},{7,2},{8,13},{9,12},{10,... | collective-permute-start | bytes 393224 | tf_op jit(solution)/shard_map/ppermute | solution.py:376
  37.2 18.3 %collective-permute-start.11 = (bf16[128,512]{1,0:T(8,128)(2,1)S(1)}, bf16[128,512]{1,0:T(8,128)(2,1)S(1)}, u32[]{:S(2)}, u32[]{:S(2)}) collective-permute-start(bf16[128,512]{1,0:T(8,128)(2,1)S(1)} %get-tuple-element.99), channel_id=1, source_target_pairs={{0,2},{1,3},{2,0},{3,1},{4,6},{5,7},{6,4},{7,5},{8,10},{9,11},{10,... | collective-permute-start | bytes 393224 | tf_op jit(solution)/shard_map/ppermute | solution.py:376
  37.2 18.3 %collective-permute-start.12 = (bf16[128,512]{1,0:T(8,128)(2,1)S(1)}, bf16[128,512]{1,0:T(8,128)(2,1)S(1)}, u32[]{:S(2)}, u32[]{:S(2)}) collective-permute-start(bf16[128,512]{1,0:T(8,128)(2,1)S(1)} %get-tuple-element.100), channel_id=1, source_target_pairs={{0,3},{1,2},{2,1},{3,0},{4,7},{5,6},{6,5},{7,4},{8,11},{9,10},{10,... | collective-permute-start | bytes 393224 | tf_op jit(solution)/shard_map/ppermute | solution.py:376
  45.4 12.7 %collective-permute-start.9 = (bf16[128,512]{1,0:T(8,128)(2,1)S(1)}, bf16[128,512]{1,0:T(8,128)(2,1)S(1)}, u32[]{:S(2)}, u32[]{:S(2)}) collective-permute-start(bf16[128,512]{1,0:T(8,128)(2,1)S(1)} %get-tuple-element.95), channel_id=1, source_target_pairs={{0,6},{1,7},{2,4},{3,5},{4,2},{5,3},{6,0},{7,1},{8,14},{9,15},{10,... | collective-permute-start | bytes 393224 | tf_op jit(solution)/shard_map/ppermute | solution.py:376
  47.5 11.9 %collective-permute-start.7 = (bf16[128,512]{1,0:T(8,128)(2,1)S(1)}, bf16[128,512]{1,0:T(8,128)(2,1)S(1)}, u32[]{:S(2)}, u32[]{:S(2)}) collective-permute-start(bf16[128,512]{1,0:T(8,128)(2,1)S(1)} %get-tuple-element.91), channel_id=1, source_target_pairs={{0,7},{1,6},{2,5},{3,4},{4,3},{5,2},{6,1},{7,0},{8,15},{9,14},{10,... | collective-permute-start | bytes 393224 | tf_op jit(solution)/shard_map/ppermute | solution.py:376
  60.5 8.3 %collective-permute-start.14 = (bf16[128,512]{1,0:T(8,128)(2,1)S(1)}, bf16[128,512]{1,0:T(8,128)(2,1)S(1)}, u32[]{:S(2)}, u32[]{:S(2)}) collective-permute-start(bf16[128,512]{1,0:T(8,128)(2,1)S(1)} %get-tuple-element.106), channel_id=1, source_target_pairs={{0,6},{1,7},{2,4},{3,5},{4,2},{5,3},{6,0},{7,1},{8,14},{9,15},{10,... | collective-permute-start | bytes 393224 | tf_op jit(solution)/shard_map/ppermute | solution.py:376
  62.2 10.4 %collective-permute-start.15 = (bf16[128,512]{1,0:T(8,128)(2,1)S(1)}, bf16[128,512]{1,0:T(8,128)(2,1)S(1)}, u32[]{:S(2)}, u32[]{:S(2)}) collective-permute-start(bf16[128,512]{1,0:T(8,128)(2,1)S(1)} %get-tuple-element.107), channel_id=1, source_target_pairs={{0,7},{1,6},{2,5},{3,4},{4,3},{5,2},{6,1},{7,0},{8,15},{9,14},{10,... | collective-permute-start | bytes 393224 | tf_op jit(solution)/shard_map/ppermute | solution.py:376
  65.3 11.8 %collective-permute-start.16 = (bf16[128,512]{1,0:T(8,128)(2,1)S(1)}, bf16[128,512]{1,0:T(8,128)(2,1)S(1)}, u32[]{:S(2)}, u32[]{:S(2)}) collective-permute-start(bf16[128,512]{1,0:T(8,128)(2,1)S(1)} %get-tuple-element.108), channel_id=1, source_target_pairs={{0,1},{1,0},{2,3},{3,2},{4,5},{5,4},{6,7},{7,6},{8,9},{9,8},{10,11... | collective-permute-start | bytes 393224 | tf_op jit(solution)/shard_map/ppermute | solution.py:376
  65.9 11.2 %collective-permute-start.17 = (bf16[128,512]{1,0:T(8,128)(2,1)S(1)}, bf16[128,512]{1,0:T(8,128)(2,1)S(1)}, u32[]{:S(2)}, u32[]{:S(2)}) collective-permute-start(bf16[128,512]{1,0:T(8,128)(2,1)S(1)} %get-tuple-element.109), channel_id=1, source_target_pairs={{0,2},{1,3},{2,0},{3,1},{4,6},{5,7},{6,4},{7,5},{8,10},{9,11},{10,... | collective-permute-start | bytes 393224 | tf_op jit(solution)/shard_map/ppermute | solution.py:376
  65.9 11.2 %collective-permute-start.18 = (bf16[128,512]{1,0:T(8,128)(2,1)S(1)}, bf16[128,512]{1,0:T(8,128)(2,1)S(1)}, u32[]{:S(2)}, u32[]{:S(2)}) collective-permute-start(bf16[128,512]{1,0:T(8,128)(2,1)S(1)} %get-tuple-element.110), channel_id=1, source_target_pairs={{0,3},{1,2},{2,1},{3,0},{4,7},{5,6},{6,5},{7,4},{8,11},{9,10},{10,... | collective-permute-start | bytes 393224 | tf_op jit(solution)/shard_map/ppermute | solution.py:376
  68.8 11.7 %collective-permute-start.19 = (bf16[128,512]{1,0:T(8,128)(2,1)S(1)}, bf16[128,512]{1,0:T(8,128)(2,1)S(1)}, u32[]{:S(2)}, u32[]{:S(2)}) collective-permute-start(bf16[128,512]{1,0:T(8,128)(2,1)S(1)} %get-tuple-element.111), channel_id=1, source_target_pairs={{0,4},{1,5},{2,6},{3,7},{4,0},{5,1},{6,2},{7,3},{8,12},{9,13},{10,... | collective-permute-start | bytes 393224 | tf_op jit(solution)/shard_map/ppermute | solution.py:376
  72.6 8.0 %collective-permute-start.20 = (bf16[128,512]{1,0:T(8,128)(2,1)S(1)}, bf16[128,512]{1,0:T(8,128)(2,1)S(1)}, u32[]{:S(2)}, u32[]{:S(2)}) collective-permute-start(bf16[128,512]{1,0:T(8,128)(2,1)S(1)} %get-tuple-element.112), channel_id=1, source_target_pairs={{0,5},{1,4},{2,7},{3,6},{4,1},{5,0},{6,3},{7,2},{8,13},{9,12},{10,... | collective-permute-start | bytes 393224 | tf_op jit(solution)/shard_map/ppermute | solution.py:376
  81.9 9.2 %collective-permute-start.24 = (bf16[128,512]{1,0:T(8,128)(2,1)S(1)}, bf16[128,512]{1,0:T(8,128)(2,1)S(1)}, u32[]{:S(2)}, u32[]{:S(2)}) collective-permute-start(bf16[128,512]{1,0:T(8,128)(2,1)S(1)} %get-tuple-element.118), channel_id=1, source_target_pairs={{0,1},{1,0},{2,3},{3,2},{4,5},{5,4},{6,7},{7,6},{8,9},{9,8},{10,11... | collective-permute-start | bytes 393224 | tf_op jit(solution)/shard_map/ppermute | solution.py:376
  85.2 10.3 %collective-permute-start.27 = (bf16[128,512]{1,0:T(8,128)(2,1)S(1)}, bf16[128,512]{1,0:T(8,128)(2,1)S(1)}, u32[]{:S(2)}, u32[]{:S(2)}) collective-permute-start(bf16[128,512]{1,0:T(8,128)(2,1)S(1)} %get-tuple-element.121), channel_id=1, source_target_pairs={{0,4},{1,5},{2,6},{3,7},{4,0},{5,1},{6,2},{7,3},{8,12},{9,13},{10,... | collective-permute-start | bytes 393224 | tf_op jit(solution)/shard_map/ppermute | solution.py:376
  85.7 22.9 %collective-permute-start.22 = (bf16[128,512]{1,0:T(8,128)(2,1)S(1)}, bf16[128,512]{1,0:T(8,128)(2,1)S(1)}, u32[]{:S(2)}, u32[]{:S(2)}) collective-permute-start(bf16[128,512]{1,0:T(8,128)(2,1)S(1)} %get-tuple-element.115), channel_id=1, source_target_pairs={{0,5},{1,4},{2,7},{3,6},{4,1},{5,0},{6,3},{7,2},{8,13},{9,12},{10,... | collective-permute-start | bytes 393224 | tf_op jit(solution)/shard_map/ppermute | solution.py:376
  87.7 12.0 %collective-permute-start.25 = (bf16[128,512]{1,0:T(8,128)(2,1)S(1)}, bf16[128,512]{1,0:T(8,128)(2,1)S(1)}, u32[]{:S(2)}, u32[]{:S(2)}) collective-permute-start(bf16[128,512]{1,0:T(8,128)(2,1)S(1)} %get-tuple-element.119), channel_id=1, source_target_pairs={{0,2},{1,3},{2,0},{3,1},{4,6},{5,7},{6,4},{7,5},{8,10},{9,11},{10,... | collective-permute-start | bytes 393224 | tf_op jit(solution)/shard_map/ppermute | solution.py:376
  88.7 17.3 %collective-permute-start.26 = (bf16[128,512]{1,0:T(8,128)(2,1)S(1)}, bf16[128,512]{1,0:T(8,128)(2,1)S(1)}, u32[]{:S(2)}, u32[]{:S(2)}) collective-permute-start(bf16[128,512]{1,0:T(8,128)(2,1)S(1)} %get-tuple-element.120), channel_id=1, source_target_pairs={{0,3},{1,2},{2,1},{3,0},{4,7},{5,6},{6,5},{7,4},{8,11},{9,10},{10,... | collective-permute-start | bytes 393224 | tf_op jit(solution)/shard_map/ppermute | solution.py:376
  91.1 17.5 %collective-permute-start.23 = (bf16[128,512]{1,0:T(8,128)(2,1)S(1)}, bf16[128,512]{1,0:T(8,128)(2,1)S(1)}, u32[]{:S(2)}, u32[]{:S(2)}) collective-permute-start(bf16[128,512]{1,0:T(8,128)(2,1)S(1)} %get-tuple-element.116), channel_id=1, source_target_pairs={{0,6},{1,7},{2,4},{3,5},{4,2},{5,3},{6,0},{7,1},{8,14},{9,15},{10,... | collective-permute-start | bytes 393224 | tf_op jit(solution)/shard_map/ppermute | solution.py:376
  95.6 14.5 %collective-permute-start.21 = (bf16[128,512]{1,0:T(8,128)(2,1)S(1)}, bf16[128,512]{1,0:T(8,128)(2,1)S(1)}, u32[]{:S(2)}, u32[]{:S(2)}) collective-permute-start(bf16[128,512]{1,0:T(8,128)(2,1)S(1)} %get-tuple-element.114), channel_id=1, source_target_pairs={{0,7},{1,6},{2,5},{3,4},{4,3},{5,2},{6,1},{7,0},{8,15},{9,14},{10,... | collective-permute-start | bytes 393224 | tf_op jit(solution)/shard_map/ppermute | solution.py:376
  (4 other events, 16.4 us)
